TPU v7x, 128 devices: a whole 4x4x4 slice. The times are simulated.
128 devices in a mesh: row: 16 (over x, y_lo, core), col: 8 (over y_hi, z).
Axes of the slice: x: 4, y: 4 (y_hi: 2, y_lo: 2; y = y_hi * 2 + y_lo), z: 4, core: 2. Of those that a mesh axis runs over, the one named last changes fastest.
Arguments:
- embeddings: bfloat16 [16384, 1024], P(('row', 'col'))
- partner: int32 [16384], P(('row', 'col')), may hold values from 0 to 16383, as said below
- inv_temp: float32 [1], replicated, may hold values from 8 to 128
Outputs:
- loss: float32 [1], replicated
- grad_embed: float32 [16384, 1024], P(('row', 'col'))
Inputs may be any that keep to these rules, and one draw needn't show every extreme that they name: partner pairs the views: partner[partner[i]] == i and partner[i] != i for every view.
All inputs are finite; a program needn't handle non-finite values.
Results may differ from a plain program's by a relative error of at most 0.0065.
The roundings to bfloat16 on the way count: a program that leaves them out, or rounds other values in their place, can miss the bound.
Values may be sent and summed in bfloat16 or wider, within the bound.
No kernel may reach another device: no remote copies, remote signals or barrier semaphores. Data moves between devices by JAX's collectives and lax.ppermute only.
A program may use at most 64 MiB of HBM per device.

v0:
```python
import jax
import jax.numpy as jnp
from jax import lax
from jax.sharding import PartitionSpec as P


def body(embeddings, partner, inv_temp):
    flat = embeddings.astype(jnp.float32)
    inv_norm = lax.rsqrt(jnp.sum(flat * flat, axis=1, keepdims=True) + 1e-06)
    unit = flat * inv_norm
    unit_b = unit.astype(jnp.bfloat16)
    scale = inv_temp[0]
    views = embeddings.shape[0]
    n_row = lax.axis_size("row")
    n_col = lax.axis_size("col")
    total_views = views * n_row * n_col
    row_pos = lax.axis_index("row")
    col_pos = lax.axis_index("col")
    block_a, mates = (
        lax.all_gather(unit_b, "col", axis=0, tiled=True),
        lax.all_gather(partner, "col", axis=0, tiled=True),
    )
    block_b = lax.all_gather(unit_b, "row", axis=0, tiled=True)
    rows_global = row_pos * n_col * views + jnp.arange(n_col * views, dtype=jnp.int32)
    slots = jnp.arange(n_row * views, dtype=jnp.int32)
    cols_global = slots // views * n_col * views + col_pos * views + slots % views
    scores = scale * jnp.einsum("ik,jk->ij", block_a, block_b, preferred_element_type=jnp.float32)
    scores = jnp.where(rows_global[:, None] == cols_global[None, :], -jnp.inf, scores)
    is_mate = cols_global[None, :] == mates[:, None]
    mate_mask = jnp.where(is_mate, 1.0, 0.0)
    peak = jnp.max(scores, axis=1)
    expsum = jnp.sum(jnp.exp(scores - peak[:, None]), axis=1)
    pos = jnp.sum(jnp.where(is_mate, scores, 0.0), axis=1)
    peak_all = lax.pmax(peak, "col")
    expsum_all, pos_all = lax.psum((expsum * jnp.exp(peak - peak_all), pos), "col")
    lse = peak_all + jnp.log(expsum_all)
    own_terms = lax.dynamic_slice_in_dim(lse - pos_all, col_pos * views, views, 0)
    loss = (lax.psum(jnp.sum(own_terms), ("row", "col")) / total_views).reshape(1)
    prob = jnp.exp(scores - lse[:, None])
    coef = ((prob - mate_mask) / total_views).astype(jnp.bfloat16)
    picked = coef
    from_rows = lax.psum_scatter(
        jnp.dot(picked, block_b, preferred_element_type=jnp.float32),
        "col",
        scatter_dimension=0,
        tiled=True,
    )
    picked = coef
    from_columns = lax.psum_scatter(
        jnp.einsum("ij,ik->jk", picked, block_a, preferred_element_type=jnp.float32),
        "row",
        scatter_dimension=0,
        tiled=True,
    )
    dunit = scale * (from_rows + from_columns)
    grad_embed = inv_norm * (dunit - unit * jnp.sum(unit * dunit, axis=1, keepdims=True))
    return (loss, grad_embed)


def solution(mesh):
    in_specs = (P(("row", "col"), None), P(("row", "col")), P())
    out_specs = (P(), P(("row", "col"), None))
    return jax.shard_map(body, mesh=mesh, in_specs=in_specs, out_specs=out_specs, check_vma=False)
```

profile of v0, /device:TPU:1, one launch (start us, length us, event | category | flops | bytes accessed | tf_op | source)
XLA Modules:
  0.0 368.9 jit_solution(13835103650312627709)
XLA Ops:
  7.2 0.0 all-gather.4.cloned.1.call-start
  7.2 1.1 fusion.10
  8.3 1.8 fusion.6
  10.1 0.0 all-gather.6.cloned.1.call-start
  10.1 0.7 all-gather.6.cloned.1.call-update
  10.8 0.0 reduce-scatter.3.cloned.1.call-start
  11.5 21.9 %all-gather = s32[8,1,128]{2,1,0:T(1,128)S(1)} all-gather(s32[1,1,128]{2,1,0:T(1,128)} %bitcast.15), channel_id=1, replica_groups=mesh['row'=16,'col'=8] {'col'}, dimensions={0}, use_global_device_ids=true | all-gather | bytes 4608 | tf_op jit(solution)/shard_map/all_gather | solution.py:21
  33.5 34.3 %all-gather.4.cloned.1.call-done = bf16[1024,1024]{1,0:T(8,128)(2,1)} async-done(((bf16[128,1024]{1,0:T(8,128)(2,1)}), bf16[1024,1024]{1,0:T(8,128)(2,1)}) %all-gather.4.cloned.1.call-update) | async-done | bytes 2097168 | tf_op jit(solution)/shard_map/all_gather | solution.py:20
  67.8 38.1 %all-gather.6.cloned.1.call-done = bf16[2048,1024]{1,0:T(8,128)(2,1)} async-done(((bf16[128,1024]{1,0:T(8,128)(2,1)}), bf16[2048,1024]{1,0:T(8,128)(2,1)}) %all-gather.6.cloned.1.call-update) | async-done | bytes 4194320 | tf_op jit(solution)/shard_map/all_gather | solution.py:23
  105.9 10.7 %fusion.22 = (f32[1024]{0:T(1024)S(1)}, f32[1024,2048]{1,0:T(8,128)}) fusion(bf16[1024,1024]{1,0:T(8,128)(2,1)} %all-gather.4.cloned.1.call-done, bf16[2048,1024]{1,0:T(8,128)(2,1)} %all-gather.6.cloned.1.call-done, f32[]{:T(128)} %bitcast.10, s32[2048]{0:T(1024)S(1)} %fusion.19, s32[1024]{0:T(1024)S(1)} %iota_add_fusion), kind=kOutput, calls=%fused_computation.38 | convolution fusion | flops 4303354880 | bytes 14696452 | tf_op jit(solution)/shard_map/ik,jk->ij/dot_general | solution.py:27
  116.7 20.3 %pmax.7 = f32[1024]{0:T(1024)S(1)} all-reduce(f32[1024]{0:T(1024)S(1)} %get-tuple-element.8), channel_id=1, replica_groups=mesh['row'=16,'col'=8] {'col'}, use_global_device_ids=true, to_apply=%region_2.3 | all-reduce | flops 1024 | bytes 8192 | tf_op jit(solution)/shard_map/pmax | solution.py:34
  137.0 4.7 %fusion = (f32[1024]{0:T(1024)S(1)}, f32[1024]{0:T(1024)S(1)}) fusion(f32[1024,2048]{1,0:T(8,128)} %get-tuple-element.9, s32[2048]{0:T(1024)S(1)} %fusion.19, s32[1024]{0:T(1024)S(1)} %bitcast.13, f32[1024]{0:T(1024)S(1)} %get-tuple-element.8), kind=kLoop, calls=%fused_computation.2 | loop fusion | flops 10483712 | bytes 8413184 | tf_op jit(solution)/shard_map/reduce_sum | solution.py:33
  141.7 15.7 %all-reduce = (f32[1024]{0:T(1024)S(1)}, f32[1024]{0:T(1024)S(1)}) all-reduce(f32[1024]{0:T(1024)S(1)} %exponential_multiply_fusion, f32[1024]{0:T(1024)S(1)} %get-tuple-element.2), channel_id=1, replica_groups=mesh['row'=16,'col'=8] {'col'}, use_global_device_ids=true, to_apply=%region_4.5 | all-reduce | flops 2048 | bytes 16384 | tf_op jit(solution)/shard_map/psum | solution.py:35
  157.5 4.8 %fusion.3 = bf16[1024,2048]{1,0:T(8,128)(2,1)S(1)} fusion(f32[1024,2048]{1,0:T(8,128)} %get-tuple-element.9, f32[1024]{0:T(1024)S(1)} %get-tuple-element.7, s32[2048]{0:T(1024)S(1)} %fusion.19, s32[1024]{0:T(1024)S(1)} %bitcast.14), kind=kLoop, calls=%fused_computation.5 | loop fusion | flops 12582912 | bytes 12599296 | tf_op jit(solution)/shard_map/convert_element_type | solution.py:40
  162.3 1.9 copy-done
  164.3 6.0 %fusion.23 = f32[1024,1024]{1,0:T(8,128)} fusion(bf16[1024,2048]{1,0:T(8,128)(2,1)S(1)} %fusion.3, bf16[2048,1024]{1,0:T(8,128)(2,1)S(1)} %copy-done.2), kind=kOutput, calls=%fused_computation.39 | convolution fusion | flops 4294967296 | bytes 12582912 | tf_op jit(solution)/shard_map/dot_general | solution.py:43
  170.3 0.0 reduce-scatter.5.cloned.1.call-start
  170.4 9.1 %fusion.24 = f32[2048,1024]{1,0:T(8,128)} fusion(bf16[1024,2048]{1,0:T(8,128)(2,1)} %copy-done, bf16[1024,1024]{1,0:T(8,128)(2,1)S(1)} %copy-done.3), kind=kOutput, calls=%fused_computation.40 | convolution fusion | flops 4294967296 | bytes 14680064 | tf_op jit(solution)/shard_map/ij,ik->jk/dot_general | solution.py:50
  179.5 0.7 dynamic-slice_reduce_fusion
  180.1 74.7 %psum.23 = f32[]{:T(128)} all-reduce(f32[]{:T(128)} %dynamic-slice_reduce_fusion), channel_id=1, replica_groups=mesh['row'=16,'col'=8] {'row','col'}, use_global_device_ids=true, to_apply=%region_8.9 | all-reduce | flops 1 | bytes 8 | tf_op jit(solution)/shard_map/psum | solution.py:38
  255.5 3.4 reduce-scatter.3.cloned.1.call-done
  258.9 98.7 %reduce-scatter.5.cloned.1.call-done = f32[128,1024]{1,0:T(8,128)} async-done(((f32[2048,1024]{1,0:T(8,128)}), f32[128,1024]{1,0:T(8,128)}) %reduce-scatter.5.cloned.1.call-update) | async-done | bytes 524304 | tf_op jit(solution)/shard_map/reduce_scatter | solution.py:49
  357.6 1.4 fusion.7
  359.0 2.2 fusion.9
  (15 shorter events, 0.1 us)
Async XLA Ops:
  7.2 60.6 %all-gather.4.cloned.1.call-start = ((), (), s32[]{:S(2)}) async-start(), calls=%async_computation.2 | async-start | bytes 2359296 | tf_op jit(solution)/shard_map/all_gather | solution.py:20
  10.1 95.8 %all-gather.6.cloned.1.call-start = ((), (), s32[]{:S(2)}) async-start(), calls=%async_computation.3 | async-start | bytes 4456448 | tf_op jit(solution)/shard_map/all_gather | solution.py:23
  10.8 248.0 %reduce-scatter.3.cloned.1.call-start = ((), (), s32[]{:S(2)}) async-start(), calls=%async_computation.4 | async-start | bytes 4718592 | tf_op jit(solution)/shard_map/reduce_scatter | solution.py:42
  157.5 6.8 %copy-start.2 = (bf16[2048,1024]{1,0:T(8,128)(2,1)S(1)}, bf16[2048,1024]{1,0:T(8,128)(2,1)}, u32[]{:S(2)}) copy-start(bf16[2048,1024]{1,0:T(8,128)(2,1)} %all-gather.6.cloned.1.call-done) | copy-start | bytes 12582916
  162.3 2.0 copy-start
  164.3 6.1 %copy-start.3 = (bf16[1024,1024]{1,0:T(8,128)(2,1)S(1)}, bf16[1024,1024]{1,0:T(8,128)(2,1)}, u32[]{:S(2)}) copy-start(bf16[1024,1024]{1,0:T(8,128)(2,1)} %all-gather.4.cloned.1.call-done) | copy-start | bytes 6291460
  170.3 187.3 %reduce-scatter.5.cloned.1.call-start = ((), (), s32[]{:S(2)}) async-start(), calls=%async_computation.5 | async-start | bytes 8912896 | tf_op jit(solution)/shard_map/reduce_scatter | solution.py:49
  179.4 178.1 %copy-start.1 = (bf16[128,1024]{1,0:T(8,128)(2,1)S(1)}, bf16[128,1024]{1,0:T(8,128)(2,1)}, u32[]{:S(2)}) copy-start(bf16[128,1024]{1,0:T(8,128)(2,1)} %param.3) | copy-start | bytes 786436
Sparse Core Ops, SparseCore 0:
  10.9 56.7 all-gather.3
  70.1 35.8 all-gather.5
  170.4 88.4 reduce-scatter.2
  261.3 96.2 reduce-scatter.4
where the time goes:
time: 370 us; the launch traced here: 369 us
  waiting for transfers between devices  175 us (47%)
  blocking collectives  133 us (36%)
  matrix products  25.8 us (7%)
  other arithmetic  16.8 us (5%)
  between operations  16.3 us (4%)
    reduce_scatter x1, waiting for transfers between devices, body(): lax.psum_scatter(jnp.einsum('ij,ik->jk', picked, block_a, preferred_eleme...  98.7 us
    psum x1, blocking collectives, body(): lax.psum(jnp.sum(own_terms), ('row', 'col')) / total_views  74.7 us
    all_gather x1, waiting for transfers between devices, body(): block_b = lax.all_gather(unit_b, 'row', axis=0, tiled=True)  38.1 us
    all_gather x1, waiting for transfers between devices, body(): lax.all_gather(unit_b, 'col', axis=0, tiled=True)  34.3 us
    all_gather x1, blocking collectives, body(): lax.all_gather(partner, 'col', axis=0, tiled=True)  21.9 us
    pmax x1, blocking collectives, body(): peak_all = lax.pmax(peak, 'col')  20.3 us
    psum x1, blocking collectives, body(): lax.psum((expsum * jnp.exp(peak - peak_all), pos), 'col')  15.7 us
    dot_general x1, matrix products, body(): jnp.einsum('ik,jk->ij', block_a, block_b, preferred_element_type=jnp.floa...  10.7 us
  transfers between devices with their start and end apart: 4, of which 4 were waited for; matrix products, arithmetic and copies ran while one was open for 3% of the time, Pallas kernels for 0%

commit v1 on v0

v1 whole, which is shorter than its diff:
```python
import functools
import numpy as np
import jax
import jax.numpy as jnp
from jax import lax
from jax.experimental import pallas as pl
from jax.experimental.pallas import tpu as pltpu
from jax.sharding import PartitionSpec as P

LOG2E = 1.4426950408889634
LN2 = 0.6931471805599453
F32 = jnp.float32
BF16 = jnp.bfloat16


def device_id(x, y, z, core):
    return ((x % 4) * 4 + (y % 2) * 2 + core) * 8 + (y % 4) // 2 * 4 + z % 4


def groups_of_rows():
    return [
        [device_id(x, y, z, k) for y in (p, p + 1) for z in range(4)]
        for x in range(4)
        for p in (0, 2)
        for k in range(2)
    ]


def groups_of_columns():
    return [
        [device_id(x, y, z, k) for y in (p, p + 1) for x in range(4)]
        for z in range(4)
        for p in (1, 3)
        for k in range(2)
    ]


def table(groups):
    rows = np.zeros((128, len(groups[0])), np.int32)
    for g in groups:
        for d in g:
            rows[d] = g
    return rows


def unit_kernel(x_ref, out_ref):
    flat = x_ref[...].astype(F32)
    inv = lax.rsqrt(jnp.sum(flat * flat, axis=1, keepdims=True) + 1e-06)
    out_ref[...] = (flat * inv).astype(BF16)


def score_kernel(scale_ref, a_ref, b_ref, rows_ref, mates_ref, cols_ref, s_ref, peak_ref, sums_ref, pos_ref):
    scale2 = scale_ref[0] * LOG2E
    s = lax.dot_general(a_ref[...], b_ref[...], (((1,), (1,)), ((), ())), preferred_element_type=F32)
    s = s * scale2
    cols = cols_ref[...]
    s = jnp.where(rows_ref[...] == cols, -jnp.inf, s)
    s_ref[...] = s
    peak = jnp.max(s, axis=1, keepdims=True)
    peak_ref[...] = peak
    sums_ref[...] = jnp.sum(jnp.exp2(s - peak), axis=1, keepdims=True)
    pos_ref[...] = jnp.sum(jnp.where(mates_ref[...] == cols, s, 0.0), axis=1, keepdims=True)


def grad_kernel(s_ref, b_ref, lse_row_ref, lse_col_ref, mates_ref, cols_ref, out_ref):
    s = s_ref[...]
    d = jnp.exp2(s - lse_row_ref[...]) + jnp.exp2(s - lse_col_ref[...])
    d = d - jnp.where(mates_ref[...] == cols_ref[...], 2.0, 0.0)
    out_ref[...] = jnp.dot(d.astype(BF16), b_ref[...], preferred_element_type=F32).astype(BF16)


def final_kernel(scale_ref, x_ref, parts_ref, out_ref):
    flat = x_ref[...].astype(F32)
    inv = lax.rsqrt(jnp.sum(flat * flat, axis=1, keepdims=True) + 1e-06)
    unit = flat * inv
    dunit = jnp.sum(parts_ref[...].astype(F32), axis=0) * (scale_ref[0] / 16384.0)
    out_ref[...] = inv * (dunit - unit * jnp.sum(unit * dunit, axis=1, keepdims=True))


VMEM = pl.BlockSpec(memory_space=pltpu.VMEM)
SMEM = pl.BlockSpec(memory_space=pltpu.SMEM)


def body(embeddings, partner, inv_temp):
    views, width = embeddings.shape
    me = lax.axis_index("row") * 8 + lax.axis_index("col")
    rows_groups, cols_groups = groups_of_rows(), groups_of_columns()
    other_core = [(d, d ^ 8) for d in range(128)]
    axes = ("row", "col")

    def spread(v, groups):
        n = len(groups[0])
        v = jnp.broadcast_to(v[None], (n, *v.shape))
        return lax.all_to_all(v, axes, 0, 0, tiled=True, axis_index_groups=groups)

    unit_b = pl.pallas_call(
        unit_kernel, out_shape=jax.ShapeDtypeStruct((views, width), BF16), in_specs=[VMEM], out_specs=VMEM
    )(embeddings)
    mates = spread(partner.reshape(1, views), rows_groups).reshape(-1, 1)
    block_a = spread(unit_b, rows_groups).reshape(-1, width)
    block_b = spread(unit_b, cols_groups).reshape(-1, width)
    block_b2 = lax.ppermute(block_b, axes, other_core)
    block_b = jnp.concatenate([block_b, block_b2], axis=0)
    n_a, n_b = block_a.shape[0], block_b.shape[0]
    ids_a = jnp.asarray(table(rows_groups))[me]
    ids_b = jnp.asarray(table(cols_groups))[me]
    ids_b = jnp.concatenate([ids_b, ids_b ^ 8])
    lane = jnp.arange(views, dtype=jnp.int32)
    rows_global = (ids_a[:, None] * views + lane[None, :]).reshape(n_a, 1)
    cols_global = (ids_b[:, None] * views + lane[None, :]).reshape(1, n_b)

    bm = 256
    col_spec = pl.BlockSpec((bm, 1), lambda i: (i, 0))
    scores, peak, sums, pos = pl.pallas_call(
        score_kernel,
        grid=(n_a // bm,),
        out_shape=[
            jax.ShapeDtypeStruct((n_a, n_b), F32),
            jax.ShapeDtypeStruct((n_a, 1), F32),
            jax.ShapeDtypeStruct((n_a, 1), F32),
            jax.ShapeDtypeStruct((n_a, 1), F32),
        ],
        in_specs=[
            SMEM,
            pl.BlockSpec((bm, width), lambda i: (i, 0)),
            pl.BlockSpec((n_b, width), lambda i: (0, 0)),
            col_spec,
            col_spec,
            pl.BlockSpec((1, n_b), lambda i: (0, 0)),
        ],
        out_specs=[pl.BlockSpec((bm, n_b), lambda i: (i, 0)), col_spec, col_spec, col_spec],
        compiler_params=pltpu.CompilerParams(vmem_limit_bytes=48 << 20),
    )(inv_temp, block_a, block_b, rows_global, mates, cols_global)

    stats = jnp.concatenate([peak.reshape(8, views), sums.reshape(8, views), pos.reshape(8, views)], axis=0)
    stats = spread(stats, rows_groups).reshape(8, 3, 8, views)
    peak_all = jnp.max(stats[:, 0], axis=0)
    lse2 = peak_all + jnp.log2(jnp.sum(stats[:, 1] * jnp.exp2(stats[:, 0] - peak_all), axis=0))
    loss_rows = jnp.sum(lse2) - jnp.sum(stats[:, 2])
    position = jnp.argmax(ids_a == me)
    own_lse = lax.dynamic_slice_in_dim(lse2, position, 1, 0)
    payload = jnp.concatenate([own_lse, jnp.full((1, views), loss_rows)], axis=0)
    gathered = spread(payload, cols_groups).reshape(8, 2, views)
    swapped = lax.ppermute(gathered, axes, other_core)
    gathered = jnp.concatenate([gathered, swapped], axis=0)
    loss = (jnp.sum(gathered[:, 1, 0]) * (LN2 / 16384.0)).reshape(1)
    lse_cols = gathered[:, 0].reshape(1, n_b)

    grads = pl.pallas_call(
        grad_kernel,
        grid=(n_a // bm,),
        out_shape=jax.ShapeDtypeStruct((n_a, width), BF16),
        in_specs=[
            pl.BlockSpec((bm, n_b), lambda i: (i, 0)),
            pl.BlockSpec((n_b, width), lambda i: (0, 0)),
            col_spec,
            pl.BlockSpec((1, n_b), lambda i: (0, 0)),
            col_spec,
            pl.BlockSpec((1, n_b), lambda i: (0, 0)),
        ],
        out_specs=pl.BlockSpec((bm, width), lambda i: (i, 0)),
        compiler_params=pltpu.CompilerParams(vmem_limit_bytes=48 << 20),
    )(scores, block_b, lse2.reshape(n_a, 1), lse_cols, mates, cols_global)
    parts = lax.all_to_all(grads.reshape(8, views, width), axes, 0, 0, tiled=True, axis_index_groups=rows_groups)
    grad_embed = pl.pallas_call(
        final_kernel,
        out_shape=jax.ShapeDtypeStruct((views, width), F32),
        in_specs=[SMEM, VMEM, VMEM],
        out_specs=VMEM,
    )(inv_temp, embeddings, parts)
    return loss, grad_embed


def solution(mesh):
    in_specs = (P(("row", "col"), None), P(("row", "col")), P())
    out_specs = (P(), P(("row", "col"), None))
    return jax.shard_map(body, mesh=mesh, in_specs=in_specs, out_specs=out_specs, check_vma=False)
```

time: 370 us -> 166 us (0.45)
  waiting for transfers between devices: 175 us -> 50.1 us
  blocking collectives: 133 us -> 42.7 us
  matrix products: 25.8 us -> 0 us
  Pallas kernels: 0 us -> 25 us
  starting transfers between devices: 0.16 us -> 21 us
  between operations: 16.3 us -> 6.31 us
  local copies, waits for them, and re-layouts: 1.96 us -> 6.97 us
    reduce_scatter x2 -> x0, waiting for transfers between devices: 102 us -> none  [the longest x1 98.7 us: body(): lax.psum_scatter(jnp.einsum('ij,ik->jk', picked, block_a, preferred_eleme...]
    psum x2 -> x0, blocking collectives: 90.4 us -> none  [the longest x1 74.7 us: body(): lax.psum(jnp.sum(own_terms), ('row', 'col')) / total_views]
    all_gather x2 -> x0, waiting for transfers between devices: 72.5 us -> none  [the longest x1 38.1 us: body(): block_b = lax.all_gather(unit_b, 'row', axis=0, tiled=True)]
    all_to_all x0 -> x4, waiting for transfers between devices: none -> 49.3 us  [the longest x1 24.9 us: body(): lax.all_to_all(grads.reshape(8, views, width), axes, 0, 0, tiled=True, ax...]
    all_to_all x0 -> x2, blocking collectives: none -> 42.7 us  [spread(): return lax.all_to_all(v, axes, 0, 0, tiled=True, axis_index_groups=groups)]
    dot_general x3 -> x0, matrix products: 25.8 us -> none  [the longest x1 10.7 us: body(): jnp.einsum('ik,jk->ij', block_a, block_b, preferred_element_type=jnp.floa...]
    pallas_call x0 -> x4, Pallas kernels: none -> 25 us  [the longest x1 10.5 us: body(): pl.pallas_call(score_kernel, grid=(n_a // bm,), out_shape=[jax.ShapeDtype...]
    all_gather x1 -> x0, blocking collectives: 21.9 us -> none  [body(): lax.all_gather(partner, 'col', axis=0, tiled=True)]
  transfers between devices with their start and end apart: 4 -> 6, of which waited for: 4 -> 5; matrix products, arithmetic and copies ran while one was open for 3% -> 5% of each run, Pallas kernels for 0% -> 0%
where the time goes in v1:
time: 166 us; the launch traced here: 165 us
  waiting for transfers between devices  50.1 us (30%)
  blocking collectives  42.7 us (26%)
  Pallas kernels  25 us (15%)
  starting transfers between devices  21 us (13%)
  other arithmetic  13.3 us (8%)
  local copies, waits for them, and re-layouts  6.97 us (4%)
  between operations  6.31 us (4%)
    all_to_all x2, blocking collectives, spread(): return lax.all_to_all(v, axes, 0, 0, tiled=True, axis_index_groups=groups)  42.7 us
    all_to_all x1, waiting for transfers between devices, body(): lax.all_to_all(grads.reshape(8, views, width), axes, 0, 0, tiled=True, ax...  24.9 us
    all_to_all x3, waiting for transfers between devices, spread(): return lax.all_to_all(v, axes, 0, 0, tiled=True, axis_index_groups=groups)  24.4 us
    all_to_all x3, starting transfers between devices, spread(): return lax.all_to_all(v, axes, 0, 0, tiled=True, axis_index_groups=groups)  12.6 us
    pallas_call x1, Pallas kernels, body(): pl.pallas_call(score_kernel, grid=(n_a // bm,), out_shape=[jax.ShapeDtype...  10.5 us
    pallas_call x1, Pallas kernels, body(): pl.pallas_call(grad_kernel, grid=(n_a // bm,), out_shape=jax.ShapeDtypeSt...  9.82 us
    concatenate x1, other arithmetic, body(): block_b = jnp.concatenate([block_b, block_b2], axis=0)  4.64 us
    unnamed x13, local copies, waits for them, and re-layouts  3.82 us
  transfers between devices with their start and end apart: 6, of which 5 were waited for; matrix products, arithmetic and copies ran while one was open for 5% of the time, Pallas kernels for 0%

profile of v1, /device:TPU:1, one launch (start us, length us, event | category | flops | bytes accessed | tf_op | source)
XLA Modules:
  0.0 165.4 jit_solution(8098653600163248865)
XLA Ops:
  0.6 1.8 %shard_map.68 = bf16[128,1024]{1,0:T(8,128)(2,1)} custom-call(bf16[128,1024]{1,0:T(8,128)(2,1)} %x_ref.3), custom_call_target="tpu_custom_call" | custom-call | tf_op jit(solution)/shard_map/pallas_call | solution.py:96
  2.4 1.2 broadcast_in_dim.8
  3.7 32.4 %all_to_all.30 = bf16[8,128,1024]{2,1,0:T(8,128)(2,1)} all-to-all(bf16[8,128,1024]{2,1,0:T(8,128)(2,1)S(1)} %broadcast_in_dim.8), channel_id=1, replica_groups={{16,48,80,112,4,36,68,100},{24,56,88,120,12,44,76,108},{20,52,84,116,0,..., dimensions={0} | all-to-all | bytes 4194304 | tf_op jit(solution)/shard_map/all_to_all | solution.py:94
  36.0 1.8 %collective-permute-start = (bf16[1024,1024]{1,0:T(8,128)(2,1)}, bf16[1024,1024]{1,0:T(8,128)(2,1)}, u32[]{:S(2)}, u32[]{:S(2)}) collective-permute-start(bf16[1024,1024]{1,0:T(8,128)(2,1)} %bitcast.1), channel_id=1, source_target_pairs={{0,8},{1,9},{2,10},{3,11},{4,12},{5,13},{6,14},{7,15},{8,0},{9,1},... | collective-permute-start | bytes 6291464 | tf_op jit(solution)/shard_map/ppermute | solution.py:102
  37.9 10.3 %all_to_all.31 = s32[8,1,128]{2,1,0:T(1,128)S(1)} all-to-all(s32[8,1,128]{2,1,0:T(1,128)S(1)} %broadcast_in_dim.9), channel_id=1, replica_groups={{0,1,2,3,16,17,18,19},{8,9,10,11,24,25,26,27},{4,5,6,7,20,21,22,23},{12..., dimensions={0} | all-to-all | bytes 8192 | tf_op jit(solution)/shard_map/all_to_all | solution.py:94
  48.2 3.6 %all-to-all-start = ((bf16[8,128,1024]{2,1,0:T(8,128)(2,1)}), bf16[8,128,1024]{2,1,0:T(8,128)(2,1)S(1)}, u32[]{:S(2)}, u32[]{:S(2)}) async-start(bf16[8,128,1024]{2,1,0:T(8,128)(2,1)} %copy-done.3), calls=%async_computation | async-start | bytes 4194304 | tf_op jit(solution)/shard_map/all_to_all | solution.py:94
  54.6 4.6 %pad_maximum_fusion.b_ref = bf16[2048,1024]{1,0:T(8,128)(2,1)} fusion(bf16[1024,1024]{1,0:T(8,128)(2,1)} %collective-permute-done, bf16[1024,1024]{1,0:T(8,128)(2,1)} %bitcast.1), kind=kLoop, calls=%fused_computation | loop fusion | flops 8388608 | bytes 8388608 | tf_op jit(solution)/shard_map/concatenate | solution.py:103
  59.2 18.6 %all-to-all-done = bf16[8,128,1024]{2,1,0:T(8,128)(2,1)S(1)} async-done(((bf16[8,128,1024]{2,1,0:T(8,128)(2,1)}), bf16[8,128,1024]{2,1,0:T(8,128)(2,1)S(1)}, u32[]{:S(2)}, u32[]{:S(2)}) %all-to-all-start) | async-done | bytes 2097184 | tf_op jit(solution)/shard_map/all_to_all | solution.py:94
  77.8 10.5 %shard_map.69 = (f32[1024,2048]{1,0:T(8,128)}, f32[1024,1]{1,0:T(8,128)S(1)}, f32[1024,1]{1,0:T(8,128)S(1)}, f32[1024,1]{1,0:T(8,128)S(1)}) custom-call(f32[1]{0:T(128)S(6)} %copy.25.scale_ref, bf16[1024,1024]{1,0:T(8,128)(2,1)S(1)} %bitcast.39, bf16[2048,1024]{1,0:T(8,128)(2,1)} %pad_maximum_fusion.b_ref, s32[1024,1]{1,0:T(8,128)S(1)} %copy.18.rows_ref, ...), custom_call_target="tpu_custom_call" | custom-call | tf_op jit(solution)/shard_map/pallas_call | solution.py:114
  89.9 0.8 copy-done.2
  90.8 1.2 reduce.21
  92.0 1.2 reduce.22
  93.3 1.2 reduce.23
  95.2 3.7 %all-to-all-start.3 = ((f32[8,24,128]{2,1,0:T(8,128)}), f32[8,24,128]{2,1,0:T(8,128)S(1)}, u32[]{:S(2)}, u32[]{:S(2)}) async-start(f32[8,24,128]{2,1,0:T(8,128)} %broadcast_in_dim.10), calls=%async_computation.3 | async-start | bytes 196608 | tf_op jit(solution)/shard_map/all_to_all | solution.py:94
  98.9 1.4 bitcast_reduce_fusion.1
  102.1 2.1 %all-to-all-done.3 = f32[8,24,128]{2,1,0:T(8,128)S(1)} async-done(((f32[8,24,128]{2,1,0:T(8,128)}), f32[8,24,128]{2,1,0:T(8,128)S(1)}, u32[]{:S(2)}, u32[]{:S(2)}) %all-to-all-start.3) | async-done | bytes 98336 | tf_op jit(solution)/shard_map/all_to_all | solution.py:94
  107.4 5.3 %all-to-all-start.4 = ((f32[8,2,128]{2,1,0:T(2,128)}), f32[8,2,128]{2,1,0:T(2,128)S(1)}, u32[]{:S(2)}, u32[]{:S(2)}) async-start(f32[8,2,128]{2,1,0:T(2,128)} %broadcast_in_dim.11), calls=%async_computation.4 | async-start | bytes 16384 | tf_op jit(solution)/shard_map/all_to_all | solution.py:94
  112.9 3.6 %all-to-all-done.4 = f32[8,2,128]{2,1,0:T(2,128)S(1)} async-done(((f32[8,2,128]{2,1,0:T(2,128)}), f32[8,2,128]{2,1,0:T(2,128)S(1)}, u32[]{:S(2)}, u32[]{:S(2)}) %all-to-all-start.4) | async-done | bytes 8224 | tf_op jit(solution)/shard_map/all_to_all | solution.py:94
  116.5 3.1 %collective-permute-start.1 = (f32[8,2,128]{2,1,0:T(2,128)S(1)}, f32[8,2,128]{2,1,0:T(2,128)S(1)}, u32[]{:S(2)}, u32[]{:S(2)}) collective-permute-start(f32[8,2,128]{2,1,0:T(2,128)S(1)} %all-to-all-done.4), channel_id=1, source_target_pairs={{0,8},{1,9},{2,10},{3,11},{4,12},{5,13},{6,14},{7,15},{8,0},{9,1},... | collective-permute-start | bytes 24584 | tf_op jit(solution)/shard_map/ppermute | solution.py:144
  120.4 9.8 %shard_map.70 = bf16[1024,1024]{1,0:T(8,128)(2,1)} custom-call(f32[1024,2048]{1,0:T(8,128)} %get-tuple-element.11.s_ref, bf16[2048,1024]{1,0:T(8,128)(2,1)} %pad_maximum_fusion.b_ref, f32[1024,1]{1,0:T(8,128)S(1)} %copy.21.lse_row_ref, f32[1,2048]{1,0:T(1,128)S(1)} %slice_bitcast_fusion.1.lse_col_ref, s32[1024,1]{1,0:T(8,128)S(1)} %copy.19.mates_ref, ...), custom_call_target="tpu_custom_call" | custom-call | tf_op jit(solution)/shard_map/pallas_call | solution.py:149
  130.2 3.6 %all-to-all-start.5 = ((bf16[8,128,1024]{2,1,0:T(8,128)(2,1)}), bf16[8,128,1024]{2,1,0:T(8,128)(2,1)S(1)}, u32[]{:S(2)}, u32[]{:S(2)}) async-start(bf16[8,128,1024]{2,1,0:T(8,128)(2,1)} %bitcast.14), calls=%async_computation.5 | async-start | bytes 4194304 | tf_op jit(solution)/shard_map/all_to_all | solution.py:164
  135.1 24.9 %all-to-all-done.5.parts_ref = bf16[8,128,1024]{2,1,0:T(8,128)(2,1)S(1)} async-done(((bf16[8,128,1024]{2,1,0:T(8,128)(2,1)}), bf16[8,128,1024]{2,1,0:T(8,128)(2,1)S(1)}, u32[]{:S(2)}, u32[]{:S(2)}) %all-to-all-start.5) | async-done | bytes 2097184 | tf_op jit(solution)/shard_map/all_to_all | solution.py:164
  160.0 1.3 copy-done.4
  161.3 3.0 %shard_map.71 = f32[128,1024]{1,0:T(8,128)} custom-call(f32[1]{0:T(128)S(6)} %copy.25.scale_ref, bf16[128,1024]{1,0:T(8,128)(2,1)} %x_ref.3, bf16[8,128,1024]{2,1,0:T(8,128)(2,1)} %copy-done.4), custom_call_target="tpu_custom_call" | custom-call | tf_op jit(solution)/shard_map/pallas_call | solution.py:165
  (34 shorter events, 7.9 us)
Async XLA Ops:
  0.6 37.2 %copy-start.5 = (s32[128]{0:T(128)S(1)}, s32[128]{0:T(128)}, u32[]{:S(2)}) copy-start(s32[128]{0:T(128)} %param.6) | copy-start | bytes 1540
  3.6 34.2 %copy-start.3 = (bf16[8,128,1024]{2,1,0:T(8,128)(2,1)}, bf16[8,128,1024]{2,1,0:T(8,128)(2,1)S(1)}, u32[]{:S(2)}) copy-start(bf16[8,128,1024]{2,1,0:T(8,128)(2,1)S(1)} %broadcast_in_dim.8) | copy-start | bytes 6291460
  36.0 18.5 %collective-permute-start = (bf16[1024,1024]{1,0:T(8,128)(2,1)}, bf16[1024,1024]{1,0:T(8,128)(2,1)}, u32[]{:S(2)}, u32[]{:S(2)}) collective-permute-start(bf16[1024,1024]{1,0:T(8,128)(2,1)} %bitcast.1), channel_id=1, source_target_pairs={{0,8},{1,9},{2,10},{3,11},{4,12},{5,13},{6,14},{7,15},{8,0},{9,1},... | collective-permute-start | bytes 6291464 | tf_op jit(solution)/shard_map/ppermute | solution.py:102
  48.2 29.7 %all-to-all-start = ((bf16[8,128,1024]{2,1,0:T(8,128)(2,1)}), bf16[8,128,1024]{2,1,0:T(8,128)(2,1)S(1)}, u32[]{:S(2)}, u32[]{:S(2)}) async-start(bf16[8,128,1024]{2,1,0:T(8,128)(2,1)} %copy-done.3), calls=%async_computation | async-start | bytes 4194304 | tf_op jit(solution)/shard_map/all_to_all | solution.py:94
  88.3 0.8 copy-start
  89.1 0.8 copy-start.1
  89.9 0.8 copy-start.2
  95.2 9.0 %all-to-all-start.3 = ((f32[8,24,128]{2,1,0:T(8,128)}), f32[8,24,128]{2,1,0:T(8,128)S(1)}, u32[]{:S(2)}, u32[]{:S(2)}) async-start(f32[8,24,128]{2,1,0:T(8,128)} %broadcast_in_dim.10), calls=%async_computation.3 | async-start | bytes 196608 | tf_op jit(solution)/shard_map/all_to_all | solution.py:94
  107.4 9.1 %all-to-all-start.4 = ((f32[8,2,128]{2,1,0:T(2,128)}), f32[8,2,128]{2,1,0:T(2,128)S(1)}, u32[]{:S(2)}, u32[]{:S(2)}) async-start(f32[8,2,128]{2,1,0:T(2,128)} %broadcast_in_dim.11), calls=%async_computation.4 | async-start | bytes 16384 | tf_op jit(solution)/shard_map/all_to_all | solution.py:94
  116.5 3.9 %collective-permute-start.1 = (f32[8,2,128]{2,1,0:T(2,128)S(1)}, f32[8,2,128]{2,1,0:T(2,128)S(1)}, u32[]{:S(2)}, u32[]{:S(2)}) collective-permute-start(f32[8,2,128]{2,1,0:T(2,128)S(1)} %all-to-all-done.4), channel_id=1, source_target_pairs={{0,8},{1,9},{2,10},{3,11},{4,12},{5,13},{6,14},{7,15},{8,0},{9,1},... | collective-permute-start | bytes 24584 | tf_op jit(solution)/shard_map/ppermute | solution.py:144
  130.2 29.8 %all-to-all-start.5 = ((bf16[8,128,1024]{2,1,0:T(8,128)(2,1)}), bf16[8,128,1024]{2,1,0:T(8,128)(2,1)S(1)}, u32[]{:S(2)}, u32[]{:S(2)}) async-start(bf16[8,128,1024]{2,1,0:T(8,128)(2,1)} %bitcast.14), calls=%async_computation.5 | async-start | bytes 4194304 | tf_op jit(solution)/shard_map/all_to_all | solution.py:164
  160.0 1.4 copy-start.4

commit v2 on v0

v2 whole, which is shorter than its diff:
```python
import functools

import jax
import jax.numpy as jnp
from jax import lax
from jax.experimental import pallas as pl
from jax.experimental.pallas import tpu as pltpu
from jax.sharding import PartitionSpec as P

F32 = jnp.float32
BF16 = jnp.bfloat16
BLOCK = 256
VMEM = pl.BlockSpec(memory_space=pltpu.VMEM)
SMEM = pl.BlockSpec(memory_space=pltpu.SMEM)


def eye(n):
    return lax.broadcasted_iota(jnp.int32, (n, n), 0) == lax.broadcasted_iota(jnp.int32, (n, n), 1)


def to_column(row):
    n = row.shape[1]
    return jnp.sum(jnp.where(eye(n), row, jnp.zeros_like(row)), axis=1, keepdims=True)


def to_row(column):
    n = column.shape[0]
    return jnp.sum(jnp.where(eye(n), column, jnp.zeros_like(column)), axis=0, keepdims=True)


def unit_kernel(x_ref, out_ref, copies_ref):
    flat = x_ref[...].astype(F32)
    inv = lax.rsqrt(jnp.sum(flat * flat, axis=1, keepdims=True) + 1e-06)
    unit_b = (flat * inv).astype(BF16)
    out_ref[...] = unit_b
    for i in range(copies_ref.shape[0]):
        copies_ref[i] = unit_b


def columns_of(mates_ref, start, shards):
    return jnp.concatenate([to_column(mates_ref[pl.ds(start + i, 1), :]) for i in range(shards)], axis=0)


def score_kernel(place_ref, scale_ref, a_ref, b_ref, mates_ref, s_ref, stats_ref):
    step = pl.program_id(0)
    row_pos, col_pos = place_ref[0], place_ref[1]
    scale = scale_ref[0]
    a = a_ref[...]
    n_b, lanes = b_ref.shape[0], 128
    wide = 512
    for j in range(n_b // wide):
        part = lax.dot_general(
            a, b_ref[j * wide : (j + 1) * wide, :], (((1,), (1,)), ((), ())), preferred_element_type=F32
        )
        s_ref[:, j * wide : (j + 1) * wide] = part * scale
    per = BLOCK // lanes

    @pl.when(col_pos // per == step)
    def _():
        rows = pl.ds(pl.multiple_of(col_pos % per * lanes, lanes), lanes)
        cols = pl.ds(pl.multiple_of(row_pos * lanes, lanes), lanes)
        s_ref[rows, cols] = jnp.where(eye(lanes), -jnp.inf, s_ref[rows, cols])

    for i in range(per):
        rows = slice(i * lanes, (i + 1) * lanes)
        mates = to_column(mates_ref[pl.ds(step * per + i, 1), :])
        lane = lax.broadcasted_iota(jnp.int32, (lanes, lanes), 1)
        peak = s_ref[rows, 0:lanes]
        for t in range(1, n_b // lanes):
            peak = jnp.maximum(peak, s_ref[rows, t * lanes : (t + 1) * lanes])
        peak = jnp.max(peak, axis=1, keepdims=True)
        sums = jnp.zeros((lanes, lanes), F32)
        pos = jnp.zeros((lanes, lanes), F32)
        for t in range(n_b // lanes):
            s = s_ref[rows, t * lanes : (t + 1) * lanes]
            sums = sums + jnp.exp(s - peak)
            pos = pos + jnp.where(lane == mates - t * lanes, s, 0.0)
        shard = step * per + i
        peak, sums, pos = (to_row(v) for v in (peak, jnp.sum(sums, axis=1, keepdims=True), jnp.sum(pos, axis=1, keepdims=True)))
        for dest in range(stats_ref.shape[0]):
            stats_ref[dest, 0, pl.ds(shard, 1), :] = peak
            stats_ref[dest, 1, pl.ds(shard, 1), :] = sums
            stats_ref[dest, 2, pl.ds(shard, 1), :] = pos


def merge_kernel(place_ref, stats_ref, lse_ref, out_ref):
    peak = jnp.max(stats_ref[:, 0], axis=0)
    total = jnp.zeros_like(peak)
    pos = jnp.zeros_like(peak)
    for i in range(stats_ref.shape[0]):
        total = total + stats_ref[i, 1] * jnp.exp(stats_ref[i, 0] - peak)
        pos = pos + stats_ref[i, 2]
    lse = peak + jnp.log(total)
    lse_ref[...] = lse
    shard = lax.broadcasted_iota(jnp.int32, lse.shape, 0)
    own = jnp.sum(jnp.where(shard == place_ref[1], lse, 0.0), axis=0, keepdims=True)
    loss = jnp.sum(lse - pos, axis=0, keepdims=True)
    for i in range(out_ref.shape[0]):
        out_ref[i, 0:1, :] = own
        out_ref[i, 1:2, :] = loss


def grad_kernel(s_ref, b_ref, lse_ref, others_ref, mates_ref, out_ref, loss_ref, d_ref):
    step = pl.program_id(0)
    lanes = 128
    per = BLOCK // lanes
    for i in range(per):
        rows = slice(i * lanes, (i + 1) * lanes)
        mates = to_column(mates_ref[pl.ds(step * per + i, 1), :])
        own = to_column(lse_ref[pl.ds(step * per + i, 1), :])
        lane = lax.broadcasted_iota(jnp.int32, (lanes, lanes), 1)
        for t in range(others_ref.shape[0]):
            cols = slice(t * lanes, (t + 1) * lanes)
            s = s_ref[rows, cols]
            mate = jnp.where(lane == mates - t * lanes, 1.0, 0.0)
            d = (jnp.exp(s - own) - mate) + (jnp.exp(s - others_ref[t, 0:1, :]) - mate)
            d_ref[rows, cols] = d.astype(BF16)
    out_ref[...] = jnp.dot(d_ref[...], b_ref[...], preferred_element_type=F32).astype(BF16)
    total = jnp.sum(others_ref[:, 1, :], axis=0, keepdims=True)
    loss_ref[...] = jnp.sum(total, axis=1, keepdims=True)


def final_kernel(scale_ref, x_ref, parts_ref, out_ref):
    flat = x_ref[...].astype(F32)
    inv = lax.rsqrt(jnp.sum(flat * flat, axis=1, keepdims=True) + 1e-06)
    unit = flat * inv
    dunit = parts_ref[0].astype(F32)
    for i in range(1, parts_ref.shape[0]):
        dunit = dunit + parts_ref[i].astype(F32)
    dunit = dunit * scale_ref[0]
    out_ref[...] = inv * (dunit - unit * jnp.sum(unit * dunit, axis=1, keepdims=True))


def shape(dims, dtype):
    return jax.ShapeDtypeStruct(dims, dtype)


def body(embeddings, partner, inv_temp):
    views, width = embeddings.shape
    n_row, n_col = lax.axis_size("row"), lax.axis_size("col")
    n_a, n_b, total = n_col * views, n_row * views, n_row * n_col * views
    row_pos, col_pos = lax.axis_index("row"), lax.axis_index("col")
    place = jnp.stack([row_pos, col_pos]).astype(jnp.int32)

    unit_b, copies = pl.pallas_call(
        unit_kernel,
        out_shape=[shape((views, width), BF16), shape((n_col, views, width), BF16)],
        in_specs=[VMEM],
        out_specs=[VMEM, VMEM],
    )(embeddings)
    block_b = lax.all_gather(unit_b, "row", axis=0, tiled=True)
    block_a = lax.all_to_all(copies, "col", 0, 0, tiled=True).reshape(n_a, width)
    shard, lane = partner // views, partner % views
    local = shard // n_col * views + lane
    dest = jnp.arange(n_col, dtype=jnp.int32)[:, None]
    sent = jnp.where((shard % n_col)[None, :] == dest, local[None, :], -(1 << 20))
    mates = lax.all_to_all(sent.reshape(n_col, 1, views), "col", 0, 0, tiled=True).reshape(n_col, views)

    steps = (n_a // BLOCK,)
    params = pltpu.CompilerParams(vmem_limit_bytes=48 << 20)
    whole = lambda *dims: pl.BlockSpec(dims, lambda i: (0,) * len(dims))
    scores, stats = pl.pallas_call(
        score_kernel,
        grid=steps,
        out_shape=[shape((n_a, n_b), F32), shape((n_col, 3, n_col, views), F32)],
        in_specs=[SMEM, SMEM, pl.BlockSpec((BLOCK, width), lambda i: (i, 0)), whole(n_b, width), whole(n_col, views)],
        out_specs=[pl.BlockSpec((BLOCK, n_b), lambda i: (i, 0)), whole(n_col, 3, n_col, views)],
        compiler_params=params,
    )(place, inv_temp, block_a, block_b, mates)
    stats = lax.all_to_all(stats, "col", 0, 0, tiled=True)
    lse, own = pl.pallas_call(
        merge_kernel,
        out_shape=[shape((n_col, views), F32), shape((n_row, 2, views), F32)],
        in_specs=[SMEM, VMEM],
        out_specs=[VMEM, VMEM],
    )(place, stats)
    others = lax.all_to_all(own, "row", 0, 0, tiled=True)
    grads, loss = pl.pallas_call(
        grad_kernel,
        grid=steps,
        out_shape=[shape((n_a, width), BF16), shape((1, 1), F32)],
        in_specs=[
            pl.BlockSpec((BLOCK, n_b), lambda i: (i, 0)),
            whole(n_b, width),
            whole(n_col, views),
            whole(n_row, 2, views),
            whole(n_col, views),
        ],
        out_specs=[pl.BlockSpec((BLOCK, width), lambda i: (i, 0)), whole(1, 1)],
        scratch_shapes=[pltpu.VMEM((BLOCK, n_b), BF16)],
        compiler_params=params,
    )(scores, block_b, lse, others, mates)
    parts = lax.all_to_all(grads.reshape(n_col, views, width), "col", 0, 0, tiled=True)
    grad_embed = pl.pallas_call(
        final_kernel,
        out_shape=shape((views, width), F32),
        in_specs=[SMEM, VMEM, VMEM],
        out_specs=VMEM,
    )(inv_temp / total, embeddings, parts)
    return (loss / total).reshape(1), grad_embed


def solution(mesh):
    in_specs = (P(("row", "col"), None), P(("row", "col")), P())
    out_specs = (P(), P(("row", "col"), None))
    return jax.shard_map(body, mesh=mesh, in_specs=in_specs, out_specs=out_specs, check_vma=False)
```

time: 370 us -> 160 us (0.43)
  waiting for transfers between devices: 175 us -> 64.2 us
  blocking collectives: 133 us -> 38.2 us
  Pallas kernels: 0 us -> 29.7 us
  matrix products: 25.8 us -> 0 us
  other arithmetic: 16.8 us -> 1.42 us
  starting transfers between devices: 0.16 us -> 7.25 us
    reduce_scatter x2 -> x0, waiting for transfers between devices: 102 us -> none  [the longest x1 98.7 us: body(): lax.psum_scatter(jnp.einsum('ij,ik->jk', picked, block_a, preferred_eleme...]
    psum x2 -> x0, blocking collectives: 90.4 us -> none  [the longest x1 74.7 us: body(): lax.psum(jnp.sum(own_terms), ('row', 'col')) / total_views]
    all_to_all x0 -> x2, waiting for transfers between devices: none -> 64.2 us  [the longest x1 38.7 us: body(): lax.all_to_all(copies, 'col', 0, 0, tiled=True).reshape(n_a, width)]
    all_to_all x0 -> x3, blocking collectives: none -> 38.2 us  [the longest x1 14.8 us: body(): lax.all_to_all(sent.reshape(n_col, 1, views), 'col', 0, 0, tiled=True)]
    all_gather x1, waiting for transfers between devices: 38.1 us -> 0.01 us  [body(): block_b = lax.all_gather(unit_b, 'row', axis=0, tiled=True)]
    all_gather x1 -> x0, waiting for transfers between devices: 34.3 us -> none  [body(): lax.all_gather(unit_b, 'col', axis=0, tiled=True)]
    pallas_call x0 -> x5, Pallas kernels: none -> 29.7 us  [the longest x1 11.6 us: body(): pl.pallas_call(grad_kernel, grid=steps, out_shape=[shape((n_a, width), BF...]
    dot_general x3 -> x0, matrix products: 25.8 us -> none  [the longest x1 10.7 us: body(): jnp.einsum('ik,jk->ij', block_a, block_b, preferred_element_type=jnp.floa...]
  transfers between devices with their start and end apart: 4 -> 3, of which waited for: 4 -> 2; matrix products, arithmetic and copies ran while one was open for 3% -> 1% of each run, Pallas kernels for 0% -> 0%
where the time goes in v2:
time: 160 us; the launch traced here: 159 us
  waiting for transfers between devices  64.2 us (40%)
  blocking collectives  38.2 us (24%)
  Pallas kernels  29.7 us (19%)
  between operations  16.5 us (10%)
  starting transfers between devices  7.25 us (5%)
  local copies, waits for them, and re-layouts  2.02 us (1%)
    all_to_all x1, waiting for transfers between devices, body(): lax.all_to_all(copies, 'col', 0, 0, tiled=True).reshape(n_a, width)  38.7 us
    all_to_all x1, waiting for transfers between devices, body(): lax.all_to_all(grads.reshape(n_col, views, width), 'col', 0, 0, tiled=True)  25.5 us
    all_to_all x1, blocking collectives, body(): lax.all_to_all(sent.reshape(n_col, 1, views), 'col', 0, 0, tiled=True)  14.8 us
    all_to_all x1, blocking collectives, body(): others = lax.all_to_all(own, 'row', 0, 0, tiled=True)  12.6 us
    pallas_call x1, Pallas kernels, body(): pl.pallas_call(grad_kernel, grid=steps, out_shape=[shape((n_a, width), BF...  11.6 us
    pallas_call x1, Pallas kernels, body(): pl.pallas_call(score_kernel, grid=steps, out_shape=[shape((n_a, n_b), F32...  11.1 us
    all_to_all x1, blocking collectives, body(): stats = lax.all_to_all(stats, 'col', 0, 0, tiled=True)  10.9 us
    all_to_all x1, starting transfers between devices, body(): lax.all_to_all(copies, 'col', 0, 0, tiled=True).reshape(n_a, width)  3.61 us
  transfers between devices with their start and end apart: 3, of which 2 were waited for; matrix products, arithmetic and copies ran while one was open for 1% of the time, Pallas kernels for 0%

profile of v2, /device:TPU:1, one launch (start us, length us, event | category | flops | bytes accessed | tf_op | source)
XLA Modules:
  0.0 159.3 jit_solution(8174051850830695814)
XLA Ops:
  7.2 0.0 all-gather.2.cloned.1.call-start
  7.2 2.6 %shard_map.50 = (bf16[128,1024]{1,0:T(8,128)(2,1)}, bf16[8,128,1024]{2,1,0:T(8,128)(2,1)}) custom-call(bf16[128,1024]{1,0:T(8,128)(2,1)} %x_ref.3), custom_call_target="tpu_custom_call" | custom-call | tf_op jit(solution)/shard_map/pallas_call | solution.py:145
  9.8 0.0 all-gather.2.cloned.1.call-update
  9.9 0.7 and_select_fusion.2
  10.5 0.7 fusion
  11.2 14.8 %all_to_all.25 = s32[8,1,128]{2,1,0:T(1,128)S(1)} all-to-all(s32[8,1,128]{2,1,0:T(1,128)S(1)} %compare_select_fusion), channel_id=1, replica_groups=mesh['row'=16,'col'=8] {'col'}, dimensions={0} | all-to-all | bytes 8192 | tf_op jit(solution)/shard_map/all_to_all | solution.py:157
  26.0 3.6 %all-to-all-start = ((bf16[8,128,1024]{2,1,0:T(8,128)(2,1)}), bf16[8,128,1024]{2,1,0:T(8,128)(2,1)S(1)}, u32[]{:S(2)}, u32[]{:S(2)}) async-start(bf16[8,128,1024]{2,1,0:T(8,128)(2,1)} %get-tuple-element.10), calls=%async_computation | async-start | bytes 4194304 | tf_op jit(solution)/shard_map/all_to_all | solution.py:152
  30.3 0.1 pad_add_fusion.place_ref
  30.4 0.0 copy-start.1
  30.4 38.7 %all-to-all-done = bf16[8,128,1024]{2,1,0:T(8,128)(2,1)S(1)} async-done(((bf16[8,128,1024]{2,1,0:T(8,128)(2,1)}), bf16[8,128,1024]{2,1,0:T(8,128)(2,1)S(1)}, u32[]{:S(2)}, u32[]{:S(2)}) %all-to-all-start) | async-done | bytes 2097184 | tf_op jit(solution)/shard_map/all_to_all | solution.py:152
  69.0 0.0 all-gather.2.cloned.1.call-done.b_ref
  69.0 11.1 %shard_map.51 = (f32[1024,2048]{1,0:T(8,128)}, f32[8,3,8,128]{3,2,1,0:T(8,128)S(1)}) custom-call(s32[2]{0:T(128)S(1)} %pad_add_fusion.place_ref, f32[1]{0:T(128)S(6)} %copy.5.scale_ref, bf16[1024,1024]{1,0:T(8,128)(2,1)S(1)} %bitcast.6, bf16[2048,1024]{1,0:T(8,128)(2,1)} %all-gather.2.cloned.1.call-done.b_ref, s32[8,128]{1,0:T(8,128)S(1)} %bitcast.7), custom_call_target="tpu_custom_call" | custom-call | tf_op jit(solution)/shard_map/pallas_call | solution.py:162
  80.1 0.0 copy-done.1
  80.1 10.9 %all_to_all.26.stats_ref = f32[8,3,8,128]{3,2,1,0:T(8,128)} all-to-all(f32[8,3,8,128]{3,2,1,0:T(8,128)S(1)} %get-tuple-element.13), channel_id=1, replica_groups=mesh['row'=16,'col'=8] {'col'}, dimensions={0} | all-to-all | bytes 196608 | tf_op jit(solution)/shard_map/all_to_all | solution.py:170
  91.0 1.6 shard_map.52
  92.5 12.6 %all_to_all.27.others_ref = f32[16,2,128]{2,1,0:T(2,128)S(1)} all-to-all(f32[16,2,128]{2,1,0:T(2,128)} %get-tuple-element.15), channel_id=1, replica_groups=mesh['row'=16,'col'=8] {'row'}, dimensions={0} | all-to-all | bytes 32768 | tf_op jit(solution)/shard_map/all_to_all | solution.py:177
  105.1 0.0 copy-start
  105.1 0.7 copy-done
  105.7 11.6 %shard_map.53 = (bf16[1024,1024]{1,0:T(8,128)(2,1)}, f32[1,1]{1,0:T(1,128)}) custom-call(f32[1024,2048]{1,0:T(8,128)} %get-tuple-element.12.s_ref, bf16[2048,1024]{1,0:T(8,128)(2,1)} %all-gather.2.cloned.1.call-done.b_ref, f32[8,128]{1,0:T(8,128)S(1)} %copy-done, f32[16,2,128]{2,1,0:T(2,128)S(1)} %all_to_all.27.others_ref, s32[8,128]{1,0:T(8,128)S(1)} %bitcast.8), custom_call_target="tpu_custom_call" | custom-call | tf_op jit(solution)/shard_map/pallas_call | solution.py:178
  117.3 3.6 %all-to-all-start.4 = ((bf16[8,128,1024]{2,1,0:T(8,128)(2,1)}), bf16[8,128,1024]{2,1,0:T(8,128)(2,1)S(1)}, u32[]{:S(2)}, u32[]{:S(2)}) async-start(bf16[8,128,1024]{2,1,0:T(8,128)(2,1)} %bitcast.5), calls=%async_computation.4 | async-start | bytes 4194304 | tf_op jit(solution)/shard_map/all_to_all | solution.py:193
  121.6 25.5 %all-to-all-done.4.parts_ref = bf16[8,128,1024]{2,1,0:T(8,128)(2,1)S(1)} async-done(((bf16[8,128,1024]{2,1,0:T(8,128)(2,1)}), bf16[8,128,1024]{2,1,0:T(8,128)(2,1)S(1)}, u32[]{:S(2)}, u32[]{:S(2)}) %all-to-all-start.4) | async-done | bytes 2097184 | tf_op jit(solution)/shard_map/all_to_all | solution.py:193
  147.1 0.0 copy-start.2
  147.1 1.3 copy-done.2
  148.4 2.9 %shard_map.54 = f32[128,1024]{1,0:T(8,128)} custom-call(f32[1]{0:T(128)S(6)} %div.37.scale_ref, bf16[128,1024]{1,0:T(8,128)(2,1)} %x_ref.3, bf16[8,128,1024]{2,1,0:T(8,128)(2,1)} %copy-done.2), custom_call_target="tpu_custom_call" | custom-call | tf_op jit(solution)/shard_map/pallas_call | solution.py:194
  (1 shorter events, 0.0 us)
Async XLA Ops:
  7.2 61.9 %all-gather.2.cloned.1.call-start = ((), (), s32[]{:S(2)}) async-start(), calls=%async_computation.5 | async-start | bytes 4456448 | tf_op jit(solution)/shard_map/all_gather | solution.py:151
  26.0 43.0 %all-to-all-start = ((bf16[8,128,1024]{2,1,0:T(8,128)(2,1)}), bf16[8,128,1024]{2,1,0:T(8,128)(2,1)S(1)}, u32[]{:S(2)}, u32[]{:S(2)}) async-start(bf16[8,128,1024]{2,1,0:T(8,128)(2,1)} %get-tuple-element.10), calls=%async_computation | async-start | bytes 4194304 | tf_op jit(solution)/shard_map/all_to_all | solution.py:152
  30.4 49.8 %copy-start.1 = (s32[2]{0:T(128)}, s32[2]{0:T(128)S(1)}, u32[]{:S(2)}) copy-start(s32[2]{0:T(128)S(1)} %pad_add_fusion.place_ref) | copy-start | bytes 28
  105.1 0.7 copy-start
  117.3 29.7 %all-to-all-start.4 = ((bf16[8,128,1024]{2,1,0:T(8,128)(2,1)}), bf16[8,128,1024]{2,1,0:T(8,128)(2,1)S(1)}, u32[]{:S(2)}, u32[]{:S(2)}) async-start(bf16[8,128,1024]{2,1,0:T(8,128)(2,1)} %bitcast.5), calls=%async_computation.4 | async-start | bytes 4194304 | tf_op jit(solution)/shard_map/all_to_all | solution.py:193
  147.1 1.3 copy-start.2
Sparse Core Ops, SparseCore 0:
  10.3 51.1 all-gather.1

commit v3 on v0

v3 whole, which is shorter than its diff:
```python
import functools

import jax
import jax.numpy as jnp
from jax import lax
from jax.experimental import pallas as pl
from jax.experimental.pallas import tpu as pltpu
from jax.sharding import PartitionSpec as P

F32 = jnp.float32
BF16 = jnp.bfloat16
I32 = jnp.int32
LANES = 128
EXTRA = 8
BLOCK = 256
VMEM_LIMIT = 36 << 20
AXES = ("row", "col")
VMEM = pl.BlockSpec(memory_space=pltpu.VMEM)
SMEM = pl.BlockSpec(memory_space=pltpu.SMEM)
ANY = pl.BlockSpec(memory_space=pl.ANY)


def device_id(x, y, z, core):
    return ((x % 4) * 4 + (y % 2) * 2 + core) * 8 + (y % 4) // 2 * 4 + z % 4


def mate_a(y):
    return y ^ 1


def mate_b(y):
    return (y + 1) % 4 if y % 2 else (y - 1) % 4


def to(where):
    pairs = []
    for x in range(4):
        for y in range(4):
            for z in range(4):
                for k in range(2):
                    pairs.append((device_id(x, y, z, k), device_id(*where(x, y, z, k, 1 - 2 * k))))
    return pairs


SWAP = to(lambda x, y, z, k, g: (x, y, z, 1 - k))
ALONG_Z = to(lambda x, y, z, k, g: (x, y, z + g, k))
ALONG_X = to(lambda x, y, z, k, g: (x + g, y, z, k))
ALONG_YZ = to(lambda x, y, z, k, g: (x, mate_a(y), z + g, k))
ALONG_XY = to(lambda x, y, z, k, g: (x + g, mate_b(y), z, k))
ALONG_Y = to(lambda x, y, z, k, g: (x, mate_b(y) if k else mate_a(y), z, k))

PARTNER_A = to(lambda x, y, z, k, g: (x, mate_a(y), z, k))
PARTNER_B = to(lambda x, y, z, k, g: (x, mate_b(y), z, k))
FROM_Z = [to(lambda x, y, z, k, g, d=d: (x, y, z - d, k)) for d in (1, 2, 3)]
FROM_X = [to(lambda x, y, z, k, g, d=d: (x - d, y, z, k)) for d in (1, 2, 3)]

GROUPS_A = [
    [device_id(x, y, z, k) for y in (p, p + 1) for z in range(4)] for x in range(4) for p in (0, 2) for k in range(2)
]
COLUMNS = [
    (0, 0, 0), (0, 0, 1), (-1, 0, 0), (-1, 0, 1), (-1, 1, 0), (-1, 1, 1), (1, 0, 1), (1, 0, 0),
    (1, 1, 1), (1, 1, 0), (2, 0, 0), (2, 1, 0), (2, 0, 1), (2, 1, 1), (0, 1, 0), (0, 1, 1),
]


def eye(n):
    return lax.broadcasted_iota(I32, (n, n), 0) == lax.broadcasted_iota(I32, (n, n), 1)


def to_column(row):
    return jnp.sum(jnp.where(eye(row.shape[1]), row, jnp.zeros_like(row)), axis=1, keepdims=True)


def to_row(column):
    return jnp.sum(jnp.where(eye(column.shape[0]), column, jnp.zeros_like(column)), axis=0, keepdims=True)


def unit_kernel(x_ref, mates_ref, out_ref):
    flat = x_ref[...].astype(F32)
    inv = lax.rsqrt(jnp.sum(flat * flat, axis=1, keepdims=True) + 1e-06)
    out_ref[0:LANES, :] = (flat * inv).astype(BF16)
    mates = mates_ref[...]
    row = jnp.concatenate([mates >> 7, mates & 127, jnp.zeros((1, out_ref.shape[1] - 2 * LANES), I32)], axis=1)
    out_ref[LANES:, :] = jnp.broadcast_to(row.astype(F32), (2 * EXTRA, row.shape[1])).astype(BF16)


def score_kernel(
    place, scale_ref, own, rz, d_a, fz, s_z, ry, s_ry, rx, d_b, s_rx, s_db, fx, s_fx,
    s_ref, b_ref, stats_ref, mates_ref, a_ref,
):
    core, y, z = place[0], place[1], place[2]
    scale = scale_ref[0]
    n, e = LANES, 2 * LANES

    def put(ref, at, src, start, rows=n):
        ref[at * n : at * n + rows, :] = src[start : start + rows, :]

    put(a_ref, 0, own, 0)
    put(a_ref, 1, rz, 0)
    put(a_ref, 2, d_a, 0)
    put(a_ref, 3, fz, 0, e)
    put(a_ref, 5, s_z, 0, e)
    for src, at in ((own, 0), (rx, 2), (d_b, 4), (s_rx, 6), (s_db, 8), (fx, 10), (s_fx, 12)):
        put(b_ref, at, src, 0, e)

    @pl.when(core == 0)
    def _():
        put(a_ref, 7, ry, 0)
        put(b_ref, 14, s_ry, n)
        put(b_ref, 15, s_ry, 0)

    @pl.when(core == 1)
    def _():
        put(a_ref, 7, s_ry, n)
        put(b_ref, 14, ry, 0, e)

    tail = lambda src: src[e : e + 2 * EXTRA, 0 : 2 * n].astype(F32)
    tails = [tail(src) for src in (own, rz, d_a, fz, s_z, ry, s_ry)]
    head = [(0, 0), (1, 0), (2, 0), (3, 0), (3, EXTRA), (4, 0), (4, EXTRA)]
    rows = [tails[p][r : r + 1] for p, r in head]
    rows.append(jnp.where(core == 0, tails[5][0:1], tails[6][EXTRA : EXTRA + 1]))
    rows = jnp.concatenate(rows, axis=0).astype(I32)
    shard, lane = rows[:, 0:n], rows[:, n:]
    mate_x, mate_k, mate_z = shard >> 5, (shard >> 3) & 1, shard & 3
    mate_y = ((shard >> 2) & 1) * 2 + ((shard >> 4) & 1)
    slot = (1 - (mate_y & 1)) * 4 + mate_x + jnp.where(mate_k == core, 0, 8)
    local = jnp.zeros_like(slot)
    for t in range(16):
        local = jnp.where(slot == place[11 + t], t * n + lane, local)
    here = (mate_z == z) & ((((mate_y + 1) & 3) >> 1) == (((y + 1) & 3) >> 1))
    mates_ref[...] = jnp.where(here, local, -1)

    n_a, n_b = s_ref.shape
    wide = 512
    per = BLOCK // n

    def scores_of(step):
        a = a_ref[step * BLOCK : (step + 1) * BLOCK, :]
        for j in range(n_b // wide):
            b = b_ref[j * wide : (j + 1) * wide, :]
            part = lax.dot_general(a, b, (((1,), (1,)), ((), ())), preferred_element_type=F32) * scale
            if step == 0 and j == 0:
                r = lax.broadcasted_iota(I32, (BLOCK, wide), 0)
                c = lax.broadcasted_iota(I32, (BLOCK, wide), 1)
                part = jnp.where((r == c) & (r < n), -jnp.inf, part)
            s_ref[step * BLOCK : (step + 1) * BLOCK, j * wide : (j + 1) * wide] = part

    def stats_of(step):
        lane = lax.broadcasted_iota(I32, (n, n), 1)
        for i in range(per):
            shard = step * per + i
            rows = slice(shard * n, (shard + 1) * n)
            mates = to_column(mates_ref[shard : shard + 1, :])
            peak = s_ref[rows, 0:n]
            for t in range(1, n_b // n):
                peak = jnp.maximum(peak, s_ref[rows, t * n : (t + 1) * n])
            peak = jnp.max(peak, axis=1, keepdims=True)
            sums = jnp.zeros((n, n), F32)
            pos = jnp.zeros((n, n), F32)
            for t in range(n_b // n):
                s = s_ref[rows, t * n : (t + 1) * n]
                sums = sums + jnp.exp(s - peak)
                pos = pos + jnp.where(lane == mates - t * n, s, 0.0)
            values = (peak, jnp.sum(sums, axis=1, keepdims=True), jnp.sum(pos, axis=1, keepdims=True))
            for q, value in enumerate(values):
                value = to_row(value)
                stats_ref[q, pl.ds(place[3 + shard], 1), :] = value

    steps = n_a // BLOCK
    scores_of(0)
    for step in range(steps):
        if step + 1 < steps:
            scores_of(step + 1)
        stats_of(step)


def merge_kernel(place, g0, g1, g2, g3, lse_ref, out_ref):
    y, z = place[1], place[2]
    parts = []
    for slot in range(8):
        turn = jnp.where((y & 1) == slot // 4, 0, 1)
        step = (slot % 4 - z) & 3
        part = g0[turn]
        for d, g in ((1, g1), (2, g2), (3, g3)):
            part = jnp.where(step == d, g[turn], part)
        parts.append(part)
    peak = parts[0][0]
    for part in parts[1:]:
        peak = jnp.maximum(peak, part[0])
    total = jnp.zeros_like(peak)
    pos = jnp.zeros_like(peak)
    for part in parts:
        total = total + part[1] * jnp.exp(part[0] - peak)
        pos = pos + part[2]
    lse = peak + jnp.log(total)
    lse_ref[...] = lse
    shard = lax.broadcasted_iota(I32, lse.shape, 0)
    out_ref[0:1, :] = jnp.sum(jnp.where(shard == place[3], lse, 0.0), axis=0, keepdims=True)
    out_ref[1:2, :] = jnp.sum(lse - pos, axis=0, keepdims=True)


def grad_kernel(
    place, s_ref, b_ref, lse_ref, h0, h1, h2, h3, mates_ref, out, loss_ref, d_ref, o_ref, sems
):
    n = LANES
    per = BLOCK // n
    n_a, n_b = s_ref.shape
    core, y, x = place[0], place[1], place[27]
    total = jnp.zeros((1, n), F32)
    for i in range(16):
        step = (i // 4 - x) & 3
        at = jnp.where((y >> 1) == i // 2 % 2, 0, 2) + jnp.where(core == i % 2, 0, 1)
        part = h0[at, 1:2, :]
        for d, h in ((1, h1), (2, h2), (3, h3)):
            part = jnp.where(step == d, h[at, 1:2, :], part)
        total = total + part
    loss_ref[...] = jnp.sum(total, axis=1, keepdims=True)
    copies = []
    lane = lax.broadcasted_iota(I32, (n, n), 1)

    forward = jnp.where(core == 0, 1, 0)

    def other_lse(t):
        turn, twin = COLUMNS[t][1:]
        at = 2 * turn + twin
        if COLUMNS[t][0] == 0:
            return h0[at, 0:1, :]
        if COLUMNS[t][0] == 2:
            return h2[at, 0:1, :]
        ahead, behind = h1[at, 0:1, :], h3[at, 0:1, :]
        return jnp.where(forward == (1 if COLUMNS[t][0] > 0 else 0), ahead, behind)

    others = [other_lse(t) for t in range(n_b // n)]

    def coefs_of(step):
        for i in range(per):
            shard = step * per + i
            rows = slice(shard * n, (shard + 1) * n)
            mates = to_column(mates_ref[shard : shard + 1, :])
            mine = to_column(lse_ref[pl.ds(place[3 + shard], 1), :])
            for t in range(n_b // n):
                cols = slice(t * n, (t + 1) * n)
                s = s_ref[rows, cols]
                mate = jnp.where(lane == mates - t * n, 1.0, 0.0)
                d = (jnp.exp(s - mine) - mate) + (jnp.exp(s - others[t]) - mate)
                d_ref[rows, cols] = d.astype(BF16)

    def grads_of(step):
        rows = slice(step * BLOCK, (step + 1) * BLOCK)
        o_ref[rows, :] = jnp.dot(d_ref[rows, :], b_ref[...], preferred_element_type=F32).astype(BF16)
        for i in range(per):
            shard = step * per + i
            copies.append(pltpu.make_async_copy(o_ref.at[pl.ds(shard * n, n)], out.at[place[3 + shard]], sems.at[shard]))
            copies[-1].start()

    steps = n_a // BLOCK
    coefs_of(0)
    for step in range(steps):
        if step + 1 < steps:
            coefs_of(step + 1)
        grads_of(step)
    for copy in copies:
        copy.wait()


def final_kernel(scale_ref, x_ref, parts_ref, out_ref):
    flat = x_ref[...].astype(F32)
    inv = lax.rsqrt(jnp.sum(flat * flat, axis=1, keepdims=True) + 1e-06)
    unit = flat * inv
    dunit = parts_ref[0].astype(F32)
    for i in range(1, parts_ref.shape[0]):
        dunit = dunit + parts_ref[i].astype(F32)
    dunit = dunit * scale_ref[0]
    out_ref[...] = inv * (dunit - unit * jnp.sum(unit * dunit, axis=1, keepdims=True))


def shape(dims, dtype):
    return jax.ShapeDtypeStruct(dims, dtype)


def body(embeddings, partner, inv_temp):
    views, width = embeddings.shape
    row, col = lax.axis_index("row").astype(I32), lax.axis_index("col").astype(I32)
    x, core, z = row >> 2, row & 1, col & 3
    y = (col >> 2) * 2 + ((row >> 1) & 1)
    sign = 1 - 2 * core
    other_y = jnp.where((y & 1) == 1, y + 1, y - 1) & 3
    slot_a = lambda yy, zz: (yy & 1) * 4 + (zz & 3)
    slot_b = lambda xx, yy, same: (1 - (yy & 1)) * 4 + (xx & 3) + (0 if same else 8)
    slots_a = [
        slot_a(y, z), slot_a(y, z - sign), slot_a(y ^ 1, z - sign), slot_a(y, z + 2),
        slot_a(y ^ 1, z + 2), slot_a(y, z + sign), slot_a(y ^ 1, z + sign), slot_a(y ^ 1, z),
    ]
    slots_b = [
        slot_b(x, y, True), slot_b(x, y, False),
        slot_b(x - sign, y, True), slot_b(x - sign, y, False),
        slot_b(x - sign, other_y, True), slot_b(x - sign, other_y, False),
        slot_b(x + sign, y, False), slot_b(x + sign, y, True),
        slot_b(x + sign, other_y, False), slot_b(x + sign, other_y, True),
        slot_b(x + 2, y, True), slot_b(x + 2, other_y, True),
        slot_b(x + 2, y, False), slot_b(x + 2, other_y, False),
        slot_b(x, other_y, True), slot_b(x, other_y, False),
    ]
    place = jnp.stack([core, y, z, *slots_a, *slots_b, x]).astype(I32)
    send = lambda v, pairs: lax.ppermute(v, AXES, pairs)
    n = LANES
    params = pltpu.CompilerParams(vmem_limit_bytes=VMEM_LIMIT)

    mine = pl.pallas_call(
        unit_kernel, out_shape=shape((views + 2 * EXTRA, width), BF16), in_specs=[VMEM, VMEM], out_specs=VMEM
    )(embeddings, partner.reshape(1, views))
    twin = send(mine, SWAP)
    own = jnp.concatenate([mine[:n], twin[:n], mine[n : n + EXTRA], twin[n : n + EXTRA]], axis=0)
    both = own[: 2 * n]
    d_a = send(own, ALONG_YZ)
    d_b = send(both, ALONG_XY)
    rz = send(own, ALONG_Z)
    rx = send(both, ALONG_X)
    ry = send(own, ALONG_Y)
    e = 2 * n
    fz = send(jnp.concatenate([rz[:n], d_a[:n], rz[e : e + EXTRA], d_a[e : e + EXTRA]], axis=0), ALONG_Z)
    fx = send(jnp.concatenate([rx[:n], d_b[:n]], axis=0), ALONG_X)
    s_rx, s_db, s_ry = send(rx, SWAP), send(d_b, SWAP), send(ry, SWAP)
    s_z = send(jnp.concatenate([rz[n:e], d_a[n:e], rz[e + EXTRA :], d_a[e + EXTRA :]], axis=0), SWAP)
    s_fx = send(fx, SWAP)

    n_a, n_b = 8 * views, 16 * views
    fast = lambda v: pltpu.with_memory_space_constraint(v, pltpu.VMEM)
    pieces = [fast(v) for v in (own, rz, d_a, fz, s_z, ry, s_ry, rx, d_b, s_rx, s_db, fx, s_fx)]
    scores, block_b, stats, mates = pl.pallas_call(
        score_kernel,
        out_shape=[
            pltpu.VMEM((n_a, n_b), F32),
            pltpu.VMEM((n_b, width), BF16),
            shape((3, 8, views), F32),
            shape((8, views), I32),
        ],
        in_specs=[SMEM, SMEM] + [VMEM] * 13,
        out_specs=[VMEM] * 4,
        scratch_shapes=[pltpu.VMEM((n_a, width), BF16)],
        compiler_params=params,
    )(place, inv_temp, *pieces)
    pair = jnp.stack([stats, send(stats, PARTNER_A)])
    g1, g2, g3 = (send(pair, pairs) for pairs in FROM_Z)
    lse, spread = pl.pallas_call(
        merge_kernel,
        out_shape=[shape((8, views), F32), shape((2, views), F32)],
        in_specs=[SMEM] + [VMEM] * 4,
        out_specs=[VMEM, VMEM],
    )(place, pair, g1, g2, g3)
    twins = jnp.stack([spread, send(spread, SWAP)])
    four = jnp.concatenate([twins, send(twins, PARTNER_B)], axis=0)
    h1, h2, h3 = (send(four, pairs) for pairs in FROM_X)
    grads, loss = pl.pallas_call(
        grad_kernel,
        out_shape=[shape((8, views, width), BF16), shape((1, 1), F32)],
        in_specs=[SMEM] + [VMEM] * 8,
        out_specs=[ANY, VMEM],
        scratch_shapes=[
            pltpu.VMEM((n_a, n_b), BF16),
            pltpu.VMEM((n_a, width), BF16),
            pltpu.SemaphoreType.DMA((8,)),
        ],
        compiler_params=params,
    )(place, fast(scores), fast(block_b), lse, four, h1, h2, h3, mates)
    parts = lax.all_to_all(grads, AXES, 0, 0, tiled=True, axis_index_groups=GROUPS_A)
    total = views * 128
    grad_embed = pl.pallas_call(
        final_kernel,
        out_shape=shape((views, width), F32),
        in_specs=[SMEM, VMEM, VMEM],
        out_specs=VMEM,
    )(inv_temp / total, embeddings, parts)
    return (loss / total).reshape(1), grad_embed


def solution(mesh):
    in_specs = (P(("row", "col"), None), P(("row", "col")), P())
    out_specs = (P(), P(("row", "col"), None))
    return jax.shard_map(body, mesh=mesh, in_specs=in_specs, out_specs=out_specs, check_vma=False)
```

time: 370 us -> 138 us (0.37)
  blocking collectives: 133 us -> 0 us
  waiting for transfers between devices: 175 us -> 52.1 us
  starting transfers between devices: 0.16 us -> 34.9 us
  matrix products: 25.8 us -> 0 us
  Pallas kernels: 0 us -> 24.2 us
  local copies, waits for them, and re-layouts: 1.96 us -> 19.1 us
  between operations: 16.3 us -> 3.18 us
  other arithmetic: 16.8 us -> 3.85 us
    reduce_scatter x2 -> x0, waiting for transfers between devices: 102 us -> none  [the longest x1 98.7 us: body(): lax.psum_scatter(jnp.einsum('ij,ik->jk', picked, block_a, preferred_eleme...]
    psum x2 -> x0, blocking collectives: 90.4 us -> none  [the longest x1 74.7 us: body(): lax.psum(jnp.sum(own_terms), ('row', 'col')) / total_views]
    all_gather x2 -> x0, waiting for transfers between devices: 72.5 us -> none  [the longest x1 38.1 us: body(): block_b = lax.all_gather(unit_b, 'row', axis=0, tiled=True)]
    ppermute x0 -> x22, starting transfers between devices: none -> 31.2 us  [body(): send = lambda v, pairs: lax.ppermute(v, AXES, pairs)]
    ppermute x0 -> x22, waiting for transfers between devices: none -> 27.1 us  [body(): send = lambda v, pairs: lax.ppermute(v, AXES, pairs)]
    dot_general x3 -> x0, matrix products: 25.8 us -> none  [the longest x1 10.7 us: body(): jnp.einsum('ik,jk->ij', block_a, block_b, preferred_element_type=jnp.floa...]
    all_to_all x0 -> x1, waiting for transfers between devices: none -> 25 us  [body(): lax.all_to_all(grads, AXES, 0, 0, tiled=True, axis_index_groups=GROUPS_A)]
    pallas_call x0 -> x5, Pallas kernels: none -> 24.2 us  [the longest x1 9.05 us: body(): pl.pallas_call(grad_kernel, out_shape=[shape((8, views, width), BF16), sh...]
  transfers between devices with their start and end apart: 4 -> 23, of which waited for: 4 -> 11; matrix products, arithmetic and copies ran while one was open for 3% -> 3% of each run, Pallas kernels for 0% -> 0%
where the time goes in v3:
time: 138 us; the launch traced here: 137 us
  waiting for transfers between devices  52.1 us (38%)
  starting transfers between devices  34.9 us (25%)
  Pallas kernels  24.2 us (18%)
  local copies, waits for them, and re-layouts  19.1 us (14%)
  other arithmetic  3.85 us (3%)
  between operations  3.18 us (2%)
    ppermute x22, starting transfers between devices, body(): send = lambda v, pairs: lax.ppermute(v, AXES, pairs)  31.2 us
    ppermute x22, waiting for transfers between devices, body(): send = lambda v, pairs: lax.ppermute(v, AXES, pairs)  27.1 us
    all_to_all x1, waiting for transfers between devices, body(): lax.all_to_all(grads, AXES, 0, 0, tiled=True, axis_index_groups=GROUPS_A)  25 us
    unnamed x28, local copies, waits for them, and re-layouts  16.6 us
    pallas_call x1, Pallas kernels, body(): pl.pallas_call(grad_kernel, out_shape=[shape((8, views, width), BF16), sh...  9.05 us
    pallas_call x1, Pallas kernels, body(): pl.pallas_call(score_kernel, out_shape=[pltpu.VMEM((n_a, n_b), F32), pltp...  8.93 us
    all_to_all x1, starting transfers between devices, body(): lax.all_to_all(grads, AXES, 0, 0, tiled=True, axis_index_groups=GROUPS_A)  3.61 us
    pallas_call x1, Pallas kernels, body(): pl.pallas_call(final_kernel, out_shape=shape((views, width), F32), in_spe...  2.94 us
  transfers between devices with their start and end apart: 23, of which 11 were waited for; matrix products, arithmetic and copies ran while one was open for 3% of the time, Pallas kernels for 0%

profile of v3, /device:TPU:1, one launch (start us, length us, event | category | flops | bytes accessed | tf_op | source)
XLA Modules:
  0.0 137.2 jit_solution(17037143232626532220)
XLA Ops:
  0.6 1.8 %shard_map.50 = bf16[144,1024]{1,0:T(8,128)(2,1)} custom-call(bf16[128,1024]{1,0:T(8,128)(2,1)} %x_ref.3, s32[1,128]{1,0:T(1,128)} %bitcast.40), custom_call_target="tpu_custom_call" | custom-call | tf_op jit(solution)/shard_map/pallas_call | solution.py:309
  5.6 2.6 %collective-permute-start.7 = (bf16[256,1024]{1,0:T(8,128)(2,1)S(1)}, bf16[256,1024]{1,0:T(8,128)(2,1)S(1)}, u32[]{:S(2)}, u32[]{:S(2)}) collective-permute-start(bf16[256,1024]{1,0:T(8,128)(2,1)S(1)} %pad_maximum_fusion.3), channel_id=1, source_target_pairs={{0,32},{8,104},{1,33},{9,105},{2,34},{10,106},{3,35},{11,107},{16,... | collective-permute-start | bytes 1572872 | tf_op jit(solution)/shard_map/ppermute | solution.py:305
  8.3 3.0 %collective-permute-start.8 = (bf16[256,1024]{1,0:T(8,128)(2,1)S(1)}, bf16[256,1024]{1,0:T(8,128)(2,1)S(1)}, u32[]{:S(2)}, u32[]{:S(2)}) collective-permute-start(bf16[256,1024]{1,0:T(8,128)(2,1)S(1)} %pad_maximum_fusion.3), channel_id=1, source_target_pairs={{0,52},{8,124},{1,53},{9,125},{2,54},{10,126},{3,55},{11,127},{16,... | collective-permute-start | bytes 1572872 | tf_op jit(solution)/shard_map/ppermute | solution.py:305
  11.3 3.8 %collective-permute-start.1 = (bf16[272,1024]{1,0:T(8,128)(2,1)S(1)}, bf16[272,1024]{1,0:T(8,128)(2,1)S(1)}, u32[]{:S(2)}, u32[]{:S(2)}) collective-permute-start(bf16[272,1024]{1,0:T(8,128)(2,1)S(1)} %pad_maximum_fusion.own), channel_id=1, source_target_pairs={{0,1},{8,11},{1,2},{9,8},{2,3},{10,9},{3,0},{11,10},{16,17},{24,27... | collective-permute-start | bytes 1671176 | tf_op jit(solution)/shard_map/ppermute | solution.py:305
  15.6 11.8 %collective-permute-done.8.d_b = bf16[256,1024]{1,0:T(8,128)(2,1)S(1)} collective-permute-done((bf16[256,1024]{1,0:T(8,128)(2,1)S(1)}, bf16[256,1024]{1,0:T(8,128)(2,1)S(1)}, u32[]{:S(2)}, u32[]{:S(2)}) %collective-permute-start.8) | collective-permute-done | bytes 524320 | tf_op jit(solution)/shard_map/ppermute | solution.py:305
  27.5 2.2 %collective-permute-start.11 = (bf16[256,1024]{1,0:T(8,128)(2,1)S(1)}, bf16[256,1024]{1,0:T(8,128)(2,1)}, u32[]{:S(2)}, u32[]{:S(2)}) collective-permute-start(bf16[256,1024]{1,0:T(8,128)(2,1)S(1)} %pad_maximum_fusion.4), channel_id=1, source_target_pairs={{0,32},{8,104},{1,33},{9,105},{2,34},{10,106},{3,35},{11,107},{16,... | collective-permute-start | bytes 1572872 | tf_op jit(solution)/shard_map/ppermute | solution.py:305
  32.0 3.8 %collective-permute-start.3 = (bf16[272,1024]{1,0:T(8,128)(2,1)}, bf16[272,1024]{1,0:T(8,128)(2,1)}, u32[]{:S(2)}, u32[]{:S(2)}) collective-permute-start(bf16[272,1024]{1,0:T(8,128)(2,1)} %pad_maximum_fusion.1), channel_id=1, source_target_pairs={{0,1},{8,11},{1,2},{9,8},{2,3},{10,9},{3,0},{11,10},{16,17},{24,27... | collective-permute-start | bytes 1671176 | tf_op jit(solution)/shard_map/ppermute | solution.py:305
  36.0 3.0 %collective-permute-start.9 = (bf16[256,1024]{1,0:T(8,128)(2,1)S(1)}, bf16[256,1024]{1,0:T(8,128)(2,1)}, u32[]{:S(2)}, u32[]{:S(2)}) collective-permute-start(bf16[256,1024]{1,0:T(8,128)(2,1)S(1)} %collective-permute-done.7.rx), channel_id=1, source_target_pairs={{0,8},{8,0},{1,9},{9,1},{2,10},{10,2},{3,11},{11,3},{16,24},{24,16... | collective-permute-start | bytes 1572872 | tf_op jit(solution)/shard_map/ppermute | solution.py:305
  43.6 8.9 %shard_map.51 = (f32[1024,2048]{1,0:T(8,128)S(1)}, bf16[2048,1024]{1,0:T(8,128)(2,1)S(1)}, f32[3,8,128]{2,1,0:T(8,128)}, s32[8,128]{1,0:T(8,128)}) custom-call(s32[28]{0:T(128)} %stack.133.place, f32[1]{0:T(128)S(6)} %copy.5.scale_ref, bf16[272,1024]{1,0:T(8,128)(2,1)S(1)} %pad_maximum_fusion.own, bf16[272,1024]{1,0:T(8,128)(2,1)S(1)} %collective-permute-done.1.rz, ...), custom_call_target="tpu_custom_call" | custom-call | tf_op jit(solution)/shard_map/pallas_call | solution.py:330
  52.5 3.3 %copy-done = f32[1024,2048]{1,0:T(8,128)} copy-done((f32[1024,2048]{1,0:T(8,128)}, f32[1024,2048]{1,0:T(8,128)S(1)}, u32[]{:S(2)}) %copy-start) | copy-done | bytes 8388632
  55.8 2.0 %copy-done.2 = bf16[2048,1024]{1,0:T(8,128)(2,1)} copy-done((bf16[2048,1024]{1,0:T(8,128)(2,1)}, bf16[2048,1024]{1,0:T(8,128)(2,1)S(1)}, u32[]{:S(2)}) %copy-start.2) | copy-done | bytes 4194328
  57.8 2.8 %collective-permute-done.13 = f32[3,8,128]{2,1,0:T(8,128)S(1)} collective-permute-done((f32[3,8,128]{2,1,0:T(8,128)}, f32[3,8,128]{2,1,0:T(8,128)S(1)}, u32[]{:S(2)}, u32[]{:S(2)}) %collective-permute-start.13) | collective-permute-done | bytes 12320 | tf_op jit(solution)/shard_map/ppermute | solution.py:305
  61.3 3.3 %collective-permute-start.14 = (f32[2,3,8,128]{3,2,1,0:T(8,128)S(1)}, f32[2,3,8,128]{3,2,1,0:T(8,128)S(1)}, u32[]{:S(2)}, u32[]{:S(2)}) collective-permute-start(f32[2,3,8,128]{3,2,1,0:T(8,128)S(1)} %pad_maximum_fusion.5.g0), channel_id=1, source_target_pairs={{0,3},{8,11},{1,0},{9,8},{2,1},{10,9},{3,2},{11,10},{16,19},{24,27... | collective-permute-start | bytes 73736 | tf_op jit(solution)/shard_map/ppermute | solution.py:305
  65.5 3.2 %collective-permute-done.15.g2 = f32[2,3,8,128]{3,2,1,0:T(8,128)S(1)} collective-permute-done((f32[2,3,8,128]{3,2,1,0:T(8,128)S(1)}, f32[2,3,8,128]{3,2,1,0:T(8,128)S(1)}, u32[]{:S(2)}, u32[]{:S(2)}) %collective-permute-start.15) | collective-permute-done | bytes 24608 | tf_op jit(solution)/shard_map/ppermute | solution.py:305
  71.4 2.7 %collective-permute-start.17 = (f32[2,128]{1,0:T(2,128)}, f32[2,128]{1,0:T(2,128)S(1)}, u32[]{:S(2)}, u32[]{:S(2)}) collective-permute-start(f32[2,128]{1,0:T(2,128)} %get-tuple-element.14), channel_id=1, source_target_pairs={{0,8},{8,0},{1,9},{9,1},{2,10},{10,2},{3,11},{11,3},{16,24},{24,16... | collective-permute-start | bytes 3080 | tf_op jit(solution)/shard_map/ppermute | solution.py:305
  75.7 3.6 %collective-permute-done.18 = f32[2,2,128]{2,1,0:T(2,128)S(1)} collective-permute-done((f32[2,2,128]{2,1,0:T(2,128)S(1)}, f32[2,2,128]{2,1,0:T(2,128)S(1)}, u32[]{:S(2)}, u32[]{:S(2)}) %collective-permute-start.18) | collective-permute-done | bytes 2080 | tf_op jit(solution)/shard_map/ppermute | solution.py:305
  80.0 1.7 %collective-permute-start.19 = (f32[4,2,128]{2,1,0:T(2,128)S(1)}, f32[4,2,128]{2,1,0:T(2,128)S(1)}, u32[]{:S(2)}, u32[]{:S(2)}) collective-permute-start(f32[4,2,128]{2,1,0:T(2,128)S(1)} %pad_maximum_fusion.6.h0), channel_id=1, source_target_pairs={{0,96},{8,104},{1,97},{9,105},{2,98},{10,106},{3,99},{11,107},{16,... | collective-permute-start | bytes 12296 | tf_op jit(solution)/shard_map/ppermute | solution.py:305
  83.7 1.9 %collective-permute-done.20.h2 = f32[4,2,128]{2,1,0:T(2,128)S(1)} collective-permute-done((f32[4,2,128]{2,1,0:T(2,128)S(1)}, f32[4,2,128]{2,1,0:T(2,128)S(1)}, u32[]{:S(2)}, u32[]{:S(2)}) %collective-permute-start.20) | collective-permute-done | bytes 4128 | tf_op jit(solution)/shard_map/ppermute | solution.py:305
  86.6 3.4 %copy-done.1 = f32[1024,2048]{1,0:T(8,128)S(1)} copy-done((f32[1024,2048]{1,0:T(8,128)S(1)}, f32[1024,2048]{1,0:T(8,128)}, u32[]{:S(2)}) %copy-start.1) | copy-done | bytes 8388632
  89.9 2.2 %copy-done.3 = bf16[2048,1024]{1,0:T(8,128)(2,1)S(1)} copy-done((bf16[2048,1024]{1,0:T(8,128)(2,1)S(1)}, bf16[2048,1024]{1,0:T(8,128)(2,1)}, u32[]{:S(2)}) %copy-start.3) | copy-done | bytes 4194328
  93.5 9.1 %shard_map.53 = (bf16[8,128,1024]{2,1,0:T(8,128)(2,1)}, f32[1,1]{1,0:T(1,128)}) custom-call(s32[28]{0:T(128)S(1)} %copy-done.6, f32[1024,2048]{1,0:T(8,128)S(1)} %copy-done.1, bf16[2048,1024]{1,0:T(8,128)(2,1)S(1)} %copy-done.3, f32[8,128]{1,0:T(8,128)S(1)} %copy-done.8, f32[4,2,128]{2,1,0:T(2,128)S(1)} %pad_maximum_fusion.6.h0, ...), custom_call_target="tpu_custom_call" | custom-call | tf_op jit(solution)/shard_map/pallas_call | solution.py:354
  102.5 3.6 %all-to-all-start = ((bf16[8,128,1024]{2,1,0:T(8,128)(2,1)}), bf16[8,128,1024]{2,1,0:T(8,128)(2,1)S(1)}, u32[]{:S(2)}, u32[]{:S(2)}) async-start(bf16[8,128,1024]{2,1,0:T(8,128)(2,1)} %get-tuple-element.17), calls=%async_computation | async-start | bytes 4194304 | tf_op jit(solution)/shard_map/all_to_all | solution.py:366
  106.8 25.0 %all-to-all-done.parts_ref = bf16[8,128,1024]{2,1,0:T(8,128)(2,1)S(1)} async-done(((bf16[8,128,1024]{2,1,0:T(8,128)(2,1)}), bf16[8,128,1024]{2,1,0:T(8,128)(2,1)S(1)}, u32[]{:S(2)}, u32[]{:S(2)}) %all-to-all-start) | async-done | bytes 2097184 | tf_op jit(solution)/shard_map/all_to_all | solution.py:366
  133.1 2.9 %shard_map.54 = f32[128,1024]{1,0:T(8,128)} custom-call(f32[1]{0:T(128)S(6)} %div.7.scale_ref, bf16[128,1024]{1,0:T(8,128)(2,1)} %x_ref.3, bf16[8,128,1024]{2,1,0:T(8,128)(2,1)} %copy-done.9), custom_call_target="tpu_custom_call" | custom-call | tf_op jit(solution)/shard_map/pallas_call | solution.py:368
  (74 shorter events, 22.4 us)
Async XLA Ops:
  2.4 3.1 %collective-permute-start = (bf16[144,1024]{1,0:T(8,128)(2,1)}, bf16[144,1024]{1,0:T(8,128)(2,1)S(1)}, u32[]{:S(2)}, u32[]{:S(2)}) collective-permute-start(bf16[144,1024]{1,0:T(8,128)(2,1)} %shard_map.50), channel_id=1, source_target_pairs={{0,8},{8,0},{1,9},{9,1},{2,10},{10,2},{3,11},{11,3},{16,24},{24,16... | collective-permute-start | bytes 884744 | tf_op jit(solution)/shard_map/ppermute | solution.py:305
  5.6 10.0 %collective-permute-start.7 = (bf16[256,1024]{1,0:T(8,128)(2,1)S(1)}, bf16[256,1024]{1,0:T(8,128)(2,1)S(1)}, u32[]{:S(2)}, u32[]{:S(2)}) collective-permute-start(bf16[256,1024]{1,0:T(8,128)(2,1)S(1)} %pad_maximum_fusion.3), channel_id=1, source_target_pairs={{0,32},{8,104},{1,33},{9,105},{2,34},{10,106},{3,35},{11,107},{16,... | collective-permute-start | bytes 1572872 | tf_op jit(solution)/shard_map/ppermute | solution.py:305
  8.3 19.2 %collective-permute-start.8 = (bf16[256,1024]{1,0:T(8,128)(2,1)S(1)}, bf16[256,1024]{1,0:T(8,128)(2,1)S(1)}, u32[]{:S(2)}, u32[]{:S(2)}) collective-permute-start(bf16[256,1024]{1,0:T(8,128)(2,1)S(1)} %pad_maximum_fusion.3), channel_id=1, source_target_pairs={{0,52},{8,124},{1,53},{9,125},{2,54},{10,126},{3,55},{11,127},{16,... | collective-permute-start | bytes 1572872 | tf_op jit(solution)/shard_map/ppermute | solution.py:305
  11.3 18.6 %collective-permute-start.1 = (bf16[272,1024]{1,0:T(8,128)(2,1)S(1)}, bf16[272,1024]{1,0:T(8,128)(2,1)S(1)}, u32[]{:S(2)}, u32[]{:S(2)}) collective-permute-start(bf16[272,1024]{1,0:T(8,128)(2,1)S(1)} %pad_maximum_fusion.own), channel_id=1, source_target_pairs={{0,1},{8,11},{1,2},{9,8},{2,3},{10,9},{3,0},{11,10},{16,17},{24,27... | collective-permute-start | bytes 1671176 | tf_op jit(solution)/shard_map/ppermute | solution.py:305
  15.1 15.1 %collective-permute-start.2 = (bf16[272,1024]{1,0:T(8,128)(2,1)S(1)}, bf16[272,1024]{1,0:T(8,128)(2,1)S(1)}, u32[]{:S(2)}, u32[]{:S(2)}) collective-permute-start(bf16[272,1024]{1,0:T(8,128)(2,1)S(1)} %pad_maximum_fusion.own), channel_id=1, source_target_pairs={{0,17},{8,27},{1,18},{9,24},{2,19},{10,25},{3,16},{11,26},{16,1},{... | collective-permute-start | bytes 1671176 | tf_op jit(solution)/shard_map/ppermute | solution.py:305
  15.1 20.6 %collective-permute-start.5 = (bf16[272,1024]{1,0:T(8,128)(2,1)S(1)}, bf16[272,1024]{1,0:T(8,128)(2,1)S(1)}, u32[]{:S(2)}, u32[]{:S(2)}) collective-permute-start(bf16[272,1024]{1,0:T(8,128)(2,1)S(1)} %pad_maximum_fusion.own), channel_id=1, source_target_pairs={{0,16},{8,28},{1,17},{9,29},{2,18},{10,30},{3,19},{11,31},{16,0},{... | collective-permute-start | bytes 1671176 | tf_op jit(solution)/shard_map/ppermute | solution.py:305
  27.5 8.5 %collective-permute-start.11 = (bf16[256,1024]{1,0:T(8,128)(2,1)S(1)}, bf16[256,1024]{1,0:T(8,128)(2,1)}, u32[]{:S(2)}, u32[]{:S(2)}) collective-permute-start(bf16[256,1024]{1,0:T(8,128)(2,1)S(1)} %pad_maximum_fusion.4), channel_id=1, source_target_pairs={{0,32},{8,104},{1,33},{9,105},{2,34},{10,106},{3,35},{11,107},{16,... | collective-permute-start | bytes 1572872 | tf_op jit(solution)/shard_map/ppermute | solution.py:305
  29.7 9.3 %collective-permute-start.10 = (bf16[256,1024]{1,0:T(8,128)(2,1)S(1)}, bf16[256,1024]{1,0:T(8,128)(2,1)S(1)}, u32[]{:S(2)}, u32[]{:S(2)}) collective-permute-start(bf16[256,1024]{1,0:T(8,128)(2,1)S(1)} %collective-permute-done.8.d_b), channel_id=1, source_target_pairs={{0,8},{8,0},{1,9},{9,1},{2,10},{10,2},{3,11},{11,3},{16,24},{24,16... | collective-permute-start | bytes 1572872 | tf_op jit(solution)/shard_map/ppermute | solution.py:305
  31.1 10.1 %collective-permute-start.4 = (bf16[272,1024]{1,0:T(8,128)(2,1)}, bf16[272,1024]{1,0:T(8,128)(2,1)}, u32[]{:S(2)}, u32[]{:S(2)}) collective-permute-start(bf16[272,1024]{1,0:T(8,128)(2,1)} %pad_maximum_fusion.2), channel_id=1, source_target_pairs={{0,8},{8,0},{1,9},{9,1},{2,10},{10,2},{3,11},{11,3},{16,24},{24,16... | collective-permute-start | bytes 1671176 | tf_op jit(solution)/shard_map/ppermute | solution.py:305
  32.0 10.6 %collective-permute-start.3 = (bf16[272,1024]{1,0:T(8,128)(2,1)}, bf16[272,1024]{1,0:T(8,128)(2,1)}, u32[]{:S(2)}, u32[]{:S(2)}) collective-permute-start(bf16[272,1024]{1,0:T(8,128)(2,1)} %pad_maximum_fusion.1), channel_id=1, source_target_pairs={{0,1},{8,11},{1,2},{9,8},{2,3},{10,9},{3,0},{11,10},{16,17},{24,27... | collective-permute-start | bytes 1671176 | tf_op jit(solution)/shard_map/ppermute | solution.py:305
  35.8 6.8 %collective-permute-start.6 = (bf16[272,1024]{1,0:T(8,128)(2,1)S(1)}, bf16[272,1024]{1,0:T(8,128)(2,1)}, u32[]{:S(2)}, u32[]{:S(2)}) collective-permute-start(bf16[272,1024]{1,0:T(8,128)(2,1)S(1)} %collective-permute-done.5.ry), channel_id=1, source_target_pairs={{0,8},{8,0},{1,9},{9,1},{2,10},{10,2},{3,11},{11,3},{16,24},{24,16... | collective-permute-start | bytes 1671176 | tf_op jit(solution)/shard_map/ppermute | solution.py:305
  36.0 5.1 %collective-permute-start.9 = (bf16[256,1024]{1,0:T(8,128)(2,1)S(1)}, bf16[256,1024]{1,0:T(8,128)(2,1)}, u32[]{:S(2)}, u32[]{:S(2)}) collective-permute-start(bf16[256,1024]{1,0:T(8,128)(2,1)S(1)} %collective-permute-done.7.rx), channel_id=1, source_target_pairs={{0,8},{8,0},{1,9},{9,1},{2,10},{10,2},{3,11},{11,3},{16,24},{24,16... | collective-permute-start | bytes 1572872 | tf_op jit(solution)/shard_map/ppermute | solution.py:305
  39.8 2.8 %collective-permute-start.12 = (bf16[256,1024]{1,0:T(8,128)(2,1)}, bf16[256,1024]{1,0:T(8,128)(2,1)}, u32[]{:S(2)}, u32[]{:S(2)}) collective-permute-start(bf16[256,1024]{1,0:T(8,128)(2,1)} %collective-permute-done.11.fx), channel_id=1, source_target_pairs={{0,8},{8,0},{1,9},{9,1},{2,10},{10,2},{3,11},{11,3},{16,24},{24,16... | collective-permute-start | bytes 1572872 | tf_op jit(solution)/shard_map/ppermute | solution.py:305
  43.6 42.9 %copy-start.6 = (s32[28]{0:T(128)S(1)}, s32[28]{0:T(128)}, u32[]{:S(2)}) copy-start(s32[28]{0:T(128)} %stack.133.place) | copy-start | bytes 340
  57.8 2.8 %collective-permute-start.13 = (f32[3,8,128]{2,1,0:T(8,128)}, f32[3,8,128]{2,1,0:T(8,128)S(1)}, u32[]{:S(2)}, u32[]{:S(2)}) collective-permute-start(f32[3,8,128]{2,1,0:T(8,128)} %get-tuple-element.12), channel_id=1, source_target_pairs={{0,16},{8,24},{1,17},{9,25},{2,18},{10,26},{3,19},{11,27},{16,0},{... | collective-permute-start | bytes 36872 | tf_op jit(solution)/shard_map/ppermute | solution.py:305
  61.3 4.2 %collective-permute-start.14 = (f32[2,3,8,128]{3,2,1,0:T(8,128)S(1)}, f32[2,3,8,128]{3,2,1,0:T(8,128)S(1)}, u32[]{:S(2)}, u32[]{:S(2)}) collective-permute-start(f32[2,3,8,128]{3,2,1,0:T(8,128)S(1)} %pad_maximum_fusion.5.g0), channel_id=1, source_target_pairs={{0,3},{8,11},{1,0},{9,8},{2,1},{10,9},{3,2},{11,10},{16,19},{24,27... | collective-permute-start | bytes 73736 | tf_op jit(solution)/shard_map/ppermute | solution.py:305
  64.5 4.2 %collective-permute-start.15 = (f32[2,3,8,128]{3,2,1,0:T(8,128)S(1)}, f32[2,3,8,128]{3,2,1,0:T(8,128)S(1)}, u32[]{:S(2)}, u32[]{:S(2)}) collective-permute-start(f32[2,3,8,128]{3,2,1,0:T(8,128)S(1)} %pad_maximum_fusion.5.g0), channel_id=1, source_target_pairs={{0,2},{8,10},{1,3},{9,11},{2,0},{10,8},{3,1},{11,9},{16,18},{24,26... | collective-permute-start | bytes 73736 | tf_op jit(solution)/shard_map/ppermute | solution.py:305
  64.6 4.2 %collective-permute-start.16 = (f32[2,3,8,128]{3,2,1,0:T(8,128)S(1)}, f32[2,3,8,128]{3,2,1,0:T(8,128)S(1)}, u32[]{:S(2)}, u32[]{:S(2)}) collective-permute-start(f32[2,3,8,128]{3,2,1,0:T(8,128)S(1)} %pad_maximum_fusion.5.g0), channel_id=1, source_target_pairs={{0,1},{8,9},{1,2},{9,10},{2,3},{10,11},{3,0},{11,8},{16,17},{24,25... | collective-permute-start | bytes 73736 | tf_op jit(solution)/shard_map/ppermute | solution.py:305
  71.4 3.6 %collective-permute-start.17 = (f32[2,128]{1,0:T(2,128)}, f32[2,128]{1,0:T(2,128)S(1)}, u32[]{:S(2)}, u32[]{:S(2)}) collective-permute-start(f32[2,128]{1,0:T(2,128)} %get-tuple-element.14), channel_id=1, source_target_pairs={{0,8},{8,0},{1,9},{9,1},{2,10},{10,2},{3,11},{11,3},{16,24},{24,16... | collective-permute-start | bytes 3080 | tf_op jit(solution)/shard_map/ppermute | solution.py:305
  75.7 3.6 %collective-permute-start.18 = (f32[2,2,128]{2,1,0:T(2,128)S(1)}, f32[2,2,128]{2,1,0:T(2,128)S(1)}, u32[]{:S(2)}, u32[]{:S(2)}) collective-permute-start(f32[2,2,128]{2,1,0:T(2,128)S(1)} %pad_maximum_fusion.7), channel_id=1, source_target_pairs={{0,20},{8,28},{1,21},{9,29},{2,22},{10,30},{3,23},{11,31},{16,4},{... | collective-permute-start | bytes 6152 | tf_op jit(solution)/shard_map/ppermute | solution.py:305
  80.0 3.8 %collective-permute-start.19 = (f32[4,2,128]{2,1,0:T(2,128)S(1)}, f32[4,2,128]{2,1,0:T(2,128)S(1)}, u32[]{:S(2)}, u32[]{:S(2)}) collective-permute-start(f32[4,2,128]{2,1,0:T(2,128)S(1)} %pad_maximum_fusion.6.h0), channel_id=1, source_target_pairs={{0,96},{8,104},{1,97},{9,105},{2,98},{10,106},{3,99},{11,107},{16,... | collective-permute-start | bytes 12296 | tf_op jit(solution)/shard_map/ppermute | solution.py:305
  81.7 4.0 %collective-permute-start.20 = (f32[4,2,128]{2,1,0:T(2,128)S(1)}, f32[4,2,128]{2,1,0:T(2,128)S(1)}, u32[]{:S(2)}, u32[]{:S(2)}) collective-permute-start(f32[4,2,128]{2,1,0:T(2,128)S(1)} %pad_maximum_fusion.6.h0), channel_id=1, source_target_pairs={{0,64},{8,72},{1,65},{9,73},{2,66},{10,74},{3,67},{11,75},{16,80},... | collective-permute-start | bytes 12296 | tf_op jit(solution)/shard_map/ppermute | solution.py:305
  82.9 3.7 %collective-permute-start.21 = (f32[4,2,128]{2,1,0:T(2,128)S(1)}, f32[4,2,128]{2,1,0:T(2,128)S(1)}, u32[]{:S(2)}, u32[]{:S(2)}) collective-permute-start(f32[4,2,128]{2,1,0:T(2,128)S(1)} %pad_maximum_fusion.6.h0), channel_id=1, source_target_pairs={{0,32},{8,40},{1,33},{9,41},{2,34},{10,42},{3,35},{11,43},{16,48},... | collective-permute-start | bytes 12296 | tf_op jit(solution)/shard_map/ppermute | solution.py:305
  102.5 29.3 %all-to-all-start = ((bf16[8,128,1024]{2,1,0:T(8,128)(2,1)}), bf16[8,128,1024]{2,1,0:T(8,128)(2,1)S(1)}, u32[]{:S(2)}, u32[]{:S(2)}) async-start(bf16[8,128,1024]{2,1,0:T(8,128)(2,1)} %get-tuple-element.17), calls=%async_computation | async-start | bytes 4194304 | tf_op jit(solution)/shard_map/all_to_all | solution.py:366
  (13 other events, 27.3 us)

commit v4 on v3

--- a/solution.py
+++ b/solution.py
@@ -54,9 +54,17 @@
 FROM_Z = [to(lambda x, y, z, k, g, d=d: (x, y, z - d, k)) for d in (1, 2, 3)]
 FROM_X = [to(lambda x, y, z, k, g, d=d: (x - d, y, z, k)) for d in (1, 2, 3)]
 
-GROUPS_A = [
-    [device_id(x, y, z, k) for y in (p, p + 1) for z in range(4)] for x in range(4) for p in (0, 2) for k in range(2)
+OWNERS = [
+    None,
+    PARTNER_A,
+    to(lambda x, y, z, k, g: (x, y, z - g, k)),
+    ALONG_Z,
+    to(lambda x, y, z, k, g: (x, y, z + 2, k)),
+    ALONG_YZ,
+    to(lambda x, y, z, k, g: (x, mate_a(y), z + 2, k)),
+    to(lambda x, y, z, k, g: (x, mate_a(y), z - g, k)),
 ]
+
 COLUMNS = [
     (0, 0, 0), (0, 0, 1), (-1, 0, 0), (-1, 0, 1), (-1, 1, 0), (-1, 1, 1), (1, 0, 1), (1, 0, 0),
     (1, 1, 1), (1, 1, 0), (2, 0, 0), (2, 1, 0), (2, 0, 1), (2, 1, 1), (0, 1, 0), (0, 1, 1),
@@ -96,29 +104,31 @@
         ref[at * n : at * n + rows, :] = src[start : start + rows, :]
 
     put(a_ref, 0, own, 0)
-    put(a_ref, 1, rz, 0)
-    put(a_ref, 2, d_a, 0)
-    put(a_ref, 3, fz, 0, e)
-    put(a_ref, 5, s_z, 0, e)
+    put(a_ref, 2, rz, 0)
+    put(a_ref, 3, s_z, 0)
+    put(a_ref, 4, fz, 0)
+    put(a_ref, 5, s_z, n)
+    put(a_ref, 6, fz, n)
+    put(a_ref, 7, d_a, 0)
     for src, at in ((own, 0), (rx, 2), (d_b, 4), (s_rx, 6), (s_db, 8), (fx, 10), (s_fx, 12)):
         put(b_ref, at, src, 0, e)
 
     @pl.when(core == 0)
     def _():
-        put(a_ref, 7, ry, 0)
+        put(a_ref, 1, ry, 0)
         put(b_ref, 14, s_ry, n)
         put(b_ref, 15, s_ry, 0)
 
     @pl.when(core == 1)
     def _():
-        put(a_ref, 7, s_ry, n)
+        put(a_ref, 1, s_ry, n)
         put(b_ref, 14, ry, 0, e)
 
     tail = lambda src: src[e : e + 2 * EXTRA, 0 : 2 * n].astype(F32)
     tails = [tail(src) for src in (own, rz, d_a, fz, s_z, ry, s_ry)]
-    head = [(0, 0), (1, 0), (2, 0), (3, 0), (3, EXTRA), (4, 0), (4, EXTRA)]
+    head = [(0, 0), (1, 0), (4, 0), (3, 0), (4, EXTRA), (3, EXTRA), (2, 0)]
     rows = [tails[p][r : r + 1] for p, r in head]
-    rows.append(jnp.where(core == 0, tails[5][0:1], tails[6][EXTRA : EXTRA + 1]))
+    rows.insert(1, jnp.where(core == 0, tails[5][0:1], tails[6][EXTRA : EXTRA + 1]))
     rows = jnp.concatenate(rows, axis=0).astype(I32)
     shard, lane = rows[:, 0:n], rows[:, n:]
     mate_x, mate_k, mate_z = shard >> 5, (shard >> 3) & 1, shard & 3
@@ -199,23 +209,23 @@
     out_ref[1:2, :] = jnp.sum(lse - pos, axis=0, keepdims=True)
 
 
-def grad_kernel(
-    place, s_ref, b_ref, lse_ref, h0, h1, h2, h3, mates_ref, out, loss_ref, d_ref, o_ref, sems
-):
+def grad_kernel(which, place, s_ref, b_ref, lse_ref, h0, h1, h2, h3, mates_ref, *refs):
     n = LANES
     per = BLOCK // n
-    n_a, n_b = s_ref.shape
-    core, y, x = place[0], place[1], place[27]
-    total = jnp.zeros((1, n), F32)
-    for i in range(16):
-        step = (i // 4 - x) & 3
-        at = jnp.where((y >> 1) == i // 2 % 2, 0, 2) + jnp.where(core == i % 2, 0, 1)
-        part = h0[at, 1:2, :]
-        for d, h in ((1, h1), (2, h2), (3, h3)):
-            part = jnp.where(step == d, h[at, 1:2, :], part)
-        total = total + part
-    loss_ref[...] = jnp.sum(total, axis=1, keepdims=True)
-    copies = []
+    n_b = s_ref.shape[1]
+    outs, d_ref = refs[:per], refs[-1]
+    if which == 0:
+        core, y, x = place[0], place[1], place[27]
+        total = jnp.zeros((1, n), F32)
+        for i in range(16):
+            step = (i // 4 - x) & 3
+            at = jnp.where((y >> 1) == i // 2 % 2, 0, 2) + jnp.where(core == i % 2, 0, 1)
+            part = h0[at, 1:2, :]
+            for d, h in ((1, h1), (2, h2), (3, h3)):
+                part = jnp.where(step == d, h[at, 1:2, :], part)
+            total = total + part
+        refs[per][...] = jnp.sum(total, axis=1, keepdims=True)
+    core = place[0]
     lane = lax.broadcasted_iota(I32, (n, n), 1)
 
     forward = jnp.where(core == 0, 1, 0)
@@ -232,44 +242,29 @@
 
     others = [other_lse(t) for t in range(n_b // n)]
 
-    def coefs_of(step):
-        for i in range(per):
-            shard = step * per + i
-            rows = slice(shard * n, (shard + 1) * n)
-            mates = to_column(mates_ref[shard : shard + 1, :])
-            mine = to_column(lse_ref[pl.ds(place[3 + shard], 1), :])
-            for t in range(n_b // n):
-                cols = slice(t * n, (t + 1) * n)
-                s = s_ref[rows, cols]
-                mate = jnp.where(lane == mates - t * n, 1.0, 0.0)
-                d = (jnp.exp(s - mine) - mate) + (jnp.exp(s - others[t]) - mate)
-                d_ref[rows, cols] = d.astype(BF16)
-
-    def grads_of(step):
-        rows = slice(step * BLOCK, (step + 1) * BLOCK)
-        o_ref[rows, :] = jnp.dot(d_ref[rows, :], b_ref[...], preferred_element_type=F32).astype(BF16)
-        for i in range(per):
-            shard = step * per + i
-            copies.append(pltpu.make_async_copy(o_ref.at[pl.ds(shard * n, n)], out.at[place[3 + shard]], sems.at[shard]))
-            copies[-1].start()
-
-    steps = n_a // BLOCK
-    coefs_of(0)
-    for step in range(steps):
-        if step + 1 < steps:
-            coefs_of(step + 1)
-        grads_of(step)
-    for copy in copies:
-        copy.wait()
-
-
-def final_kernel(scale_ref, x_ref, parts_ref, out_ref):
+    for i in range(per):
+        shard = which * per + i
+        mates = to_column(mates_ref[shard : shard + 1, :])
+        mine = to_column(lse_ref[pl.ds(place[3 + shard], 1), :])
+        for t in range(n_b // n):
+            cols = slice(t * n, (t + 1) * n)
+            s = s_ref[shard * n : (shard + 1) * n, cols]
+            mate = jnp.where(lane == mates - t * n, 1.0, 0.0)
+            d = (jnp.exp(s - mine) - mate) + (jnp.exp(s - others[t]) - mate)
+            d_ref[i * n : (i + 1) * n, cols] = d.astype(BF16)
+    out = jnp.dot(d_ref[...], b_ref[...], preferred_element_type=F32).astype(BF16)
+    for i in range(per):
+        outs[i][...] = out[i * n : (i + 1) * n]
+
+
+def final_kernel(scale_ref, x_ref, *refs):
+    parts, out_ref = refs[:-1], refs[-1]
     flat = x_ref[...].astype(F32)
     inv = lax.rsqrt(jnp.sum(flat * flat, axis=1, keepdims=True) + 1e-06)
     unit = flat * inv
-    dunit = parts_ref[0].astype(F32)
-    for i in range(1, parts_ref.shape[0]):
-        dunit = dunit + parts_ref[i].astype(F32)
+    dunit = parts[0][...].astype(F32)
+    for part in parts[1:]:
+        dunit = dunit + part[...].astype(F32)
     dunit = dunit * scale_ref[0]
     out_ref[...] = inv * (dunit - unit * jnp.sum(unit * dunit, axis=1, keepdims=True))
 
@@ -288,8 +283,8 @@
     slot_a = lambda yy, zz: (yy & 1) * 4 + (zz & 3)
     slot_b = lambda xx, yy, same: (1 - (yy & 1)) * 4 + (xx & 3) + (0 if same else 8)
     slots_a = [
-        slot_a(y, z), slot_a(y, z - sign), slot_a(y ^ 1, z - sign), slot_a(y, z + 2),
-        slot_a(y ^ 1, z + 2), slot_a(y, z + sign), slot_a(y ^ 1, z + sign), slot_a(y ^ 1, z),
+        slot_a(y, z), slot_a(y ^ 1, z), slot_a(y, z - sign), slot_a(y, z + sign),
+        slot_a(y, z + 2), slot_a(y ^ 1, z + sign), slot_a(y ^ 1, z + 2), slot_a(y ^ 1, z - sign),
     ]
     slots_b = [
         slot_b(x, y, True), slot_b(x, y, False),
@@ -305,17 +300,17 @@
     send = lambda v, pairs: lax.ppermute(v, AXES, pairs)
     n = LANES
     params = pltpu.CompilerParams(vmem_limit_bytes=VMEM_LIMIT)
+    small = pltpu.CompilerParams(vmem_limit_bytes=8 << 20)
 
     mine = pl.pallas_call(
-        unit_kernel, out_shape=shape((views + 2 * EXTRA, width), BF16), in_specs=[VMEM, VMEM], out_specs=VMEM
+        unit_kernel, out_shape=shape((views + 2 * EXTRA, width), BF16), in_specs=[VMEM, VMEM], out_specs=VMEM, compiler_params=small
     )(embeddings, partner.reshape(1, views))
     twin = send(mine, SWAP)
     own = jnp.concatenate([mine[:n], twin[:n], mine[n : n + EXTRA], twin[n : n + EXTRA]], axis=0)
-    both = own[: 2 * n]
     d_a = send(own, ALONG_YZ)
-    d_b = send(both, ALONG_XY)
+    d_b = send(own, ALONG_XY)
     rz = send(own, ALONG_Z)
-    rx = send(both, ALONG_X)
+    rx = send(own, ALONG_X)
     ry = send(own, ALONG_Y)
     e = 2 * n
     fz = send(jnp.concatenate([rz[:n], d_a[:n], rz[e : e + EXTRA], d_a[e : e + EXTRA]], axis=0), ALONG_Z)
@@ -347,30 +342,39 @@
         out_shape=[shape((8, views), F32), shape((2, views), F32)],
         in_specs=[SMEM] + [VMEM] * 4,
         out_specs=[VMEM, VMEM],
+        compiler_params=small,
     )(place, pair, g1, g2, g3)
     twins = jnp.stack([spread, send(spread, SWAP)])
     four = jnp.concatenate([twins, send(twins, PARTNER_B)], axis=0)
     h1, h2, h3 = (send(four, pairs) for pairs in FROM_X)
-    grads, loss = pl.pallas_call(
-        grad_kernel,
-        out_shape=[shape((8, views, width), BF16), shape((1, 1), F32)],
-        in_specs=[SMEM] + [VMEM] * 8,
-        out_specs=[ANY, VMEM],
-        scratch_shapes=[
-            pltpu.VMEM((n_a, n_b), BF16),
-            pltpu.VMEM((n_a, width), BF16),
-            pltpu.SemaphoreType.DMA((8,)),
-        ],
-        compiler_params=params,
-    )(place, fast(scores), fast(block_b), lse, four, h1, h2, h3, mates)
-    parts = lax.all_to_all(grads, AXES, 0, 0, tiled=True, axis_index_groups=GROUPS_A)
+    scores, block_b = fast(scores), fast(block_b)
+    parts = [None] * 8
+    for step in reversed(range(4)):
+        outs = [shape((views, width), BF16)] * 2 + ([shape((1, 1), F32)] if step == 0 else [])
+        got = pl.pallas_call(
+            functools.partial(grad_kernel, step),
+            out_shape=outs,
+            in_specs=[SMEM] + [VMEM] * 8,
+            out_specs=[VMEM] * len(outs),
+            scratch_shapes=[pltpu.VMEM((BLOCK, n_b), BF16)],
+            compiler_params=pltpu.CompilerParams(vmem_limit_bytes=16 << 20),
+            cost_estimate=pl.CostEstimate(flops=4 * BLOCK * n_b * width, bytes_accessed=1 << 20, transcendentals=0),
+        )(place, scores, block_b, lse, four, h1, h2, h3, mates)
+        for i in (1, 0):
+            shard = 2 * step + i
+            parts[shard] = send(got[i], OWNERS[shard]) if shard else got[i]
+    loss = got[2]
     total = views * 128
+    rows = views // 4
+    block = pl.BlockSpec((rows, width), lambda i: (i, 0))
     grad_embed = pl.pallas_call(
         final_kernel,
+        grid=(views // rows,),
         out_shape=shape((views, width), F32),
-        in_specs=[SMEM, VMEM, VMEM],
-        out_specs=VMEM,
-    )(inv_temp / total, embeddings, parts)
+        in_specs=[SMEM] + [block] * 9,
+        out_specs=block,
+        compiler_params=small,
+    )(inv_temp / total, embeddings, *parts)
     return (loss / total).reshape(1), grad_embed
 
 

time: 138 us -> 113 us (0.82)
  local copies, waits for them, and re-layouts: 19.1 us -> 4.99 us
  waiting for transfers between devices: 52.1 us -> 39.2 us
  starting transfers between devices: 34.9 us -> 41.6 us
  other arithmetic: 3.85 us -> 1.67 us
  Pallas kernels: 24.2 us -> 22.1 us
    all_to_all x1 -> x0, waiting for transfers between devices: 25 us -> none  [body(): lax.all_to_all(grads, AXES, 0, 0, tiled=True, axis_index_groups=GROUPS_A)]
    unnamed x28 -> x14, local copies, waits for them, and re-layouts: 16.6 us -> 4.13 us
    ppermute x22 -> x29, waiting for transfers between devices: 27.1 us -> 39.2 us  [body(): send = lambda v, pairs: lax.ppermute(v, AXES, pairs)]
    ppermute x22 -> x29, starting transfers between devices: 31.2 us -> 41.6 us  [body(): send = lambda v, pairs: lax.ppermute(v, AXES, pairs)]
    all_to_all x1 -> x0, starting transfers between devices: 3.61 us -> none  [body(): lax.all_to_all(grads, AXES, 0, 0, tiled=True, axis_index_groups=GROUPS_A)]
    pallas_call x1, Pallas kernels: 1.81 us -> 0.14 us  [body(): pl.pallas_call(unit_kernel, out_shape=shape((views + 2 * EXTRA, width), B...]
    pallas_call x2 -> x5, Pallas kernels: 12 us -> 12.4 us  [the longest x4 10.5 us: body(): pl.pallas_call(functools.partial(grad_kernel, step), out_shape=outs, in_s...]
  transfers between devices with their start and end apart: 23 -> 29, of which waited for: 11 -> 14; matrix products, arithmetic and copies ran while one was open for 3% -> 2% of each run, Pallas kernels for 0% -> 7%
where the time goes in v4:
time: 113 us
  starting transfers between devices  41.6 us (37%)
  waiting for transfers between devices  39.2 us (35%)
  Pallas kernels  22.1 us (20%)
  local copies, waits for them, and re-layouts  4.99 us (4%)
  between operations  3.24 us (3%)
  other arithmetic  1.67 us (1%)
    ppermute x29, starting transfers between devices, body(): send = lambda v, pairs: lax.ppermute(v, AXES, pairs)  41.6 us
    ppermute x29, waiting for transfers between devices, body(): send = lambda v, pairs: lax.ppermute(v, AXES, pairs)  39.2 us
    pallas_call x4, Pallas kernels, body(): pl.pallas_call(functools.partial(grad_kernel, step), out_shape=outs, in_s...  10.5 us
    pallas_call x1, Pallas kernels, body(): pl.pallas_call(score_kernel, out_shape=[pltpu.VMEM((n_a, n_b), F32), pltp...  8.94 us
    unnamed x14, local copies, waits for them, and re-layouts  4.13 us
  transfers between devices with their start and end apart: 29, of which 14 were waited for; matrix products, arithmetic and copies ran while one was open for 2% of the time, Pallas kernels for 7%

profile of v4, /device:TPU:1, one launch (start us, length us, event | category | flops | bytes accessed | tf_op | source)
XLA Modules:
  0.0 112.8 jit_solution(13564500938582032283)
XLA Ops:
  5.2 2.6 %collective-permute-start.7 = (bf16[272,1024]{1,0:T(8,128)(2,1)S(1)}, bf16[272,1024]{1,0:T(8,128)(2,1)S(1)}, u32[]{:S(2)}, u32[]{:S(2)}) collective-permute-start(bf16[272,1024]{1,0:T(8,128)(2,1)S(1)} %pad_maximum_fusion.own), channel_id=1, source_target_pairs={{0,32},{8,104},{1,33},{9,105},{2,34},{10,106},{3,35},{11,107},{16,... | collective-permute-start | bytes 1671176 | tf_op jit(solution)/shard_map/ppermute | solution.py:300
  7.8 3.0 %collective-permute-start.8 = (bf16[272,1024]{1,0:T(8,128)(2,1)S(1)}, bf16[272,1024]{1,0:T(8,128)(2,1)S(1)}, u32[]{:S(2)}, u32[]{:S(2)}) collective-permute-start(bf16[272,1024]{1,0:T(8,128)(2,1)S(1)} %pad_maximum_fusion.own), channel_id=1, source_target_pairs={{0,52},{8,124},{1,53},{9,125},{2,54},{10,126},{3,55},{11,127},{16,... | collective-permute-start | bytes 1671176 | tf_op jit(solution)/shard_map/ppermute | solution.py:300
  10.8 3.8 %collective-permute-start.1 = (bf16[272,1024]{1,0:T(8,128)(2,1)S(1)}, bf16[272,1024]{1,0:T(8,128)(2,1)S(1)}, u32[]{:S(2)}, u32[]{:S(2)}) collective-permute-start(bf16[272,1024]{1,0:T(8,128)(2,1)S(1)} %pad_maximum_fusion.own), channel_id=1, source_target_pairs={{0,1},{8,11},{1,2},{9,8},{2,3},{10,9},{3,0},{11,10},{16,17},{24,27... | collective-permute-start | bytes 1671176 | tf_op jit(solution)/shard_map/ppermute | solution.py:300
  15.1 12.8 %collective-permute-done.8.d_b = bf16[272,1024]{1,0:T(8,128)(2,1)S(1)} collective-permute-done((bf16[272,1024]{1,0:T(8,128)(2,1)S(1)}, bf16[272,1024]{1,0:T(8,128)(2,1)S(1)}, u32[]{:S(2)}, u32[]{:S(2)}) %collective-permute-start.8) | collective-permute-done | bytes 557088 | tf_op jit(solution)/shard_map/ppermute | solution.py:300
  27.9 2.3 %collective-permute-start.11 = (bf16[256,1024]{1,0:T(8,128)(2,1)S(1)}, bf16[256,1024]{1,0:T(8,128)(2,1)}, u32[]{:S(2)}, u32[]{:S(2)}) collective-permute-start(bf16[256,1024]{1,0:T(8,128)(2,1)S(1)} %pad_maximum_fusion.3), channel_id=1, source_target_pairs={{0,32},{8,104},{1,33},{9,105},{2,34},{10,106},{3,35},{11,107},{16,... | collective-permute-start | bytes 1572872 | tf_op jit(solution)/shard_map/ppermute | solution.py:300
  31.6 3.8 %collective-permute-start.3 = (bf16[272,1024]{1,0:T(8,128)(2,1)}, bf16[272,1024]{1,0:T(8,128)(2,1)}, u32[]{:S(2)}, u32[]{:S(2)}) collective-permute-start(bf16[272,1024]{1,0:T(8,128)(2,1)} %pad_maximum_fusion.1), channel_id=1, source_target_pairs={{0,1},{8,11},{1,2},{9,8},{2,3},{10,9},{3,0},{11,10},{16,17},{24,27... | collective-permute-start | bytes 1671176 | tf_op jit(solution)/shard_map/ppermute | solution.py:300
  36.4 3.5 %collective-permute-start.6 = (bf16[272,1024]{1,0:T(8,128)(2,1)S(1)}, bf16[272,1024]{1,0:T(8,128)(2,1)}, u32[]{:S(2)}, u32[]{:S(2)}) collective-permute-start(bf16[272,1024]{1,0:T(8,128)(2,1)S(1)} %collective-permute-done.5.ry), channel_id=1, source_target_pairs={{0,8},{8,0},{1,9},{9,1},{2,10},{10,2},{3,11},{11,3},{16,24},{24,16... | collective-permute-start | bytes 1671176 | tf_op jit(solution)/shard_map/ppermute | solution.py:300
  44.0 8.9 %shard_map.51 = (f32[1024,2048]{1,0:T(8,128)S(1)}, bf16[2048,1024]{1,0:T(8,128)(2,1)S(1)}, f32[3,8,128]{2,1,0:T(8,128)}, s32[8,128]{1,0:T(8,128)}) custom-call(s32[28]{0:T(128)} %stack.133.place, f32[1]{0:T(128)S(6)} %copy.5.scale_ref, bf16[272,1024]{1,0:T(8,128)(2,1)S(1)} %pad_maximum_fusion.own, bf16[272,1024]{1,0:T(8,128)(2,1)S(1)} %collective-permute-done.1.rz, ...), custom_call_target="tpu_custom_call" | custom-call | tf_op jit(solution)/shard_map/pallas_call | solution.py:325
  52.9 2.8 %collective-permute-done.13 = f32[3,8,128]{2,1,0:T(8,128)S(1)} collective-permute-done((f32[3,8,128]{2,1,0:T(8,128)}, f32[3,8,128]{2,1,0:T(8,128)S(1)}, u32[]{:S(2)}, u32[]{:S(2)}) %collective-permute-start.13) | collective-permute-done | bytes 12320 | tf_op jit(solution)/shard_map/ppermute | solution.py:300
  56.4 3.8 %collective-permute-start.14 = (f32[2,3,8,128]{3,2,1,0:T(8,128)S(1)}, f32[2,3,8,128]{3,2,1,0:T(8,128)S(1)}, u32[]{:S(2)}, u32[]{:S(2)}) collective-permute-start(f32[2,3,8,128]{3,2,1,0:T(8,128)S(1)} %pad_maximum_fusion.4.g0), channel_id=1, source_target_pairs={{0,3},{8,11},{1,0},{9,8},{2,1},{10,9},{3,2},{11,10},{16,19},{24,27... | collective-permute-start | bytes 73736 | tf_op jit(solution)/shard_map/ppermute | solution.py:300
  61.1 3.2 %collective-permute-done.15.g2 = f32[2,3,8,128]{3,2,1,0:T(8,128)S(1)} collective-permute-done((f32[2,3,8,128]{3,2,1,0:T(8,128)S(1)}, f32[2,3,8,128]{3,2,1,0:T(8,128)S(1)}, u32[]{:S(2)}, u32[]{:S(2)}) %collective-permute-start.15) | collective-permute-done | bytes 24608 | tf_op jit(solution)/shard_map/ppermute | solution.py:300
  65.0 2.8 %collective-permute-start.17 = (f32[2,128]{1,0:T(2,128)S(1)}, f32[2,128]{1,0:T(2,128)S(1)}, u32[]{:S(2)}, u32[]{:S(2)}) collective-permute-start(f32[2,128]{1,0:T(2,128)S(1)} %get-tuple-element.21), channel_id=1, source_target_pairs={{0,8},{8,0},{1,9},{9,1},{2,10},{10,2},{3,11},{11,3},{16,24},{24,16... | collective-permute-start | bytes 3080 | tf_op jit(solution)/shard_map/ppermute | solution.py:300
  68.6 3.6 %collective-permute-done.18 = f32[2,2,128]{2,1,0:T(2,128)S(1)} collective-permute-done((f32[2,2,128]{2,1,0:T(2,128)S(1)}, f32[2,2,128]{2,1,0:T(2,128)S(1)}, u32[]{:S(2)}, u32[]{:S(2)}) %collective-permute-start.18) | collective-permute-done | bytes 2080 | tf_op jit(solution)/shard_map/ppermute | solution.py:300
  72.2 1.7 %collective-permute-start.19 = (f32[4,2,128]{2,1,0:T(2,128)S(1)}, f32[4,2,128]{2,1,0:T(2,128)S(1)}, u32[]{:S(2)}, u32[]{:S(2)}) collective-permute-start(f32[4,2,128]{2,1,0:T(2,128)S(1)} %pad_maximum_fusion.5.h0), channel_id=1, source_target_pairs={{0,96},{8,104},{1,97},{9,105},{2,98},{10,106},{3,99},{11,107},{16,... | collective-permute-start | bytes 12296 | tf_op jit(solution)/shard_map/ppermute | solution.py:300
  74.8 3.2 %collective-permute-done.20.h2 = f32[4,2,128]{2,1,0:T(2,128)S(1)} collective-permute-done((f32[4,2,128]{2,1,0:T(2,128)S(1)}, f32[4,2,128]{2,1,0:T(2,128)S(1)}, u32[]{:S(2)}, u32[]{:S(2)}) %collective-permute-start.20) | collective-permute-done | bytes 4128 | tf_op jit(solution)/shard_map/ppermute | solution.py:300
  78.6 2.5 %shard_map.56 = (bf16[128,1024]{1,0:T(8,128)(2,1)S(1)}, bf16[128,1024]{1,0:T(8,128)(2,1)S(1)}) custom-call(s32[28]{0:T(128)S(1)} %copy-done.5, f32[1024,2048]{1,0:T(8,128)S(1)} %get-tuple-element.17.s_ref, bf16[2048,1024]{1,0:T(8,128)(2,1)S(1)} %get-tuple-element.18.b_ref, f32[8,128]{1,0:T(8,128)S(1)} %get-tuple-element.20.lse_ref, ...), custom_call_target="tpu_custom_call" | custom-call | flops 2147483648 | bytes 1048576 | tf_op jit(solution)/shard_map/pallas_call | solution.py:354
  81.3 2.0 %collective-permute-start.28 = (bf16[128,1024]{1,0:T(8,128)(2,1)S(1)}, bf16[128,1024]{1,0:T(8,128)(2,1)S(1)}, u32[]{:S(2)}, u32[]{:S(2)}) collective-permute-start(bf16[128,1024]{1,0:T(8,128)(2,1)S(1)} %get-tuple-element.31), channel_id=1, source_target_pairs={{0,19},{8,25},{1,16},{9,26},{2,17},{10,27},{3,18},{11,24},{16,3},{... | collective-permute-start | bytes 786440 | tf_op jit(solution)/shard_map/ppermute | solution.py:300
  83.3 2.5 %shard_map.55 = (bf16[128,1024]{1,0:T(8,128)(2,1)S(1)}, bf16[128,1024]{1,0:T(8,128)(2,1)S(1)}) custom-call(s32[28]{0:T(128)S(1)} %copy-done.5, f32[1024,2048]{1,0:T(8,128)S(1)} %get-tuple-element.17.s_ref, bf16[2048,1024]{1,0:T(8,128)(2,1)S(1)} %get-tuple-element.18.b_ref, f32[8,128]{1,0:T(8,128)S(1)} %get-tuple-element.20.lse_ref, ...), custom_call_target="tpu_custom_call" | custom-call | flops 2147483648 | bytes 1048576 | tf_op jit(solution)/shard_map/pallas_call | solution.py:354
  85.8 2.0 %collective-permute-start.25 = (bf16[128,1024]{1,0:T(8,128)(2,1)S(1)}, bf16[128,1024]{1,0:T(8,128)(2,1)S(1)}, u32[]{:S(2)}, u32[]{:S(2)}) collective-permute-start(bf16[128,1024]{1,0:T(8,128)(2,1)S(1)} %get-tuple-element.28), channel_id=1, source_target_pairs={{0,2},{8,10},{1,3},{9,11},{2,0},{10,8},{3,1},{11,9},{16,18},{24,26... | collective-permute-start | bytes 786440 | tf_op jit(solution)/shard_map/ppermute | solution.py:300
  88.6 2.5 %shard_map.54 = (bf16[128,1024]{1,0:T(8,128)(2,1)S(1)}, bf16[128,1024]{1,0:T(8,128)(2,1)S(1)}) custom-call(s32[28]{0:T(128)S(1)} %copy-done.5, f32[1024,2048]{1,0:T(8,128)S(1)} %get-tuple-element.17.s_ref, bf16[2048,1024]{1,0:T(8,128)(2,1)S(1)} %get-tuple-element.18.b_ref, f32[8,128]{1,0:T(8,128)S(1)} %get-tuple-element.20.lse_ref, ...), custom_call_target="tpu_custom_call" | custom-call | flops 2147483648 | bytes 1048576 | tf_op jit(solution)/shard_map/pallas_call | solution.py:354
  92.3 3.0 %shard_map.53 = (bf16[128,1024]{1,0:T(8,128)(2,1)S(1)}, bf16[128,1024]{1,0:T(8,128)(2,1)S(1)}, f32[1,1]{1,0:T(1,128)}) custom-call(s32[28]{0:T(128)S(1)} %copy-done.5, f32[1024,2048]{1,0:T(8,128)S(1)} %get-tuple-element.17.s_ref, bf16[2048,1024]{1,0:T(8,128)(2,1)S(1)} %get-tuple-element.18.b_ref, f32[8,128]{1,0:T(8,128)S(1)} %get-tuple-element.20.lse_ref, ...), custom_call_target="tpu_custom_call" | custom-call | flops 2147483648 | bytes 1048576 | tf_op jit(solution)/shard_map/pallas_call | solution.py:354
  96.9 2.3 %collective-permute-start.22 = (bf16[128,1024]{1,0:T(8,128)(2,1)S(1)}, bf16[128,1024]{1,0:T(8,128)(2,1)S(1)}, u32[]{:S(2)}, u32[]{:S(2)}) collective-permute-start(bf16[128,1024]{1,0:T(8,128)(2,1)S(1)} %get-tuple-element.25), channel_id=1, source_target_pairs={{0,16},{8,24},{1,17},{9,25},{2,18},{10,26},{3,19},{11,27},{16,0},{... | collective-permute-start | bytes 786440 | tf_op jit(solution)/shard_map/ppermute | solution.py:300
  100.8 7.3 %collective-permute-done.23.refs_2_ = bf16[128,1024]{1,0:T(8,128)(2,1)S(1)} collective-permute-done((bf16[128,1024]{1,0:T(8,128)(2,1)S(1)}, bf16[128,1024]{1,0:T(8,128)(2,1)S(1)}, u32[]{:S(2)}, u32[]{:S(2)}) %collective-permute-start.23) | collective-permute-done | bytes 262176 | tf_op jit(solution)/shard_map/ppermute | solution.py:300
  109.7 1.9 %shard_map.57 = f32[128,1024]{1,0:T(8,128)} custom-call(f32[1]{0:T(128)S(6)} %div.7.scale_ref, bf16[128,1024]{1,0:T(8,128)(2,1)S(1)} %copy-done.1, bf16[128,1024]{1,0:T(8,128)(2,1)S(1)} %get-tuple-element.24.refs_0_, bf16[128,1024]{1,0:T(8,128)(2,1)S(1)} %collective-permute-done.22.refs_1_, bf16[128,1024]{1,0:T(8,128)(2,1)S(1)} %collective-permute-done.23.refs_2_, ...), custom_call_target="tpu_custom_call" | custom-call | tf_op jit(solution)/shard_map/pallas_call | solution.py:370
  (74 shorter events, 21.9 us)
Async XLA Ops:
  5.2 9.9 %collective-permute-start.7 = (bf16[272,1024]{1,0:T(8,128)(2,1)S(1)}, bf16[272,1024]{1,0:T(8,128)(2,1)S(1)}, u32[]{:S(2)}, u32[]{:S(2)}) collective-permute-start(bf16[272,1024]{1,0:T(8,128)(2,1)S(1)} %pad_maximum_fusion.own), channel_id=1, source_target_pairs={{0,32},{8,104},{1,33},{9,105},{2,34},{10,106},{3,35},{11,107},{16,... | collective-permute-start | bytes 1671176 | tf_op jit(solution)/shard_map/ppermute | solution.py:300
  7.8 20.0 %collective-permute-start.8 = (bf16[272,1024]{1,0:T(8,128)(2,1)S(1)}, bf16[272,1024]{1,0:T(8,128)(2,1)S(1)}, u32[]{:S(2)}, u32[]{:S(2)}) collective-permute-start(bf16[272,1024]{1,0:T(8,128)(2,1)S(1)} %pad_maximum_fusion.own), channel_id=1, source_target_pairs={{0,52},{8,124},{1,53},{9,125},{2,54},{10,126},{3,55},{11,127},{16,... | collective-permute-start | bytes 1671176 | tf_op jit(solution)/shard_map/ppermute | solution.py:300
  10.8 19.4 %collective-permute-start.1 = (bf16[272,1024]{1,0:T(8,128)(2,1)S(1)}, bf16[272,1024]{1,0:T(8,128)(2,1)S(1)}, u32[]{:S(2)}, u32[]{:S(2)}) collective-permute-start(bf16[272,1024]{1,0:T(8,128)(2,1)S(1)} %pad_maximum_fusion.own), channel_id=1, source_target_pairs={{0,1},{8,11},{1,2},{9,8},{2,3},{10,9},{3,0},{11,10},{16,17},{24,27... | collective-permute-start | bytes 1671176 | tf_op jit(solution)/shard_map/ppermute | solution.py:300
  14.6 15.7 %collective-permute-start.2 = (bf16[272,1024]{1,0:T(8,128)(2,1)S(1)}, bf16[272,1024]{1,0:T(8,128)(2,1)S(1)}, u32[]{:S(2)}, u32[]{:S(2)}) collective-permute-start(bf16[272,1024]{1,0:T(8,128)(2,1)S(1)} %pad_maximum_fusion.own), channel_id=1, source_target_pairs={{0,17},{8,27},{1,18},{9,24},{2,19},{10,25},{3,16},{11,26},{16,1},{... | collective-permute-start | bytes 1671176 | tf_op jit(solution)/shard_map/ppermute | solution.py:300
  14.6 20.8 %collective-permute-start.5 = (bf16[272,1024]{1,0:T(8,128)(2,1)S(1)}, bf16[272,1024]{1,0:T(8,128)(2,1)S(1)}, u32[]{:S(2)}, u32[]{:S(2)}) collective-permute-start(bf16[272,1024]{1,0:T(8,128)(2,1)S(1)} %pad_maximum_fusion.own), channel_id=1, source_target_pairs={{0,16},{8,28},{1,17},{9,29},{2,18},{10,30},{3,19},{11,31},{16,0},{... | collective-permute-start | bytes 1671176 | tf_op jit(solution)/shard_map/ppermute | solution.py:300
  27.9 8.5 %collective-permute-start.11 = (bf16[256,1024]{1,0:T(8,128)(2,1)S(1)}, bf16[256,1024]{1,0:T(8,128)(2,1)}, u32[]{:S(2)}, u32[]{:S(2)}) collective-permute-start(bf16[256,1024]{1,0:T(8,128)(2,1)S(1)} %pad_maximum_fusion.3), channel_id=1, source_target_pairs={{0,32},{8,104},{1,33},{9,105},{2,34},{10,106},{3,35},{11,107},{16,... | collective-permute-start | bytes 1572872 | tf_op jit(solution)/shard_map/ppermute | solution.py:300
  30.4 9.5 %collective-permute-start.4 = (bf16[272,1024]{1,0:T(8,128)(2,1)S(1)}, bf16[272,1024]{1,0:T(8,128)(2,1)S(1)}, u32[]{:S(2)}, u32[]{:S(2)}) collective-permute-start(bf16[272,1024]{1,0:T(8,128)(2,1)S(1)} %pad_maximum_fusion.2), channel_id=1, source_target_pairs={{0,8},{8,0},{1,9},{9,1},{2,10},{10,2},{3,11},{11,3},{16,24},{24,16... | collective-permute-start | bytes 1671176 | tf_op jit(solution)/shard_map/ppermute | solution.py:300
  31.6 10.6 %collective-permute-start.3 = (bf16[272,1024]{1,0:T(8,128)(2,1)}, bf16[272,1024]{1,0:T(8,128)(2,1)}, u32[]{:S(2)}, u32[]{:S(2)}) collective-permute-start(bf16[272,1024]{1,0:T(8,128)(2,1)} %pad_maximum_fusion.1), channel_id=1, source_target_pairs={{0,1},{8,11},{1,2},{9,8},{2,3},{10,9},{3,0},{11,10},{16,17},{24,27... | collective-permute-start | bytes 1671176 | tf_op jit(solution)/shard_map/ppermute | solution.py:300
  35.4 6.8 %collective-permute-start.10 = (bf16[272,1024]{1,0:T(8,128)(2,1)S(1)}, bf16[272,1024]{1,0:T(8,128)(2,1)}, u32[]{:S(2)}, u32[]{:S(2)}) collective-permute-start(bf16[272,1024]{1,0:T(8,128)(2,1)S(1)} %collective-permute-done.8.d_b), channel_id=1, source_target_pairs={{0,8},{8,0},{1,9},{9,1},{2,10},{10,2},{3,11},{11,3},{16,24},{24,16... | collective-permute-start | bytes 1671176 | tf_op jit(solution)/shard_map/ppermute | solution.py:300
  35.4 6.8 %collective-permute-start.9 = (bf16[272,1024]{1,0:T(8,128)(2,1)S(1)}, bf16[272,1024]{1,0:T(8,128)(2,1)}, u32[]{:S(2)}, u32[]{:S(2)}) collective-permute-start(bf16[272,1024]{1,0:T(8,128)(2,1)S(1)} %collective-permute-done.7.rx), channel_id=1, source_target_pairs={{0,8},{8,0},{1,9},{9,1},{2,10},{10,2},{3,11},{11,3},{16,24},{24,16... | collective-permute-start | bytes 1671176 | tf_op jit(solution)/shard_map/ppermute | solution.py:300
  36.4 5.7 %collective-permute-start.6 = (bf16[272,1024]{1,0:T(8,128)(2,1)S(1)}, bf16[272,1024]{1,0:T(8,128)(2,1)}, u32[]{:S(2)}, u32[]{:S(2)}) collective-permute-start(bf16[272,1024]{1,0:T(8,128)(2,1)S(1)} %collective-permute-done.5.ry), channel_id=1, source_target_pairs={{0,8},{8,0},{1,9},{9,1},{2,10},{10,2},{3,11},{11,3},{16,24},{24,16... | collective-permute-start | bytes 1671176 | tf_op jit(solution)/shard_map/ppermute | solution.py:300
  56.4 4.7 %collective-permute-start.14 = (f32[2,3,8,128]{3,2,1,0:T(8,128)S(1)}, f32[2,3,8,128]{3,2,1,0:T(8,128)S(1)}, u32[]{:S(2)}, u32[]{:S(2)}) collective-permute-start(f32[2,3,8,128]{3,2,1,0:T(8,128)S(1)} %pad_maximum_fusion.4.g0), channel_id=1, source_target_pairs={{0,3},{8,11},{1,0},{9,8},{2,1},{10,9},{3,2},{11,10},{16,19},{24,27... | collective-permute-start | bytes 73736 | tf_op jit(solution)/shard_map/ppermute | solution.py:300
  60.2 4.2 %collective-permute-start.15 = (f32[2,3,8,128]{3,2,1,0:T(8,128)S(1)}, f32[2,3,8,128]{3,2,1,0:T(8,128)S(1)}, u32[]{:S(2)}, u32[]{:S(2)}) collective-permute-start(f32[2,3,8,128]{3,2,1,0:T(8,128)S(1)} %pad_maximum_fusion.4.g0), channel_id=1, source_target_pairs={{0,2},{8,10},{1,3},{9,11},{2,0},{10,8},{3,1},{11,9},{16,18},{24,26... | collective-permute-start | bytes 73736 | tf_op jit(solution)/shard_map/ppermute | solution.py:300
  60.2 4.2 %collective-permute-start.16 = (f32[2,3,8,128]{3,2,1,0:T(8,128)S(1)}, f32[2,3,8,128]{3,2,1,0:T(8,128)S(1)}, u32[]{:S(2)}, u32[]{:S(2)}) collective-permute-start(f32[2,3,8,128]{3,2,1,0:T(8,128)S(1)} %pad_maximum_fusion.4.g0), channel_id=1, source_target_pairs={{0,1},{8,9},{1,2},{9,10},{2,3},{10,11},{3,0},{11,8},{16,17},{24,25... | collective-permute-start | bytes 73736 | tf_op jit(solution)/shard_map/ppermute | solution.py:300
  68.6 3.6 %collective-permute-start.18 = (f32[2,2,128]{2,1,0:T(2,128)S(1)}, f32[2,2,128]{2,1,0:T(2,128)S(1)}, u32[]{:S(2)}, u32[]{:S(2)}) collective-permute-start(f32[2,2,128]{2,1,0:T(2,128)S(1)} %pad_maximum_fusion.6), channel_id=1, source_target_pairs={{0,20},{8,28},{1,21},{9,29},{2,22},{10,30},{3,23},{11,31},{16,4},{... | collective-permute-start | bytes 6152 | tf_op jit(solution)/shard_map/ppermute | solution.py:300
  74.0 4.0 %collective-permute-start.20 = (f32[4,2,128]{2,1,0:T(2,128)S(1)}, f32[4,2,128]{2,1,0:T(2,128)S(1)}, u32[]{:S(2)}, u32[]{:S(2)}) collective-permute-start(f32[4,2,128]{2,1,0:T(2,128)S(1)} %pad_maximum_fusion.5.h0), channel_id=1, source_target_pairs={{0,64},{8,72},{1,65},{9,73},{2,66},{10,74},{3,67},{11,75},{16,80},... | collective-permute-start | bytes 12296 | tf_op jit(solution)/shard_map/ppermute | solution.py:300
  74.0 3.9 %collective-permute-start.21 = (f32[4,2,128]{2,1,0:T(2,128)S(1)}, f32[4,2,128]{2,1,0:T(2,128)S(1)}, u32[]{:S(2)}, u32[]{:S(2)}) collective-permute-start(f32[4,2,128]{2,1,0:T(2,128)S(1)} %pad_maximum_fusion.5.h0), channel_id=1, source_target_pairs={{0,32},{8,40},{1,33},{9,41},{2,34},{10,42},{3,35},{11,43},{16,48},... | collective-permute-start | bytes 12296 | tf_op jit(solution)/shard_map/ppermute | solution.py:300
  81.1 14.1 %collective-permute-start.27 = (bf16[128,1024]{1,0:T(8,128)(2,1)S(1)}, bf16[128,1024]{1,0:T(8,128)(2,1)S(1)}, u32[]{:S(2)}, u32[]{:S(2)}) collective-permute-start(bf16[128,1024]{1,0:T(8,128)(2,1)S(1)} %get-tuple-element.30), channel_id=1, source_target_pairs={{0,18},{8,26},{1,19},{9,27},{2,16},{10,24},{3,17},{11,25},{16,2},{... | collective-permute-start | bytes 786440 | tf_op jit(solution)/shard_map/ppermute | solution.py:300
  81.3 15.5 %collective-permute-start.28 = (bf16[128,1024]{1,0:T(8,128)(2,1)S(1)}, bf16[128,1024]{1,0:T(8,128)(2,1)S(1)}, u32[]{:S(2)}, u32[]{:S(2)}) collective-permute-start(bf16[128,1024]{1,0:T(8,128)(2,1)S(1)} %get-tuple-element.31), channel_id=1, source_target_pairs={{0,19},{8,25},{1,16},{9,26},{2,17},{10,27},{3,18},{11,24},{16,3},{... | collective-permute-start | bytes 786440 | tf_op jit(solution)/shard_map/ppermute | solution.py:300
  85.8 15.0 %collective-permute-start.25 = (bf16[128,1024]{1,0:T(8,128)(2,1)S(1)}, bf16[128,1024]{1,0:T(8,128)(2,1)S(1)}, u32[]{:S(2)}, u32[]{:S(2)}) collective-permute-start(bf16[128,1024]{1,0:T(8,128)(2,1)S(1)} %get-tuple-element.28), channel_id=1, source_target_pairs={{0,2},{8,10},{1,3},{9,11},{2,0},{10,8},{3,1},{11,9},{16,18},{24,26... | collective-permute-start | bytes 786440 | tf_op jit(solution)/shard_map/ppermute | solution.py:300
  87.8 13.0 %collective-permute-start.26 = (bf16[128,1024]{1,0:T(8,128)(2,1)S(1)}, bf16[128,1024]{1,0:T(8,128)(2,1)S(1)}, u32[]{:S(2)}, u32[]{:S(2)}) collective-permute-start(bf16[128,1024]{1,0:T(8,128)(2,1)S(1)} %get-tuple-element.29), channel_id=1, source_target_pairs={{0,17},{8,27},{1,18},{9,24},{2,19},{10,25},{3,16},{11,26},{16,1},{... | collective-permute-start | bytes 786440 | tf_op jit(solution)/shard_map/ppermute | solution.py:300
  91.1 16.9 %collective-permute-start.23 = (bf16[128,1024]{1,0:T(8,128)(2,1)S(1)}, bf16[128,1024]{1,0:T(8,128)(2,1)S(1)}, u32[]{:S(2)}, u32[]{:S(2)}) collective-permute-start(bf16[128,1024]{1,0:T(8,128)(2,1)S(1)} %get-tuple-element.26), channel_id=1, source_target_pairs={{0,3},{8,9},{1,0},{9,10},{2,1},{10,11},{3,2},{11,8},{16,19},{24,25... | collective-permute-start | bytes 786440 | tf_op jit(solution)/shard_map/ppermute | solution.py:300
  95.3 14.4 %collective-permute-start.24 = (bf16[128,1024]{1,0:T(8,128)(2,1)S(1)}, bf16[128,1024]{1,0:T(8,128)(2,1)S(1)}, u32[]{:S(2)}, u32[]{:S(2)}) collective-permute-start(bf16[128,1024]{1,0:T(8,128)(2,1)S(1)} %get-tuple-element.27), channel_id=1, source_target_pairs={{0,1},{8,11},{1,2},{9,8},{2,3},{10,9},{3,0},{11,10},{16,17},{24,27... | collective-permute-start | bytes 786440 | tf_op jit(solution)/shard_map/ppermute | solution.py:300
  96.9 12.9 %collective-permute-start.22 = (bf16[128,1024]{1,0:T(8,128)(2,1)S(1)}, bf16[128,1024]{1,0:T(8,128)(2,1)S(1)}, u32[]{:S(2)}, u32[]{:S(2)}) collective-permute-start(bf16[128,1024]{1,0:T(8,128)(2,1)S(1)} %get-tuple-element.25), channel_id=1, source_target_pairs={{0,16},{8,24},{1,17},{9,25},{2,18},{10,26},{3,19},{11,27},{16,0},{... | collective-permute-start | bytes 786440 | tf_op jit(solution)/shard_map/ppermute | solution.py:300
  (12 other events, 57.0 us)

commit v5 on v4

--- a/solution.py
+++ b/solution.py
@@ -13,7 +13,7 @@
 LANES = 128
 EXTRA = 8
 BLOCK = 256
-VMEM_LIMIT = 36 << 20
+VMEM_LIMIT = 16 << 20
 AXES = ("row", "col")
 VMEM = pl.BlockSpec(memory_space=pltpu.VMEM)
 SMEM = pl.BlockSpec(memory_space=pltpu.SMEM)
@@ -54,16 +54,8 @@
 FROM_Z = [to(lambda x, y, z, k, g, d=d: (x, y, z - d, k)) for d in (1, 2, 3)]
 FROM_X = [to(lambda x, y, z, k, g, d=d: (x - d, y, z, k)) for d in (1, 2, 3)]
 
-OWNERS = [
-    None,
-    PARTNER_A,
-    to(lambda x, y, z, k, g: (x, y, z - g, k)),
-    ALONG_Z,
-    to(lambda x, y, z, k, g: (x, y, z + 2, k)),
-    ALONG_YZ,
-    to(lambda x, y, z, k, g: (x, mate_a(y), z + 2, k)),
-    to(lambda x, y, z, k, g: (x, mate_a(y), z - g, k)),
-]
+BACK_Z = to(lambda x, y, z, k, g: (x, y, z - g, k))
+BACK_YZ = to(lambda x, y, z, k, g: (x, mate_a(y), z - g, k))
 
 COLUMNS = [
     (0, 0, 0), (0, 0, 1), (-1, 0, 0), (-1, 0, 1), (-1, 1, 0), (-1, 1, 1), (1, 0, 1), (1, 0, 0),
@@ -105,11 +97,10 @@
 
     put(a_ref, 0, own, 0)
     put(a_ref, 2, rz, 0)
-    put(a_ref, 3, s_z, 0)
-    put(a_ref, 4, fz, 0)
-    put(a_ref, 5, s_z, n)
-    put(a_ref, 6, fz, n)
-    put(a_ref, 7, d_a, 0)
+    put(a_ref, 3, s_z, n)
+    put(a_ref, 4, s_z, 0)
+    put(a_ref, 5, d_a, 0)
+    put(a_ref, 6, fz, 0, e)
     for src, at in ((own, 0), (rx, 2), (d_b, 4), (s_rx, 6), (s_db, 8), (fx, 10), (s_fx, 12)):
         put(b_ref, at, src, 0, e)
 
@@ -126,7 +117,7 @@
 
     tail = lambda src: src[e : e + 2 * EXTRA, 0 : 2 * n].astype(F32)
     tails = [tail(src) for src in (own, rz, d_a, fz, s_z, ry, s_ry)]
-    head = [(0, 0), (1, 0), (4, 0), (3, 0), (4, EXTRA), (3, EXTRA), (2, 0)]
+    head = [(0, 0), (1, 0), (4, EXTRA), (4, 0), (2, 0), (3, 0), (3, EXTRA)]
     rows = [tails[p][r : r + 1] for p, r in head]
     rows.insert(1, jnp.where(core == 0, tails[5][0:1], tails[6][EXTRA : EXTRA + 1]))
     rows = jnp.concatenate(rows, axis=0).astype(I32)
@@ -213,7 +204,7 @@
     n = LANES
     per = BLOCK // n
     n_b = s_ref.shape[1]
-    outs, d_ref = refs[:per], refs[-1]
+    outs, d_ref = refs[per:] if which == 2 else refs, refs[-1]
     if which == 0:
         core, y, x = place[0], place[1], place[27]
         total = jnp.zeros((1, n), F32)
@@ -252,9 +243,12 @@
             mate = jnp.where(lane == mates - t * n, 1.0, 0.0)
             d = (jnp.exp(s - mine) - mate) + (jnp.exp(s - others[t]) - mate)
             d_ref[i * n : (i + 1) * n, cols] = d.astype(BF16)
-    out = jnp.dot(d_ref[...], b_ref[...], preferred_element_type=F32).astype(BF16)
+    out = jnp.dot(d_ref[...], b_ref[...], preferred_element_type=F32)
     for i in range(per):
-        outs[i][...] = out[i * n : (i + 1) * n]
+        shard = out[i * n : (i + 1) * n]
+        if which == 2:
+            shard = shard + refs[i][...].astype(F32)
+        outs[i][...] = shard.astype(BF16)
 
 
 def final_kernel(scale_ref, x_ref, *refs):
@@ -283,8 +277,8 @@
     slot_a = lambda yy, zz: (yy & 1) * 4 + (zz & 3)
     slot_b = lambda xx, yy, same: (1 - (yy & 1)) * 4 + (xx & 3) + (0 if same else 8)
     slots_a = [
-        slot_a(y, z), slot_a(y ^ 1, z), slot_a(y, z - sign), slot_a(y, z + sign),
-        slot_a(y, z + 2), slot_a(y ^ 1, z + sign), slot_a(y ^ 1, z + 2), slot_a(y ^ 1, z - sign),
+        slot_a(y, z), slot_a(y ^ 1, z), slot_a(y, z - sign), slot_a(y ^ 1, z + sign),
+        slot_a(y, z + sign), slot_a(y ^ 1, z - sign), slot_a(y, z + 2), slot_a(y ^ 1, z + 2),
     ]
     slots_b = [
         slot_b(x, y, True), slot_b(x, y, False),
@@ -348,22 +342,28 @@
     four = jnp.concatenate([twins, send(twins, PARTNER_B)], axis=0)
     h1, h2, h3 = (send(four, pairs) for pairs in FROM_X)
     scores, block_b = fast(scores), fast(block_b)
-    parts = [None] * 8
-    for step in reversed(range(4)):
-        outs = [shape((views, width), BF16)] * 2 + ([shape((1, 1), F32)] if step == 0 else [])
-        got = pl.pallas_call(
-            functools.partial(grad_kernel, step),
+
+    def part(which, outs, *more):
+        return pl.pallas_call(
+            functools.partial(grad_kernel, which),
             out_shape=outs,
-            in_specs=[SMEM] + [VMEM] * 8,
+            in_specs=[SMEM] + [VMEM] * (8 + len(more)),
             out_specs=[VMEM] * len(outs),
             scratch_shapes=[pltpu.VMEM((BLOCK, n_b), BF16)],
             compiler_params=pltpu.CompilerParams(vmem_limit_bytes=16 << 20),
             cost_estimate=pl.CostEstimate(flops=4 * BLOCK * n_b * width, bytes_accessed=1 << 20, transcendentals=0),
-        )(place, scores, block_b, lse, four, h1, h2, h3, mates)
-        for i in (1, 0):
-            shard = 2 * step + i
-            parts[shard] = send(got[i], OWNERS[shard]) if shard else got[i]
-    loss = got[2]
+        )(place, scores, block_b, lse, four, h1, h2, h3, mates, *more)
+
+    one = shape((views, width), BF16)
+    far = part(3, [one, one])
+    far = [send(far[0], ALONG_Z), send(far[1], BACK_Z)]
+    here = part(0, [one, one, shape((1, 1), F32)])
+    parts = [here[0], send(here[1], PARTNER_A)]
+    loss = here[2]
+    near = part(1, [one, one])
+    parts += [send(near[1], ALONG_YZ), send(near[0], BACK_Z)]
+    sums = part(2, [one, one], *far)
+    parts += [send(sums[1], BACK_YZ), send(sums[0], ALONG_Z)]
     total = views * 128
     rows = views // 4
     block = pl.BlockSpec((rows, width), lambda i: (i, 0))
@@ -371,7 +371,7 @@
         final_kernel,
         grid=(views // rows,),
         out_shape=shape((views, width), F32),
-        in_specs=[SMEM] + [block] * 9,
+        in_specs=[SMEM] + [block] * 7,
         out_specs=block,
         compiler_params=small,
     )(inv_temp / total, embeddings, *parts)

time: 113 us -> 109 us (0.965); the launches traced: 113 us -> 107 us
  starting transfers between devices: 41.6 us -> 39.1 us
  waiting for transfers between devices: 39.2 us -> 37.9 us
  local copies, waits for them, and re-layouts: 4.99 us -> 3.73 us
    ppermute x29, starting transfers between devices: 41.6 us -> 39.1 us  [body(): send = lambda v, pairs: lax.ppermute(v, AXES, pairs)]
    ppermute x29, waiting for transfers between devices: 39.2 us -> 37.9 us  [body(): send = lambda v, pairs: lax.ppermute(v, AXES, pairs)]
    unnamed x14 -> x10, local copies, waits for them, and re-layouts: 4.13 us -> 3.46 us
  transfers between devices with their start and end apart: 29 -> 29, of which waited for: 14 -> 13; matrix products, arithmetic and copies ran while one was open for 2% -> 1% of each run, Pallas kernels for 7% -> 8%
where the time goes in v5:
time: 109 us; the launch traced here: 107 us
  starting transfers between devices  39.1 us (36%)
  waiting for transfers between devices  37.9 us (35%)
  Pallas kernels  22.1 us (20%)
  local copies, waits for them, and re-layouts  3.73 us (3%)
  between operations  3.26 us (3%)
    ppermute x29, starting transfers between devices, body(): send = lambda v, pairs: lax.ppermute(v, AXES, pairs)  39.1 us
    ppermute x29, waiting for transfers between devices, body(): send = lambda v, pairs: lax.ppermute(v, AXES, pairs)  37.9 us
    pallas_call x4, Pallas kernels, part(): pl.pallas_call(functools.partial(grad_kernel, which), out_shape=outs, in_...  10.6 us
    pallas_call x1, Pallas kernels, body(): pl.pallas_call(score_kernel, out_shape=[pltpu.VMEM((n_a, n_b), F32), pltp...  8.82 us
    unnamed x10, local copies, waits for them, and re-layouts  3.46 us
  transfers between devices with their start and end apart: 29, of which 13 were waited for; matrix products, arithmetic and copies ran while one was open for 1% of the time, Pallas kernels for 8%

profile of v5, /device:TPU:1, one launch (start us, length us, event | category | flops | bytes accessed | tf_op | source)
XLA Modules:
  0.0 107.0 jit_solution(3269931491488529)
XLA Ops:
  2.4 1.5 %collective-permute-start = (bf16[144,1024]{1,0:T(8,128)(2,1)S(1)}, bf16[144,1024]{1,0:T(8,128)(2,1)S(1)}, u32[]{:S(2)}, u32[]{:S(2)}) collective-permute-start(bf16[144,1024]{1,0:T(8,128)(2,1)S(1)} %shard_map.50), channel_id=1, source_target_pairs={{0,8},{8,0},{1,9},{9,1},{2,10},{10,2},{3,11},{11,3},{16,24},{24,16... | collective-permute-start | bytes 884744 | tf_op jit(solution)/shard_map/ppermute | solution.py:294
  5.2 2.6 %collective-permute-start.7 = (bf16[272,1024]{1,0:T(8,128)(2,1)S(1)}, bf16[272,1024]{1,0:T(8,128)(2,1)S(1)}, u32[]{:S(2)}, u32[]{:S(2)}) collective-permute-start(bf16[272,1024]{1,0:T(8,128)(2,1)S(1)} %pad_maximum_fusion.own), channel_id=1, source_target_pairs={{0,32},{8,104},{1,33},{9,105},{2,34},{10,106},{3,35},{11,107},{16,... | collective-permute-start | bytes 1671176 | tf_op jit(solution)/shard_map/ppermute | solution.py:294
  7.8 3.0 %collective-permute-start.8 = (bf16[272,1024]{1,0:T(8,128)(2,1)S(1)}, bf16[272,1024]{1,0:T(8,128)(2,1)S(1)}, u32[]{:S(2)}, u32[]{:S(2)}) collective-permute-start(bf16[272,1024]{1,0:T(8,128)(2,1)S(1)} %pad_maximum_fusion.own), channel_id=1, source_target_pairs={{0,52},{8,124},{1,53},{9,125},{2,54},{10,126},{3,55},{11,127},{16,... | collective-permute-start | bytes 1671176 | tf_op jit(solution)/shard_map/ppermute | solution.py:294
  10.8 3.8 %collective-permute-start.1 = (bf16[272,1024]{1,0:T(8,128)(2,1)S(1)}, bf16[272,1024]{1,0:T(8,128)(2,1)S(1)}, u32[]{:S(2)}, u32[]{:S(2)}) collective-permute-start(bf16[272,1024]{1,0:T(8,128)(2,1)S(1)} %pad_maximum_fusion.own), channel_id=1, source_target_pairs={{0,1},{8,11},{1,2},{9,8},{2,3},{10,9},{3,0},{11,10},{16,17},{24,27... | collective-permute-start | bytes 1671176 | tf_op jit(solution)/shard_map/ppermute | solution.py:294
  15.1 12.8 %collective-permute-done.8.d_b = bf16[272,1024]{1,0:T(8,128)(2,1)S(1)} collective-permute-done((bf16[272,1024]{1,0:T(8,128)(2,1)S(1)}, bf16[272,1024]{1,0:T(8,128)(2,1)S(1)}, u32[]{:S(2)}, u32[]{:S(2)}) %collective-permute-start.8) | collective-permute-done | bytes 557088 | tf_op jit(solution)/shard_map/ppermute | solution.py:294
  27.9 2.3 %collective-permute-start.11 = (bf16[256,1024]{1,0:T(8,128)(2,1)S(1)}, bf16[256,1024]{1,0:T(8,128)(2,1)}, u32[]{:S(2)}, u32[]{:S(2)}) collective-permute-start(bf16[256,1024]{1,0:T(8,128)(2,1)S(1)} %pad_maximum_fusion.3), channel_id=1, source_target_pairs={{0,32},{8,104},{1,33},{9,105},{2,34},{10,106},{3,35},{11,107},{16,... | collective-permute-start | bytes 1572872 | tf_op jit(solution)/shard_map/ppermute | solution.py:294
  31.6 3.8 %collective-permute-start.3 = (bf16[272,1024]{1,0:T(8,128)(2,1)}, bf16[272,1024]{1,0:T(8,128)(2,1)}, u32[]{:S(2)}, u32[]{:S(2)}) collective-permute-start(bf16[272,1024]{1,0:T(8,128)(2,1)} %pad_maximum_fusion.1), channel_id=1, source_target_pairs={{0,1},{8,11},{1,2},{9,8},{2,3},{10,9},{3,0},{11,10},{16,17},{24,27... | collective-permute-start | bytes 1671176 | tf_op jit(solution)/shard_map/ppermute | solution.py:294
  36.4 3.5 %collective-permute-start.6 = (bf16[272,1024]{1,0:T(8,128)(2,1)S(1)}, bf16[272,1024]{1,0:T(8,128)(2,1)}, u32[]{:S(2)}, u32[]{:S(2)}) collective-permute-start(bf16[272,1024]{1,0:T(8,128)(2,1)S(1)} %collective-permute-done.5.ry), channel_id=1, source_target_pairs={{0,8},{8,0},{1,9},{9,1},{2,10},{10,2},{3,11},{11,3},{16,24},{24,16... | collective-permute-start | bytes 1671176 | tf_op jit(solution)/shard_map/ppermute | solution.py:294
  44.0 8.8 %shard_map.51 = (f32[1024,2048]{1,0:T(8,128)S(1)}, bf16[2048,1024]{1,0:T(8,128)(2,1)S(1)}, f32[3,8,128]{2,1,0:T(8,128)S(1)}, s32[8,128]{1,0:T(8,128)S(1)}) custom-call(s32[28]{0:T(128)S(1)} %stack.133.place, f32[1]{0:T(128)S(6)} %copy.5.scale_ref, bf16[272,1024]{1,0:T(8,128)(2,1)S(1)} %pad_maximum_fusion.own, ...), custom_call_target="tpu_custom_call" | custom-call | tf_op jit(solution)/shard_map/pallas_call | solution.py:319
  52.9 2.5 %collective-permute-done.13 = f32[3,8,128]{2,1,0:T(8,128)S(1)} collective-permute-done((f32[3,8,128]{2,1,0:T(8,128)S(1)}, f32[3,8,128]{2,1,0:T(8,128)S(1)}, u32[]{:S(2)}, u32[]{:S(2)}) %collective-permute-start.13) | collective-permute-done | bytes 12320 | tf_op jit(solution)/shard_map/ppermute | solution.py:294
  55.4 3.8 %collective-permute-start.14 = (f32[2,3,8,128]{3,2,1,0:T(8,128)S(1)}, f32[2,3,8,128]{3,2,1,0:T(8,128)S(1)}, u32[]{:S(2)}, u32[]{:S(2)}) collective-permute-start(f32[2,3,8,128]{3,2,1,0:T(8,128)S(1)} %pad_maximum_fusion.4.g0), channel_id=1, source_target_pairs={{0,3},{8,11},{1,0},{9,8},{2,1},{10,9},{3,2},{11,10},{16,19},{24,27... | collective-permute-start | bytes 73736 | tf_op jit(solution)/shard_map/ppermute | solution.py:294
  60.1 3.2 %collective-permute-done.15.g2 = f32[2,3,8,128]{3,2,1,0:T(8,128)S(1)} collective-permute-done((f32[2,3,8,128]{3,2,1,0:T(8,128)S(1)}, f32[2,3,8,128]{3,2,1,0:T(8,128)S(1)}, u32[]{:S(2)}, u32[]{:S(2)}) %collective-permute-start.15) | collective-permute-done | bytes 24608 | tf_op jit(solution)/shard_map/ppermute | solution.py:294
  64.0 2.8 %collective-permute-start.17 = (f32[2,128]{1,0:T(2,128)S(1)}, f32[2,128]{1,0:T(2,128)S(1)}, u32[]{:S(2)}, u32[]{:S(2)}) collective-permute-start(f32[2,128]{1,0:T(2,128)S(1)} %get-tuple-element.21), channel_id=1, source_target_pairs={{0,8},{8,0},{1,9},{9,1},{2,10},{10,2},{3,11},{11,3},{16,24},{24,16... | collective-permute-start | bytes 3080 | tf_op jit(solution)/shard_map/ppermute | solution.py:294
  67.6 3.6 %collective-permute-done.18 = f32[2,2,128]{2,1,0:T(2,128)S(1)} collective-permute-done((f32[2,2,128]{2,1,0:T(2,128)S(1)}, f32[2,2,128]{2,1,0:T(2,128)S(1)}, u32[]{:S(2)}, u32[]{:S(2)}) %collective-permute-start.18) | collective-permute-done | bytes 2080 | tf_op jit(solution)/shard_map/ppermute | solution.py:294
  71.3 1.7 %collective-permute-start.19 = (f32[4,2,128]{2,1,0:T(2,128)S(1)}, f32[4,2,128]{2,1,0:T(2,128)S(1)}, u32[]{:S(2)}, u32[]{:S(2)}) collective-permute-start(f32[4,2,128]{2,1,0:T(2,128)S(1)} %pad_maximum_fusion.5.h0), channel_id=1, source_target_pairs={{0,96},{8,104},{1,97},{9,105},{2,98},{10,106},{3,99},{11,107},{16,... | collective-permute-start | bytes 12296 | tf_op jit(solution)/shard_map/ppermute | solution.py:294
  73.8 3.2 %collective-permute-done.20.h2 = f32[4,2,128]{2,1,0:T(2,128)S(1)} collective-permute-done((f32[4,2,128]{2,1,0:T(2,128)S(1)}, f32[4,2,128]{2,1,0:T(2,128)S(1)}, u32[]{:S(2)}, u32[]{:S(2)}) %collective-permute-start.20) | collective-permute-done | bytes 4128 | tf_op jit(solution)/shard_map/ppermute | solution.py:294
  77.0 2.5 %shard_map.55 = (bf16[128,1024]{1,0:T(8,128)(2,1)S(1)}, bf16[128,1024]{1,0:T(8,128)(2,1)S(1)}) custom-call(s32[28]{0:T(128)S(1)} %stack.133.place, f32[1024,2048]{1,0:T(8,128)S(1)} %get-tuple-element.17.s_ref, bf16[2048,1024]{1,0:T(8,128)(2,1)S(1)} %get-tuple-element.18.b_ref, f32[8,128]{1,0:T(8,128)S(1)} %get-tuple-element.20.lse_ref, ...), custom_call_target="tpu_custom_call" | custom-call | flops 2147483648 | bytes 1048576 | tf_op jit(solution)/shard_map/pallas_call | solution.py:347
  81.1 2.5 %shard_map.54 = (bf16[128,1024]{1,0:T(8,128)(2,1)S(1)}, bf16[128,1024]{1,0:T(8,128)(2,1)S(1)}) custom-call(s32[28]{0:T(128)S(1)} %stack.133.place, f32[1024,2048]{1,0:T(8,128)S(1)} %get-tuple-element.17.s_ref, bf16[2048,1024]{1,0:T(8,128)(2,1)S(1)} %get-tuple-element.18.b_ref, f32[8,128]{1,0:T(8,128)S(1)} %get-tuple-element.20.lse_ref, ...), custom_call_target="tpu_custom_call" | custom-call | flops 2147483648 | bytes 1048576 | tf_op jit(solution)/shard_map/pallas_call | solution.py:347
  83.9 3.0 %shard_map.53 = (bf16[128,1024]{1,0:T(8,128)(2,1)S(1)}, bf16[128,1024]{1,0:T(8,128)(2,1)S(1)}, f32[1,1]{1,0:T(1,128)}) custom-call(s32[28]{0:T(128)S(1)} %stack.133.place, f32[1024,2048]{1,0:T(8,128)S(1)} %get-tuple-element.17.s_ref, bf16[2048,1024]{1,0:T(8,128)(2,1)S(1)} %get-tuple-element.18.b_ref, f32[8,128]{1,0:T(8,128)S(1)} %get-tuple-element.20.lse_ref, ...), custom_call_target="tpu_custom_call" | custom-call | flops 2147483648 | bytes 1048576 | tf_op jit(solution)/shard_map/pallas_call | solution.py:347
  86.9 2.8 %collective-permute-start.22 = (bf16[128,1024]{1,0:T(8,128)(2,1)S(1)}, bf16[128,1024]{1,0:T(8,128)(2,1)S(1)}, u32[]{:S(2)}, u32[]{:S(2)}) collective-permute-start(bf16[128,1024]{1,0:T(8,128)(2,1)S(1)} %get-tuple-element.25), channel_id=1, source_target_pairs={{0,16},{8,24},{1,17},{9,25},{2,18},{10,26},{3,19},{11,27},{16,0},{... | collective-permute-start | bytes 786440 | tf_op jit(solution)/shard_map/ppermute | solution.py:294
  89.7 2.6 %shard_map.56 = (bf16[128,1024]{1,0:T(8,128)(2,1)S(1)}, bf16[128,1024]{1,0:T(8,128)(2,1)S(1)}) custom-call(s32[28]{0:T(128)S(1)} %stack.133.place, f32[1024,2048]{1,0:T(8,128)S(1)} %get-tuple-element.17.s_ref, bf16[2048,1024]{1,0:T(8,128)(2,1)S(1)} %get-tuple-element.18.b_ref, f32[8,128]{1,0:T(8,128)S(1)} %get-tuple-element.20.lse_ref, ...), custom_call_target="tpu_custom_call" | custom-call | flops 2147483648 | bytes 1048576 | tf_op jit(solution)/shard_map/pallas_call | solution.py:347
  92.4 2.7 %collective-permute-start.28 = (bf16[128,1024]{1,0:T(8,128)(2,1)S(1)}, bf16[128,1024]{1,0:T(8,128)(2,1)S(1)}, u32[]{:S(2)}, u32[]{:S(2)}) collective-permute-start(bf16[128,1024]{1,0:T(8,128)(2,1)S(1)} %get-tuple-element.31), channel_id=1, source_target_pairs={{0,1},{8,11},{1,2},{9,8},{2,3},{10,9},{3,0},{11,10},{16,17},{24,27... | collective-permute-start | bytes 786440 | tf_op jit(solution)/shard_map/ppermute | solution.py:294
  96.4 7.6 %collective-permute-done.27.refs_4_ = bf16[128,1024]{1,0:T(8,128)(2,1)S(1)} collective-permute-done((bf16[128,1024]{1,0:T(8,128)(2,1)S(1)}, bf16[128,1024]{1,0:T(8,128)(2,1)S(1)}, u32[]{:S(2)}, u32[]{:S(2)}) %collective-permute-start.27) | collective-permute-done | bytes 262176 | tf_op jit(solution)/shard_map/ppermute | solution.py:294
  104.0 1.9 %shard_map.57 = f32[128,1024]{1,0:T(8,128)} custom-call(f32[1]{0:T(128)S(6)} %div.7.scale_ref, bf16[128,1024]{1,0:T(8,128)(2,1)S(1)} %copy-done.1, bf16[128,1024]{1,0:T(8,128)(2,1)S(1)} %get-tuple-element.24.refs_0_, bf16[128,1024]{1,0:T(8,128)(2,1)S(1)} %collective-permute-done.22.refs_1_, bf16[128,1024]{1,0:T(8,128)(2,1)S(1)} %collective-permute-done.23.refs_2_, ...), custom_call_target="tpu_custom_call" | custom-call | tf_op jit(solution)/shard_map/pallas_call | solution.py:370
  (70 shorter events, 15.2 us)
Async XLA Ops:
  5.2 9.9 %collective-permute-start.7 = (bf16[272,1024]{1,0:T(8,128)(2,1)S(1)}, bf16[272,1024]{1,0:T(8,128)(2,1)S(1)}, u32[]{:S(2)}, u32[]{:S(2)}) collective-permute-start(bf16[272,1024]{1,0:T(8,128)(2,1)S(1)} %pad_maximum_fusion.own), channel_id=1, source_target_pairs={{0,32},{8,104},{1,33},{9,105},{2,34},{10,106},{3,35},{11,107},{16,... | collective-permute-start | bytes 1671176 | tf_op jit(solution)/shard_map/ppermute | solution.py:294
  7.8 20.0 %collective-permute-start.8 = (bf16[272,1024]{1,0:T(8,128)(2,1)S(1)}, bf16[272,1024]{1,0:T(8,128)(2,1)S(1)}, u32[]{:S(2)}, u32[]{:S(2)}) collective-permute-start(bf16[272,1024]{1,0:T(8,128)(2,1)S(1)} %pad_maximum_fusion.own), channel_id=1, source_target_pairs={{0,52},{8,124},{1,53},{9,125},{2,54},{10,126},{3,55},{11,127},{16,... | collective-permute-start | bytes 1671176 | tf_op jit(solution)/shard_map/ppermute | solution.py:294
  10.8 19.4 %collective-permute-start.1 = (bf16[272,1024]{1,0:T(8,128)(2,1)S(1)}, bf16[272,1024]{1,0:T(8,128)(2,1)S(1)}, u32[]{:S(2)}, u32[]{:S(2)}) collective-permute-start(bf16[272,1024]{1,0:T(8,128)(2,1)S(1)} %pad_maximum_fusion.own), channel_id=1, source_target_pairs={{0,1},{8,11},{1,2},{9,8},{2,3},{10,9},{3,0},{11,10},{16,17},{24,27... | collective-permute-start | bytes 1671176 | tf_op jit(solution)/shard_map/ppermute | solution.py:294
  14.6 15.7 %collective-permute-start.2 = (bf16[272,1024]{1,0:T(8,128)(2,1)S(1)}, bf16[272,1024]{1,0:T(8,128)(2,1)S(1)}, u32[]{:S(2)}, u32[]{:S(2)}) collective-permute-start(bf16[272,1024]{1,0:T(8,128)(2,1)S(1)} %pad_maximum_fusion.own), channel_id=1, source_target_pairs={{0,17},{8,27},{1,18},{9,24},{2,19},{10,25},{3,16},{11,26},{16,1},{... | collective-permute-start | bytes 1671176 | tf_op jit(solution)/shard_map/ppermute | solution.py:294
  14.6 20.8 %collective-permute-start.5 = (bf16[272,1024]{1,0:T(8,128)(2,1)S(1)}, bf16[272,1024]{1,0:T(8,128)(2,1)S(1)}, u32[]{:S(2)}, u32[]{:S(2)}) collective-permute-start(bf16[272,1024]{1,0:T(8,128)(2,1)S(1)} %pad_maximum_fusion.own), channel_id=1, source_target_pairs={{0,16},{8,28},{1,17},{9,29},{2,18},{10,30},{3,19},{11,31},{16,0},{... | collective-permute-start | bytes 1671176 | tf_op jit(solution)/shard_map/ppermute | solution.py:294
  27.9 8.5 %collective-permute-start.11 = (bf16[256,1024]{1,0:T(8,128)(2,1)S(1)}, bf16[256,1024]{1,0:T(8,128)(2,1)}, u32[]{:S(2)}, u32[]{:S(2)}) collective-permute-start(bf16[256,1024]{1,0:T(8,128)(2,1)S(1)} %pad_maximum_fusion.3), channel_id=1, source_target_pairs={{0,32},{8,104},{1,33},{9,105},{2,34},{10,106},{3,35},{11,107},{16,... | collective-permute-start | bytes 1572872 | tf_op jit(solution)/shard_map/ppermute | solution.py:294
  30.4 9.5 %collective-permute-start.4 = (bf16[272,1024]{1,0:T(8,128)(2,1)S(1)}, bf16[272,1024]{1,0:T(8,128)(2,1)S(1)}, u32[]{:S(2)}, u32[]{:S(2)}) collective-permute-start(bf16[272,1024]{1,0:T(8,128)(2,1)S(1)} %pad_maximum_fusion.2), channel_id=1, source_target_pairs={{0,8},{8,0},{1,9},{9,1},{2,10},{10,2},{3,11},{11,3},{16,24},{24,16... | collective-permute-start | bytes 1671176 | tf_op jit(solution)/shard_map/ppermute | solution.py:294
  31.6 10.6 %collective-permute-start.3 = (bf16[272,1024]{1,0:T(8,128)(2,1)}, bf16[272,1024]{1,0:T(8,128)(2,1)}, u32[]{:S(2)}, u32[]{:S(2)}) collective-permute-start(bf16[272,1024]{1,0:T(8,128)(2,1)} %pad_maximum_fusion.1), channel_id=1, source_target_pairs={{0,1},{8,11},{1,2},{9,8},{2,3},{10,9},{3,0},{11,10},{16,17},{24,27... | collective-permute-start | bytes 1671176 | tf_op jit(solution)/shard_map/ppermute | solution.py:294
  35.4 6.8 %collective-permute-start.10 = (bf16[272,1024]{1,0:T(8,128)(2,1)S(1)}, bf16[272,1024]{1,0:T(8,128)(2,1)}, u32[]{:S(2)}, u32[]{:S(2)}) collective-permute-start(bf16[272,1024]{1,0:T(8,128)(2,1)S(1)} %collective-permute-done.8.d_b), channel_id=1, source_target_pairs={{0,8},{8,0},{1,9},{9,1},{2,10},{10,2},{3,11},{11,3},{16,24},{24,16... | collective-permute-start | bytes 1671176 | tf_op jit(solution)/shard_map/ppermute | solution.py:294
  35.4 6.8 %collective-permute-start.9 = (bf16[272,1024]{1,0:T(8,128)(2,1)S(1)}, bf16[272,1024]{1,0:T(8,128)(2,1)}, u32[]{:S(2)}, u32[]{:S(2)}) collective-permute-start(bf16[272,1024]{1,0:T(8,128)(2,1)S(1)} %collective-permute-done.7.rx), channel_id=1, source_target_pairs={{0,8},{8,0},{1,9},{9,1},{2,10},{10,2},{3,11},{11,3},{16,24},{24,16... | collective-permute-start | bytes 1671176 | tf_op jit(solution)/shard_map/ppermute | solution.py:294
  36.4 5.7 %collective-permute-start.6 = (bf16[272,1024]{1,0:T(8,128)(2,1)S(1)}, bf16[272,1024]{1,0:T(8,128)(2,1)}, u32[]{:S(2)}, u32[]{:S(2)}) collective-permute-start(bf16[272,1024]{1,0:T(8,128)(2,1)S(1)} %collective-permute-done.5.ry), channel_id=1, source_target_pairs={{0,8},{8,0},{1,9},{9,1},{2,10},{10,2},{3,11},{11,3},{16,24},{24,16... | collective-permute-start | bytes 1671176 | tf_op jit(solution)/shard_map/ppermute | solution.py:294
  55.4 4.7 %collective-permute-start.14 = (f32[2,3,8,128]{3,2,1,0:T(8,128)S(1)}, f32[2,3,8,128]{3,2,1,0:T(8,128)S(1)}, u32[]{:S(2)}, u32[]{:S(2)}) collective-permute-start(f32[2,3,8,128]{3,2,1,0:T(8,128)S(1)} %pad_maximum_fusion.4.g0), channel_id=1, source_target_pairs={{0,3},{8,11},{1,0},{9,8},{2,1},{10,9},{3,2},{11,10},{16,19},{24,27... | collective-permute-start | bytes 73736 | tf_op jit(solution)/shard_map/ppermute | solution.py:294
  59.2 4.2 %collective-permute-start.15 = (f32[2,3,8,128]{3,2,1,0:T(8,128)S(1)}, f32[2,3,8,128]{3,2,1,0:T(8,128)S(1)}, u32[]{:S(2)}, u32[]{:S(2)}) collective-permute-start(f32[2,3,8,128]{3,2,1,0:T(8,128)S(1)} %pad_maximum_fusion.4.g0), channel_id=1, source_target_pairs={{0,2},{8,10},{1,3},{9,11},{2,0},{10,8},{3,1},{11,9},{16,18},{24,26... | collective-permute-start | bytes 73736 | tf_op jit(solution)/shard_map/ppermute | solution.py:294
  59.2 4.2 %collective-permute-start.16 = (f32[2,3,8,128]{3,2,1,0:T(8,128)S(1)}, f32[2,3,8,128]{3,2,1,0:T(8,128)S(1)}, u32[]{:S(2)}, u32[]{:S(2)}) collective-permute-start(f32[2,3,8,128]{3,2,1,0:T(8,128)S(1)} %pad_maximum_fusion.4.g0), channel_id=1, source_target_pairs={{0,1},{8,9},{1,2},{9,10},{2,3},{10,11},{3,0},{11,8},{16,17},{24,25... | collective-permute-start | bytes 73736 | tf_op jit(solution)/shard_map/ppermute | solution.py:294
  67.6 3.6 %collective-permute-start.18 = (f32[2,2,128]{2,1,0:T(2,128)S(1)}, f32[2,2,128]{2,1,0:T(2,128)S(1)}, u32[]{:S(2)}, u32[]{:S(2)}) collective-permute-start(f32[2,2,128]{2,1,0:T(2,128)S(1)} %pad_maximum_fusion.6), channel_id=1, source_target_pairs={{0,20},{8,28},{1,21},{9,29},{2,22},{10,30},{3,23},{11,31},{16,4},{... | collective-permute-start | bytes 6152 | tf_op jit(solution)/shard_map/ppermute | solution.py:294
  73.0 4.0 %collective-permute-start.20 = (f32[4,2,128]{2,1,0:T(2,128)S(1)}, f32[4,2,128]{2,1,0:T(2,128)S(1)}, u32[]{:S(2)}, u32[]{:S(2)}) collective-permute-start(f32[4,2,128]{2,1,0:T(2,128)S(1)} %pad_maximum_fusion.5.h0), channel_id=1, source_target_pairs={{0,64},{8,72},{1,65},{9,73},{2,66},{10,74},{3,67},{11,75},{16,80},... | collective-permute-start | bytes 12296 | tf_op jit(solution)/shard_map/ppermute | solution.py:294
  73.0 3.9 %collective-permute-start.21 = (f32[4,2,128]{2,1,0:T(2,128)S(1)}, f32[4,2,128]{2,1,0:T(2,128)S(1)}, u32[]{:S(2)}, u32[]{:S(2)}) collective-permute-start(f32[4,2,128]{2,1,0:T(2,128)S(1)} %pad_maximum_fusion.5.h0), channel_id=1, source_target_pairs={{0,32},{8,40},{1,33},{9,41},{2,34},{10,42},{3,35},{11,43},{16,48},... | collective-permute-start | bytes 12296 | tf_op jit(solution)/shard_map/ppermute | solution.py:294
  79.5 10.2 %collective-permute-start.25 = (bf16[128,1024]{1,0:T(8,128)(2,1)S(1)}, bf16[128,1024]{1,0:T(8,128)(2,1)S(1)}, u32[]{:S(2)}, u32[]{:S(2)}) collective-permute-start(bf16[128,1024]{1,0:T(8,128)(2,1)S(1)} %get-tuple-element.28), channel_id=1, source_target_pairs={{0,1},{8,11},{1,2},{9,8},{2,3},{10,9},{3,0},{11,10},{16,17},{24,27... | collective-permute-start | bytes 786440 | tf_op jit(solution)/shard_map/ppermute | solution.py:294
  80.2 9.5 %collective-permute-start.26 = (bf16[128,1024]{1,0:T(8,128)(2,1)S(1)}, bf16[128,1024]{1,0:T(8,128)(2,1)S(1)}, u32[]{:S(2)}, u32[]{:S(2)}) collective-permute-start(bf16[128,1024]{1,0:T(8,128)(2,1)S(1)} %get-tuple-element.29), channel_id=1, source_target_pairs={{0,3},{8,9},{1,0},{9,10},{2,1},{10,11},{3,2},{11,8},{16,19},{24,25... | collective-permute-start | bytes 786440 | tf_op jit(solution)/shard_map/ppermute | solution.py:294
  83.6 12.1 %collective-permute-start.23 = (bf16[128,1024]{1,0:T(8,128)(2,1)S(1)}, bf16[128,1024]{1,0:T(8,128)(2,1)S(1)}, u32[]{:S(2)}, u32[]{:S(2)}) collective-permute-start(bf16[128,1024]{1,0:T(8,128)(2,1)S(1)} %get-tuple-element.26), channel_id=1, source_target_pairs={{0,17},{8,27},{1,18},{9,24},{2,19},{10,25},{3,16},{11,26},{16,1},{... | collective-permute-start | bytes 786440 | tf_op jit(solution)/shard_map/ppermute | solution.py:294
  83.9 11.9 %collective-permute-start.24 = (bf16[128,1024]{1,0:T(8,128)(2,1)S(1)}, bf16[128,1024]{1,0:T(8,128)(2,1)S(1)}, u32[]{:S(2)}, u32[]{:S(2)}) collective-permute-start(bf16[128,1024]{1,0:T(8,128)(2,1)S(1)} %get-tuple-element.27), channel_id=1, source_target_pairs={{0,3},{8,9},{1,0},{9,10},{2,1},{10,11},{3,2},{11,8},{16,19},{24,25... | collective-permute-start | bytes 786440 | tf_op jit(solution)/shard_map/ppermute | solution.py:294
  86.9 9.5 %collective-permute-start.22 = (bf16[128,1024]{1,0:T(8,128)(2,1)S(1)}, bf16[128,1024]{1,0:T(8,128)(2,1)S(1)}, u32[]{:S(2)}, u32[]{:S(2)}) collective-permute-start(bf16[128,1024]{1,0:T(8,128)(2,1)S(1)} %get-tuple-element.25), channel_id=1, source_target_pairs={{0,16},{8,24},{1,17},{9,25},{2,18},{10,26},{3,19},{11,27},{16,0},{... | collective-permute-start | bytes 786440 | tf_op jit(solution)/shard_map/ppermute | solution.py:294
  92.3 11.7 %collective-permute-start.27 = (bf16[128,1024]{1,0:T(8,128)(2,1)S(1)}, bf16[128,1024]{1,0:T(8,128)(2,1)S(1)}, u32[]{:S(2)}, u32[]{:S(2)}) collective-permute-start(bf16[128,1024]{1,0:T(8,128)(2,1)S(1)} %get-tuple-element.30), channel_id=1, source_target_pairs={{0,19},{8,25},{1,16},{9,26},{2,17},{10,27},{3,18},{11,24},{16,3},{... | collective-permute-start | bytes 786440 | tf_op jit(solution)/shard_map/ppermute | solution.py:294
  92.4 11.6 %collective-permute-start.28 = (bf16[128,1024]{1,0:T(8,128)(2,1)S(1)}, bf16[128,1024]{1,0:T(8,128)(2,1)S(1)}, u32[]{:S(2)}, u32[]{:S(2)}) collective-permute-start(bf16[128,1024]{1,0:T(8,128)(2,1)S(1)} %get-tuple-element.31), channel_id=1, source_target_pairs={{0,1},{8,11},{1,2},{9,8},{2,3},{10,9},{3,0},{11,10},{16,17},{24,27... | collective-permute-start | bytes 786440 | tf_op jit(solution)/shard_map/ppermute | solution.py:294
  (10 other events, 34.3 us)

commit v6 on v5

--- a/solution.py
+++ b/solution.py
@@ -137,6 +137,7 @@
 
     def scores_of(step):
         a = a_ref[step * BLOCK : (step + 1) * BLOCK, :]
+        peak = None
         for j in range(n_b // wide):
             b = b_ref[j * wide : (j + 1) * wide, :]
             part = lax.dot_general(a, b, (((1,), (1,)), ((), ())), preferred_element_type=F32) * scale
@@ -145,17 +146,18 @@
                 c = lax.broadcasted_iota(I32, (BLOCK, wide), 1)
                 part = jnp.where((r == c) & (r < n), -jnp.inf, part)
             s_ref[step * BLOCK : (step + 1) * BLOCK, j * wide : (j + 1) * wide] = part
-
-    def stats_of(step):
+            for t in range(wide // n):
+                s = part[:, t * n : (t + 1) * n]
+                peak = s if peak is None else jnp.maximum(peak, s)
+        return jnp.max(peak, axis=1, keepdims=True)
+
+    def stats_of(step, peaks):
         lane = lax.broadcasted_iota(I32, (n, n), 1)
         for i in range(per):
             shard = step * per + i
             rows = slice(shard * n, (shard + 1) * n)
             mates = to_column(mates_ref[shard : shard + 1, :])
-            peak = s_ref[rows, 0:n]
-            for t in range(1, n_b // n):
-                peak = jnp.maximum(peak, s_ref[rows, t * n : (t + 1) * n])
-            peak = jnp.max(peak, axis=1, keepdims=True)
+            peak = peaks[i * n : (i + 1) * n]
             sums = jnp.zeros((n, n), F32)
             pos = jnp.zeros((n, n), F32)
             for t in range(n_b // n):
@@ -168,11 +170,8 @@
                 stats_ref[q, pl.ds(place[3 + shard], 1), :] = value
 
     steps = n_a // BLOCK
-    scores_of(0)
     for step in range(steps):
-        if step + 1 < steps:
-            scores_of(step + 1)
-        stats_of(step)
+        stats_of(step, scores_of(step))
 
 
 def merge_kernel(place, g0, g1, g2, g3, lse_ref, out_ref):
@@ -295,9 +294,10 @@
     n = LANES
     params = pltpu.CompilerParams(vmem_limit_bytes=VMEM_LIMIT)
     small = pltpu.CompilerParams(vmem_limit_bytes=8 << 20)
+    whole = pltpu.CompilerParams(vmem_limit_bytes=60 << 20)
 
     mine = pl.pallas_call(
-        unit_kernel, out_shape=shape((views + 2 * EXTRA, width), BF16), in_specs=[VMEM, VMEM], out_specs=VMEM, compiler_params=small
+        unit_kernel, out_shape=shape((views + 2 * EXTRA, width), BF16), in_specs=[VMEM, VMEM], out_specs=VMEM, compiler_params=whole
     )(embeddings, partner.reshape(1, views))
     twin = send(mine, SWAP)
     own = jnp.concatenate([mine[:n], twin[:n], mine[n : n + EXTRA], twin[n : n + EXTRA]], axis=0)

time: 109 us -> 109 us (level)
  Pallas kernels: 22.1 us -> 23.2 us
    pallas_call x1, Pallas kernels: 0.14 us -> 1.81 us  [body(): pl.pallas_call(unit_kernel, out_shape=shape((views + 2 * EXTRA, width), B...]
    unnamed x10 -> x6, local copies, waits for them, and re-layouts: 3.46 us -> 1.85 us
  transfers between devices with their start and end apart: 29 -> 29, of which waited for: 13 -> 12; matrix products, arithmetic and copies ran while one was open for 1% -> 3% of each run, Pallas kernels for 8% -> 7%
where the time goes in v6:
time: 109 us; the launch traced here: 107 us
  starting transfers between devices  38.1 us (35%)
  waiting for transfers between devices  37.4 us (34%)
  Pallas kernels  23.2 us (21%)
  local copies, waits for them, and re-layouts  3.79 us (3%)
  between operations  3.24 us (3%)
    ppermute x29, starting transfers between devices, body(): send = lambda v, pairs: lax.ppermute(v, AXES, pairs)  38.1 us
    ppermute x29, waiting for transfers between devices, body(): send = lambda v, pairs: lax.ppermute(v, AXES, pairs)  37.4 us
    pallas_call x4, Pallas kernels, part(): pl.pallas_call(functools.partial(grad_kernel, which), out_shape=outs, in_...  10.5 us
    pallas_call x1, Pallas kernels, body(): pl.pallas_call(score_kernel, out_shape=[pltpu.VMEM((n_a, n_b), F32), pltp...  8.44 us
  transfers between devices with their start and end apart: 29, of which 12 were waited for; matrix products, arithmetic and copies ran while one was open for 3% of the time, Pallas kernels for 7%

profile of v6, /device:TPU:1, one launch (start us, length us, event | category | flops | bytes accessed | tf_op | source)
XLA Modules:
  0.0 106.7 jit_solution(15883064240260035532)
XLA Ops:
  0.6 1.8 %shard_map.50 = bf16[144,1024]{1,0:T(8,128)(2,1)} custom-call(bf16[128,1024]{1,0:T(8,128)(2,1)} %x_ref.3, s32[1,128]{1,0:T(1,128)} %bitcast.40), custom_call_target="tpu_custom_call" | custom-call | tf_op jit(solution)/shard_map/pallas_call | solution.py:299
  5.6 2.6 %collective-permute-start.7 = (bf16[272,1024]{1,0:T(8,128)(2,1)S(1)}, bf16[272,1024]{1,0:T(8,128)(2,1)S(1)}, u32[]{:S(2)}, u32[]{:S(2)}) collective-permute-start(bf16[272,1024]{1,0:T(8,128)(2,1)S(1)} %pad_maximum_fusion.own), channel_id=1, source_target_pairs={{0,32},{8,104},{1,33},{9,105},{2,34},{10,106},{3,35},{11,107},{16,... | collective-permute-start | bytes 1671176 | tf_op jit(solution)/shard_map/ppermute | solution.py:293
  8.3 3.0 %collective-permute-start.8 = (bf16[272,1024]{1,0:T(8,128)(2,1)S(1)}, bf16[272,1024]{1,0:T(8,128)(2,1)S(1)}, u32[]{:S(2)}, u32[]{:S(2)}) collective-permute-start(bf16[272,1024]{1,0:T(8,128)(2,1)S(1)} %pad_maximum_fusion.own), channel_id=1, source_target_pairs={{0,52},{8,124},{1,53},{9,125},{2,54},{10,126},{3,55},{11,127},{16,... | collective-permute-start | bytes 1671176 | tf_op jit(solution)/shard_map/ppermute | solution.py:293
  11.3 3.8 %collective-permute-start.1 = (bf16[272,1024]{1,0:T(8,128)(2,1)S(1)}, bf16[272,1024]{1,0:T(8,128)(2,1)S(1)}, u32[]{:S(2)}, u32[]{:S(2)}) collective-permute-start(bf16[272,1024]{1,0:T(8,128)(2,1)S(1)} %pad_maximum_fusion.own), channel_id=1, source_target_pairs={{0,1},{8,11},{1,2},{9,8},{2,3},{10,9},{3,0},{11,10},{16,17},{24,27... | collective-permute-start | bytes 1671176 | tf_op jit(solution)/shard_map/ppermute | solution.py:293
  15.5 13.1 %collective-permute-done.8.d_b = bf16[272,1024]{1,0:T(8,128)(2,1)S(1)} collective-permute-done((bf16[272,1024]{1,0:T(8,128)(2,1)S(1)}, bf16[272,1024]{1,0:T(8,128)(2,1)S(1)}, u32[]{:S(2)}, u32[]{:S(2)}) %collective-permute-start.8) | collective-permute-done | bytes 557088 | tf_op jit(solution)/shard_map/ppermute | solution.py:293
  28.7 1.9 %collective-permute-start.11 = (bf16[256,1024]{1,0:T(8,128)(2,1)S(1)}, bf16[256,1024]{1,0:T(8,128)(2,1)}, u32[]{:S(2)}, u32[]{:S(2)}) collective-permute-start(bf16[256,1024]{1,0:T(8,128)(2,1)S(1)} %pad_maximum_fusion.3), channel_id=1, source_target_pairs={{0,32},{8,104},{1,33},{9,105},{2,34},{10,106},{3,35},{11,107},{16,... | collective-permute-start | bytes 1572872 | tf_op jit(solution)/shard_map/ppermute | solution.py:293
  32.1 3.8 %collective-permute-start.3 = (bf16[272,1024]{1,0:T(8,128)(2,1)}, bf16[272,1024]{1,0:T(8,128)(2,1)}, u32[]{:S(2)}, u32[]{:S(2)}) collective-permute-start(bf16[272,1024]{1,0:T(8,128)(2,1)} %pad_maximum_fusion.1), channel_id=1, source_target_pairs={{0,1},{8,11},{1,2},{9,8},{2,3},{10,9},{3,0},{11,10},{16,17},{24,27... | collective-permute-start | bytes 1671176 | tf_op jit(solution)/shard_map/ppermute | solution.py:293
  37.2 2.8 %collective-permute-start.6 = (bf16[272,1024]{1,0:T(8,128)(2,1)S(1)}, bf16[272,1024]{1,0:T(8,128)(2,1)}, u32[]{:S(2)}, u32[]{:S(2)}) collective-permute-start(bf16[272,1024]{1,0:T(8,128)(2,1)S(1)} %collective-permute-done.5.ry), channel_id=1, source_target_pairs={{0,8},{8,0},{1,9},{9,1},{2,10},{10,2},{3,11},{11,3},{16,24},{24,16... | collective-permute-start | bytes 1671176 | tf_op jit(solution)/shard_map/ppermute | solution.py:293
  44.2 8.4 %shard_map.51 = (f32[1024,2048]{1,0:T(8,128)S(1)}, bf16[2048,1024]{1,0:T(8,128)(2,1)S(1)}, f32[3,8,128]{2,1,0:T(8,128)S(1)}, s32[8,128]{1,0:T(8,128)S(1)}) custom-call(s32[28]{0:T(128)S(1)} %stack.133.place, f32[1]{0:T(128)S(6)} %copy.5.scale_ref, bf16[272,1024]{1,0:T(8,128)(2,1)S(1)} %pad_maximum_fusion.own, ...), custom_call_target="tpu_custom_call" | custom-call | tf_op jit(solution)/shard_map/pallas_call | solution.py:319
  52.7 2.5 %collective-permute-done.13 = f32[3,8,128]{2,1,0:T(8,128)S(1)} collective-permute-done((f32[3,8,128]{2,1,0:T(8,128)S(1)}, f32[3,8,128]{2,1,0:T(8,128)S(1)}, u32[]{:S(2)}, u32[]{:S(2)}) %collective-permute-start.13) | collective-permute-done | bytes 12320 | tf_op jit(solution)/shard_map/ppermute | solution.py:293
  55.3 3.8 %collective-permute-start.14 = (f32[2,3,8,128]{3,2,1,0:T(8,128)S(1)}, f32[2,3,8,128]{3,2,1,0:T(8,128)S(1)}, u32[]{:S(2)}, u32[]{:S(2)}) collective-permute-start(f32[2,3,8,128]{3,2,1,0:T(8,128)S(1)} %pad_maximum_fusion.4.g0), channel_id=1, source_target_pairs={{0,3},{8,11},{1,0},{9,8},{2,1},{10,9},{3,2},{11,10},{16,19},{24,27... | collective-permute-start | bytes 73736 | tf_op jit(solution)/shard_map/ppermute | solution.py:293
  60.0 3.2 %collective-permute-done.15.g2 = f32[2,3,8,128]{3,2,1,0:T(8,128)S(1)} collective-permute-done((f32[2,3,8,128]{3,2,1,0:T(8,128)S(1)}, f32[2,3,8,128]{3,2,1,0:T(8,128)S(1)}, u32[]{:S(2)}, u32[]{:S(2)}) %collective-permute-start.15) | collective-permute-done | bytes 24608 | tf_op jit(solution)/shard_map/ppermute | solution.py:293
  63.8 2.8 %collective-permute-start.17 = (f32[2,128]{1,0:T(2,128)S(1)}, f32[2,128]{1,0:T(2,128)S(1)}, u32[]{:S(2)}, u32[]{:S(2)}) collective-permute-start(f32[2,128]{1,0:T(2,128)S(1)} %get-tuple-element.21), channel_id=1, source_target_pairs={{0,8},{8,0},{1,9},{9,1},{2,10},{10,2},{3,11},{11,3},{16,24},{24,16... | collective-permute-start | bytes 3080 | tf_op jit(solution)/shard_map/ppermute | solution.py:293
  67.5 3.6 %collective-permute-done.18 = f32[2,2,128]{2,1,0:T(2,128)S(1)} collective-permute-done((f32[2,2,128]{2,1,0:T(2,128)S(1)}, f32[2,2,128]{2,1,0:T(2,128)S(1)}, u32[]{:S(2)}, u32[]{:S(2)}) %collective-permute-start.18) | collective-permute-done | bytes 2080 | tf_op jit(solution)/shard_map/ppermute | solution.py:293
  71.1 1.7 %collective-permute-start.19 = (f32[4,2,128]{2,1,0:T(2,128)S(1)}, f32[4,2,128]{2,1,0:T(2,128)S(1)}, u32[]{:S(2)}, u32[]{:S(2)}) collective-permute-start(f32[4,2,128]{2,1,0:T(2,128)S(1)} %pad_maximum_fusion.5.h0), channel_id=1, source_target_pairs={{0,96},{8,104},{1,97},{9,105},{2,98},{10,106},{3,99},{11,107},{16,... | collective-permute-start | bytes 12296 | tf_op jit(solution)/shard_map/ppermute | solution.py:293
  73.6 3.2 %collective-permute-done.20.h2 = f32[4,2,128]{2,1,0:T(2,128)S(1)} collective-permute-done((f32[4,2,128]{2,1,0:T(2,128)S(1)}, f32[4,2,128]{2,1,0:T(2,128)S(1)}, u32[]{:S(2)}, u32[]{:S(2)}) %collective-permute-start.20) | collective-permute-done | bytes 4128 | tf_op jit(solution)/shard_map/ppermute | solution.py:293
  76.8 2.5 %shard_map.55 = (bf16[128,1024]{1,0:T(8,128)(2,1)S(1)}, bf16[128,1024]{1,0:T(8,128)(2,1)S(1)}) custom-call(s32[28]{0:T(128)S(1)} %stack.133.place, f32[1024,2048]{1,0:T(8,128)S(1)} %get-tuple-element.17.s_ref, bf16[2048,1024]{1,0:T(8,128)(2,1)S(1)} %get-tuple-element.18.b_ref, f32[8,128]{1,0:T(8,128)S(1)} %get-tuple-element.20.lse_ref, ...), custom_call_target="tpu_custom_call" | custom-call | flops 2147483648 | bytes 1048576 | tf_op jit(solution)/shard_map/pallas_call | solution.py:347
  80.9 2.5 %shard_map.54 = (bf16[128,1024]{1,0:T(8,128)(2,1)S(1)}, bf16[128,1024]{1,0:T(8,128)(2,1)S(1)}) custom-call(s32[28]{0:T(128)S(1)} %stack.133.place, f32[1024,2048]{1,0:T(8,128)S(1)} %get-tuple-element.17.s_ref, bf16[2048,1024]{1,0:T(8,128)(2,1)S(1)} %get-tuple-element.18.b_ref, f32[8,128]{1,0:T(8,128)S(1)} %get-tuple-element.20.lse_ref, ...), custom_call_target="tpu_custom_call" | custom-call | flops 2147483648 | bytes 1048576 | tf_op jit(solution)/shard_map/pallas_call | solution.py:347
  83.6 2.9 %shard_map.53 = (bf16[128,1024]{1,0:T(8,128)(2,1)S(1)}, bf16[128,1024]{1,0:T(8,128)(2,1)S(1)}, f32[1,1]{1,0:T(1,128)}) custom-call(s32[28]{0:T(128)S(1)} %stack.133.place, f32[1024,2048]{1,0:T(8,128)S(1)} %get-tuple-element.17.s_ref, bf16[2048,1024]{1,0:T(8,128)(2,1)S(1)} %get-tuple-element.18.b_ref, f32[8,128]{1,0:T(8,128)S(1)} %get-tuple-element.20.lse_ref, ...), custom_call_target="tpu_custom_call" | custom-call | flops 2147483648 | bytes 1048576 | tf_op jit(solution)/shard_map/pallas_call | solution.py:347
  86.6 2.8 %collective-permute-start.22 = (bf16[128,1024]{1,0:T(8,128)(2,1)S(1)}, bf16[128,1024]{1,0:T(8,128)(2,1)S(1)}, u32[]{:S(2)}, u32[]{:S(2)}) collective-permute-start(bf16[128,1024]{1,0:T(8,128)(2,1)S(1)} %get-tuple-element.25), channel_id=1, source_target_pairs={{0,16},{8,24},{1,17},{9,25},{2,18},{10,26},{3,19},{11,27},{16,0},{... | collective-permute-start | bytes 786440 | tf_op jit(solution)/shard_map/ppermute | solution.py:293
  89.4 2.5 %shard_map.56 = (bf16[128,1024]{1,0:T(8,128)(2,1)S(1)}, bf16[128,1024]{1,0:T(8,128)(2,1)S(1)}) custom-call(s32[28]{0:T(128)S(1)} %stack.133.place, f32[1024,2048]{1,0:T(8,128)S(1)} %get-tuple-element.17.s_ref, bf16[2048,1024]{1,0:T(8,128)(2,1)S(1)} %get-tuple-element.18.b_ref, f32[8,128]{1,0:T(8,128)S(1)} %get-tuple-element.20.lse_ref, ...), custom_call_target="tpu_custom_call" | custom-call | flops 2147483648 | bytes 1048576 | tf_op jit(solution)/shard_map/pallas_call | solution.py:347
  92.0 2.7 %collective-permute-start.28 = (bf16[128,1024]{1,0:T(8,128)(2,1)S(1)}, bf16[128,1024]{1,0:T(8,128)(2,1)S(1)}, u32[]{:S(2)}, u32[]{:S(2)}) collective-permute-start(bf16[128,1024]{1,0:T(8,128)(2,1)S(1)} %get-tuple-element.31), channel_id=1, source_target_pairs={{0,1},{8,11},{1,2},{9,8},{2,3},{10,9},{3,0},{11,10},{16,17},{24,27... | collective-permute-start | bytes 786440 | tf_op jit(solution)/shard_map/ppermute | solution.py:293
  96.2 7.5 %collective-permute-done.27.refs_4_ = bf16[128,1024]{1,0:T(8,128)(2,1)S(1)} collective-permute-done((bf16[128,1024]{1,0:T(8,128)(2,1)S(1)}, bf16[128,1024]{1,0:T(8,128)(2,1)S(1)}, u32[]{:S(2)}, u32[]{:S(2)}) %collective-permute-start.27) | collective-permute-done | bytes 262176 | tf_op jit(solution)/shard_map/ppermute | solution.py:293
  103.7 1.9 %shard_map.57 = f32[128,1024]{1,0:T(8,128)} custom-call(f32[1]{0:T(128)S(6)} %div.7.scale_ref, bf16[128,1024]{1,0:T(8,128)(2,1)S(1)} %copy-done, bf16[128,1024]{1,0:T(8,128)(2,1)S(1)} %get-tuple-element.24.refs_0_, bf16[128,1024]{1,0:T(8,128)(2,1)S(1)} %collective-permute-done.22.refs_1_, bf16[128,1024]{1,0:T(8,128)(2,1)S(1)} %collective-permute-done.23.refs_2_, ...), custom_call_target="tpu_custom_call" | custom-call | tf_op jit(solution)/shard_map/pallas_call | solution.py:370
  (66 shorter events, 15.8 us)
Async XLA Ops:
  5.6 9.9 %collective-permute-start.7 = (bf16[272,1024]{1,0:T(8,128)(2,1)S(1)}, bf16[272,1024]{1,0:T(8,128)(2,1)S(1)}, u32[]{:S(2)}, u32[]{:S(2)}) collective-permute-start(bf16[272,1024]{1,0:T(8,128)(2,1)S(1)} %pad_maximum_fusion.own), channel_id=1, source_target_pairs={{0,32},{8,104},{1,33},{9,105},{2,34},{10,106},{3,35},{11,107},{16,... | collective-permute-start | bytes 1671176 | tf_op jit(solution)/shard_map/ppermute | solution.py:293
  8.3 20.4 %collective-permute-start.8 = (bf16[272,1024]{1,0:T(8,128)(2,1)S(1)}, bf16[272,1024]{1,0:T(8,128)(2,1)S(1)}, u32[]{:S(2)}, u32[]{:S(2)}) collective-permute-start(bf16[272,1024]{1,0:T(8,128)(2,1)S(1)} %pad_maximum_fusion.own), channel_id=1, source_target_pairs={{0,52},{8,124},{1,53},{9,125},{2,54},{10,126},{3,55},{11,127},{16,... | collective-permute-start | bytes 1671176 | tf_op jit(solution)/shard_map/ppermute | solution.py:293
  11.3 19.4 %collective-permute-start.1 = (bf16[272,1024]{1,0:T(8,128)(2,1)S(1)}, bf16[272,1024]{1,0:T(8,128)(2,1)S(1)}, u32[]{:S(2)}, u32[]{:S(2)}) collective-permute-start(bf16[272,1024]{1,0:T(8,128)(2,1)S(1)} %pad_maximum_fusion.own), channel_id=1, source_target_pairs={{0,1},{8,11},{1,2},{9,8},{2,3},{10,9},{3,0},{11,10},{16,17},{24,27... | collective-permute-start | bytes 1671176 | tf_op jit(solution)/shard_map/ppermute | solution.py:293
  15.0 15.7 %collective-permute-start.2 = (bf16[272,1024]{1,0:T(8,128)(2,1)S(1)}, bf16[272,1024]{1,0:T(8,128)(2,1)S(1)}, u32[]{:S(2)}, u32[]{:S(2)}) collective-permute-start(bf16[272,1024]{1,0:T(8,128)(2,1)S(1)} %pad_maximum_fusion.own), channel_id=1, source_target_pairs={{0,17},{8,27},{1,18},{9,24},{2,19},{10,25},{3,16},{11,26},{16,1},{... | collective-permute-start | bytes 1671176 | tf_op jit(solution)/shard_map/ppermute | solution.py:293
  15.0 20.8 %collective-permute-start.5 = (bf16[272,1024]{1,0:T(8,128)(2,1)S(1)}, bf16[272,1024]{1,0:T(8,128)(2,1)S(1)}, u32[]{:S(2)}, u32[]{:S(2)}) collective-permute-start(bf16[272,1024]{1,0:T(8,128)(2,1)S(1)} %pad_maximum_fusion.own), channel_id=1, source_target_pairs={{0,16},{8,28},{1,17},{9,29},{2,18},{10,30},{3,19},{11,31},{16,0},{... | collective-permute-start | bytes 1671176 | tf_op jit(solution)/shard_map/ppermute | solution.py:293
  28.7 8.5 %collective-permute-start.11 = (bf16[256,1024]{1,0:T(8,128)(2,1)S(1)}, bf16[256,1024]{1,0:T(8,128)(2,1)}, u32[]{:S(2)}, u32[]{:S(2)}) collective-permute-start(bf16[256,1024]{1,0:T(8,128)(2,1)S(1)} %pad_maximum_fusion.3), channel_id=1, source_target_pairs={{0,32},{8,104},{1,33},{9,105},{2,34},{10,106},{3,35},{11,107},{16,... | collective-permute-start | bytes 1572872 | tf_op jit(solution)/shard_map/ppermute | solution.py:293
  30.8 9.3 %collective-permute-start.4 = (bf16[272,1024]{1,0:T(8,128)(2,1)S(1)}, bf16[272,1024]{1,0:T(8,128)(2,1)S(1)}, u32[]{:S(2)}, u32[]{:S(2)}) collective-permute-start(bf16[272,1024]{1,0:T(8,128)(2,1)S(1)} %pad_maximum_fusion.2), channel_id=1, source_target_pairs={{0,8},{8,0},{1,9},{9,1},{2,10},{10,2},{3,11},{11,3},{16,24},{24,16... | collective-permute-start | bytes 1671176 | tf_op jit(solution)/shard_map/ppermute | solution.py:293
  32.1 10.6 %collective-permute-start.3 = (bf16[272,1024]{1,0:T(8,128)(2,1)}, bf16[272,1024]{1,0:T(8,128)(2,1)}, u32[]{:S(2)}, u32[]{:S(2)}) collective-permute-start(bf16[272,1024]{1,0:T(8,128)(2,1)} %pad_maximum_fusion.1), channel_id=1, source_target_pairs={{0,1},{8,11},{1,2},{9,8},{2,3},{10,9},{3,0},{11,10},{16,17},{24,27... | collective-permute-start | bytes 1671176 | tf_op jit(solution)/shard_map/ppermute | solution.py:293
  35.8 6.8 %collective-permute-start.10 = (bf16[272,1024]{1,0:T(8,128)(2,1)S(1)}, bf16[272,1024]{1,0:T(8,128)(2,1)}, u32[]{:S(2)}, u32[]{:S(2)}) collective-permute-start(bf16[272,1024]{1,0:T(8,128)(2,1)S(1)} %collective-permute-done.8.d_b), channel_id=1, source_target_pairs={{0,8},{8,0},{1,9},{9,1},{2,10},{10,2},{3,11},{11,3},{16,24},{24,16... | collective-permute-start | bytes 1671176 | tf_op jit(solution)/shard_map/ppermute | solution.py:293
  35.8 6.8 %collective-permute-start.9 = (bf16[272,1024]{1,0:T(8,128)(2,1)S(1)}, bf16[272,1024]{1,0:T(8,128)(2,1)}, u32[]{:S(2)}, u32[]{:S(2)}) collective-permute-start(bf16[272,1024]{1,0:T(8,128)(2,1)S(1)} %collective-permute-done.7.rx), channel_id=1, source_target_pairs={{0,8},{8,0},{1,9},{9,1},{2,10},{10,2},{3,11},{11,3},{16,24},{24,16... | collective-permute-start | bytes 1671176 | tf_op jit(solution)/shard_map/ppermute | solution.py:293
  37.2 5.4 %collective-permute-start.6 = (bf16[272,1024]{1,0:T(8,128)(2,1)S(1)}, bf16[272,1024]{1,0:T(8,128)(2,1)}, u32[]{:S(2)}, u32[]{:S(2)}) collective-permute-start(bf16[272,1024]{1,0:T(8,128)(2,1)S(1)} %collective-permute-done.5.ry), channel_id=1, source_target_pairs={{0,8},{8,0},{1,9},{9,1},{2,10},{10,2},{3,11},{11,3},{16,24},{24,16... | collective-permute-start | bytes 1671176 | tf_op jit(solution)/shard_map/ppermute | solution.py:293
  55.3 4.7 %collective-permute-start.14 = (f32[2,3,8,128]{3,2,1,0:T(8,128)S(1)}, f32[2,3,8,128]{3,2,1,0:T(8,128)S(1)}, u32[]{:S(2)}, u32[]{:S(2)}) collective-permute-start(f32[2,3,8,128]{3,2,1,0:T(8,128)S(1)} %pad_maximum_fusion.4.g0), channel_id=1, source_target_pairs={{0,3},{8,11},{1,0},{9,8},{2,1},{10,9},{3,2},{11,10},{16,19},{24,27... | collective-permute-start | bytes 73736 | tf_op jit(solution)/shard_map/ppermute | solution.py:293
  59.0 4.2 %collective-permute-start.15 = (f32[2,3,8,128]{3,2,1,0:T(8,128)S(1)}, f32[2,3,8,128]{3,2,1,0:T(8,128)S(1)}, u32[]{:S(2)}, u32[]{:S(2)}) collective-permute-start(f32[2,3,8,128]{3,2,1,0:T(8,128)S(1)} %pad_maximum_fusion.4.g0), channel_id=1, source_target_pairs={{0,2},{8,10},{1,3},{9,11},{2,0},{10,8},{3,1},{11,9},{16,18},{24,26... | collective-permute-start | bytes 73736 | tf_op jit(solution)/shard_map/ppermute | solution.py:293
  59.0 4.2 %collective-permute-start.16 = (f32[2,3,8,128]{3,2,1,0:T(8,128)S(1)}, f32[2,3,8,128]{3,2,1,0:T(8,128)S(1)}, u32[]{:S(2)}, u32[]{:S(2)}) collective-permute-start(f32[2,3,8,128]{3,2,1,0:T(8,128)S(1)} %pad_maximum_fusion.4.g0), channel_id=1, source_target_pairs={{0,1},{8,9},{1,2},{9,10},{2,3},{10,11},{3,0},{11,8},{16,17},{24,25... | collective-permute-start | bytes 73736 | tf_op jit(solution)/shard_map/ppermute | solution.py:293
  67.4 3.6 %collective-permute-start.18 = (f32[2,2,128]{2,1,0:T(2,128)S(1)}, f32[2,2,128]{2,1,0:T(2,128)S(1)}, u32[]{:S(2)}, u32[]{:S(2)}) collective-permute-start(f32[2,2,128]{2,1,0:T(2,128)S(1)} %pad_maximum_fusion.6), channel_id=1, source_target_pairs={{0,20},{8,28},{1,21},{9,29},{2,22},{10,30},{3,23},{11,31},{16,4},{... | collective-permute-start | bytes 6152 | tf_op jit(solution)/shard_map/ppermute | solution.py:293
  72.8 4.0 %collective-permute-start.20 = (f32[4,2,128]{2,1,0:T(2,128)S(1)}, f32[4,2,128]{2,1,0:T(2,128)S(1)}, u32[]{:S(2)}, u32[]{:S(2)}) collective-permute-start(f32[4,2,128]{2,1,0:T(2,128)S(1)} %pad_maximum_fusion.5.h0), channel_id=1, source_target_pairs={{0,64},{8,72},{1,65},{9,73},{2,66},{10,74},{3,67},{11,75},{16,80},... | collective-permute-start | bytes 12296 | tf_op jit(solution)/shard_map/ppermute | solution.py:293
  72.9 3.9 %collective-permute-start.21 = (f32[4,2,128]{2,1,0:T(2,128)S(1)}, f32[4,2,128]{2,1,0:T(2,128)S(1)}, u32[]{:S(2)}, u32[]{:S(2)}) collective-permute-start(f32[4,2,128]{2,1,0:T(2,128)S(1)} %pad_maximum_fusion.5.h0), channel_id=1, source_target_pairs={{0,32},{8,40},{1,33},{9,41},{2,34},{10,42},{3,35},{11,43},{16,48},... | collective-permute-start | bytes 12296 | tf_op jit(solution)/shard_map/ppermute | solution.py:293
  79.3 10.1 %collective-permute-start.25 = (bf16[128,1024]{1,0:T(8,128)(2,1)S(1)}, bf16[128,1024]{1,0:T(8,128)(2,1)S(1)}, u32[]{:S(2)}, u32[]{:S(2)}) collective-permute-start(bf16[128,1024]{1,0:T(8,128)(2,1)S(1)} %get-tuple-element.28), channel_id=1, source_target_pairs={{0,1},{8,11},{1,2},{9,8},{2,3},{10,9},{3,0},{11,10},{16,17},{24,27... | collective-permute-start | bytes 786440 | tf_op jit(solution)/shard_map/ppermute | solution.py:293
  80.0 9.4 %collective-permute-start.26 = (bf16[128,1024]{1,0:T(8,128)(2,1)S(1)}, bf16[128,1024]{1,0:T(8,128)(2,1)S(1)}, u32[]{:S(2)}, u32[]{:S(2)}) collective-permute-start(bf16[128,1024]{1,0:T(8,128)(2,1)S(1)} %get-tuple-element.29), channel_id=1, source_target_pairs={{0,3},{8,9},{1,0},{9,10},{2,1},{10,11},{3,2},{11,8},{16,19},{24,25... | collective-permute-start | bytes 786440 | tf_op jit(solution)/shard_map/ppermute | solution.py:293
  83.4 12.0 %collective-permute-start.23 = (bf16[128,1024]{1,0:T(8,128)(2,1)S(1)}, bf16[128,1024]{1,0:T(8,128)(2,1)S(1)}, u32[]{:S(2)}, u32[]{:S(2)}) collective-permute-start(bf16[128,1024]{1,0:T(8,128)(2,1)S(1)} %get-tuple-element.26), channel_id=1, source_target_pairs={{0,17},{8,27},{1,18},{9,24},{2,19},{10,25},{3,16},{11,26},{16,1},{... | collective-permute-start | bytes 786440 | tf_op jit(solution)/shard_map/ppermute | solution.py:293
  83.6 11.8 %collective-permute-start.24 = (bf16[128,1024]{1,0:T(8,128)(2,1)S(1)}, bf16[128,1024]{1,0:T(8,128)(2,1)S(1)}, u32[]{:S(2)}, u32[]{:S(2)}) collective-permute-start(bf16[128,1024]{1,0:T(8,128)(2,1)S(1)} %get-tuple-element.27), channel_id=1, source_target_pairs={{0,3},{8,9},{1,0},{9,10},{2,1},{10,11},{3,2},{11,8},{16,19},{24,25... | collective-permute-start | bytes 786440 | tf_op jit(solution)/shard_map/ppermute | solution.py:293
  86.6 9.6 %collective-permute-start.22 = (bf16[128,1024]{1,0:T(8,128)(2,1)S(1)}, bf16[128,1024]{1,0:T(8,128)(2,1)S(1)}, u32[]{:S(2)}, u32[]{:S(2)}) collective-permute-start(bf16[128,1024]{1,0:T(8,128)(2,1)S(1)} %get-tuple-element.25), channel_id=1, source_target_pairs={{0,16},{8,24},{1,17},{9,25},{2,18},{10,26},{3,19},{11,27},{16,0},{... | collective-permute-start | bytes 786440 | tf_op jit(solution)/shard_map/ppermute | solution.py:293
  91.9 11.7 %collective-permute-start.27 = (bf16[128,1024]{1,0:T(8,128)(2,1)S(1)}, bf16[128,1024]{1,0:T(8,128)(2,1)S(1)}, u32[]{:S(2)}, u32[]{:S(2)}) collective-permute-start(bf16[128,1024]{1,0:T(8,128)(2,1)S(1)} %get-tuple-element.30), channel_id=1, source_target_pairs={{0,19},{8,25},{1,16},{9,26},{2,17},{10,27},{3,18},{11,24},{16,3},{... | collective-permute-start | bytes 786440 | tf_op jit(solution)/shard_map/ppermute | solution.py:293
  92.0 11.7 %collective-permute-start.28 = (bf16[128,1024]{1,0:T(8,128)(2,1)S(1)}, bf16[128,1024]{1,0:T(8,128)(2,1)S(1)}, u32[]{:S(2)}, u32[]{:S(2)}) collective-permute-start(bf16[128,1024]{1,0:T(8,128)(2,1)S(1)} %get-tuple-element.31), channel_id=1, source_target_pairs={{0,1},{8,11},{1,2},{9,8},{2,3},{10,9},{3,0},{11,10},{16,17},{24,27... | collective-permute-start | bytes 786440 | tf_op jit(solution)/shard_map/ppermute | solution.py:293
  (8 other events, 33.1 us)
